TPU v7x, 32 devices: a whole 2x2x4 slice. The times are simulated.
32 devices in a mesh: rep: 8 (over y, x, core), fsdp: 4 (over z).
Axes of the slice: x: 2, y: 2, z: 4, core: 2. Of those that a mesh axis runs over, the one named last changes fastest.
Arguments:
- tokens: bfloat16 [32768, 8192], P(('rep', 'fsdp')), may hold values from -6 to 6
- norm_gain: bfloat16 [8192], replicated, may hold values from 0.25 to 1.75
- deltas: bfloat16 [8, 8192, 1024], P('rep', 'fsdp'), may hold values from -0.09375 to 0.09375
- inner_steps: int32 [8, 16], replicated, may hold values from 1 to 64
- bucket_of_row: int32 [8192], P('fsdp'), may hold values from 0 to 15, never falling along the last dimension, each value on 1 to 1024 neighbouring positions
- master: float32 [8192, 1024], P(('fsdp', 'rep')), may hold values from -0.0625 to 0.0625
- momentum: float32 [8192, 1024], P(('fsdp', 'rep')), may hold values from -0.0625 to 0.0625
Outputs:
- keys: bfloat16 [32768, 1024], P(('rep', 'fsdp'))
- master_new: float32 [8192, 1024], P(('fsdp', 'rep'))
- momentum_new: float32 [8192, 1024], P(('fsdp', 'rep'))
Inputs may be any that keep to these rules, and one draw needn't show every extreme that they name: `bucket_of_row`: never falls along the rows; each bucket holds 1 to 1024 rows.
All inputs are finite; a program needn't handle non-finite values.
Results may differ from a plain program's by a relative error of at most 0.0058.
Values may be sent and summed in bfloat16 or wider, within the bound.
No kernel may reach another device: no remote copies, remote signals or barrier semaphores. Data moves between devices by JAX's collectives and lax.ppermute only.
A program may use at most 192 MiB of HBM per device.

v0:
```python
import jax
import jax.numpy as jnp
from jax import lax
from jax.sharding import PartitionSpec as P

OUTER_RATE = 0.7
MOMENTUM_KEEP = 0.9
EPSILON = 1e-05


def normalize(rows, norm_gain):
    values = rows.astype(jnp.float32)
    scale = lax.rsqrt(jnp.mean(values * values, axis=1, keepdims=True) + EPSILON)
    return (values * scale * norm_gain.astype(jnp.float32)[None, :]).astype(jnp.bfloat16)


def on_device(tokens, norm_gain, deltas, inner_steps, bucket_of_row, master, momentum):
    counts = inner_steps.astype(jnp.float32)
    share = counts / jnp.sum(counts, axis=0, keepdims=True)
    own_share = lax.dynamic_slice_in_dim(share, lax.axis_index("rep"), 1, 0)[0]
    bucket_ids = jnp.arange(counts.shape[1], dtype=jnp.int32)
    one_hot = (bucket_of_row[:, None] == bucket_ids[None, :]).astype(jnp.float32)
    row_weight = jnp.sum(one_hot * own_share[None, :], axis=1)
    weighted = row_weight[:, None] * deltas[0].astype(jnp.float32)
    averaged = lax.psum_scatter(weighted, "rep", scatter_dimension=0, tiled=True)
    momentum_new = MOMENTUM_KEEP * momentum + averaged
    master_new = master - OUTER_RATE * (averaged + MOMENTUM_KEEP * momentum_new)
    layer = master_new.astype(jnp.bfloat16)
    normed = normalize(tokens, norm_gain)
    fsdp_count = lax.axis_size("fsdp")
    rep_count = lax.axis_size("rep")
    shard_len = layer.shape[0]
    piece = lax.all_gather(layer, ("rep", "fsdp"), axis=0, tiled=True)
    order = jnp.arange(piece.shape[0], dtype=jnp.int32)
    shard = order // shard_len
    within = order % shard_len
    rep_pos = shard // fsdp_count
    fsdp_pos = shard % fsdp_count
    column_ids = (fsdp_pos * rep_count + rep_pos) * shard_len + within
    columns = jnp.take(normed, column_ids, axis=1)
    projected = jnp.dot(columns, piece, preferred_element_type=jnp.float32)
    return (projected.astype(jnp.bfloat16), master_new, momentum_new)


def solution(mesh):
    in_specs = (
        P(("rep", "fsdp"), None),
        P(),
        P("rep", "fsdp", None),
        P(),
        P("fsdp"),
        P(("fsdp", "rep"), None),
        P(("fsdp", "rep"), None),
    )
    out_specs = (P(("rep", "fsdp"), None), P(("fsdp", "rep"), None), P(("fsdp", "rep"), None))
    return jax.shard_map(
        on_device, mesh=mesh, in_specs=in_specs, out_specs=out_specs, check_vma=False
    )
```

profile of v0, /device:TPU:9, one launch (start us, length us, event | category | flops | bytes accessed | tf_op | source)
XLA Modules:
  0.0 237.1 jit_solution(10445089387695734393)
XLA Ops:
  7.2 0.0 copy-start.1
  7.2 0.0 copy-start.2
  7.2 0.0 reduce-scatter.2.cloned.1.call-start
  7.2 0.8 convert_reduce_fusion
  8.1 0.7 convert_divide_fusion
  8.8 0.8 select_reduce_fusion
  9.6 6.0 %convert_multiply_fusion.2 = f32[2048,1024]{1,0:T(8,128)} fusion(bf16[1,2048,1024]{2,1,0:T(8,128)(2,1)} %param.9, f32[2048]{0:T(1024)S(1)} %select_reduce_fusion), kind=kLoop, calls=%fused_computation.9 | loop fusion | flops 4194304 | bytes 12591104 | tf_op jit(solution)/shard_map/mul | solution.py:24
  15.6 0.0 reduce-scatter.2.cloned.1.call-update
  15.6 0.0 all-gather.2.cloned.1.call-start
  15.7 72.5 %reduce-scatter.2.cloned.1.call-done = f32[256,1024]{1,0:T(8,128)} async-done(((f32[2048,1024]{1,0:T(8,128)}), f32[256,1024]{1,0:T(8,128)}) %reduce-scatter.2.cloned.1.call-update) | async-done | bytes 1048592 | tf_op jit(solution)/shard_map/reduce_scatter | solution.py:25
  88.2 0.0 copy-done.1
  88.2 0.0 copy-done.2
  88.2 3.1 %fusion.32 = (bf16[256,1024]{1,0:T(8,128)(2,1)}, f32[256,1024]{1,0:T(8,128)}, f32[256,1024]{1,0:T(8,128)}) fusion(f32[256,1024]{1,0:T(8,128)S(1)} %copy-done.1, f32[256,1024]{1,0:T(8,128)} %reduce-scatter.2.cloned.1.call-done, f32[256,1024]{1,0:T(8,128)S(1)} %copy-done.2), kind=kLoop, calls=%fused_computation.65 | loop fusion | flops 1835008 | bytes 5767168 | tf_op jit(solution)/shard_map/convert_element_type | solution.py:28
  91.3 0.0 all-gather.2.cloned.1.call-update
  91.3 0.0 copy-start.3
  91.4 22.5 %copy.12 = bf16[1024,8192]{0,1:T(8,128)(2,1)} copy(bf16[1024,8192]{1,0:T(8,128)(2,1)} %param.7) | data formatting | bytes 33554432 | tf_op args[0]
  113.8 0.0 copy-done.3
  113.8 0.0 copy-start
  113.9 10.5 %fusion = f32[1024]{0:T(1024)S(1)} fusion(bf16[1024,8192]{0,1:T(8,128)(2,1)} %copy.12), kind=kLoop, calls=%fused_computation.3 | loop fusion | flops 25164800 | bytes 16781312 | tf_op jit(solution)/shard_map/reduce_sum | solution.py:13
  124.4 0.1 compare_select_fusion
  124.5 0.7 copy-done
  125.2 8.0 %fusion.2 = bf16[1024,8192]{0,1:T(8,128)(2,1)} fusion(bf16[1024,8192]{0,1:T(8,128)(2,1)S(1)} %copy-done, f32[8192]{0:T(1024)S(1)} %convert_element_type.26, f32[1024]{0:T(1024)S(1)} %add_rsqrt_fusion), kind=kLoop, calls=%fused_computation.5 | loop fusion | flops 33554432 | bytes 33591296 | tf_op jit(solution)/shard_map/convert_element_type | solution.py:14
  133.2 48.6 %gather_fusion = bf16[8192,1024]{1,0:T(8,128)(2,1)} fusion(bf16[1024,8192]{0,1:T(8,128)(2,1)} %fusion.2, s32[8192]{0:T(1024)S(1)} %broadcast_clamp_fusion), kind=kCustom, calls=%fused_computation | custom fusion | bytes 33587200 | tf_op jit(solution)/shard_map/jit(_take)/gather | solution.py:40
  181.9 24.6 %all-gather.2.cloned.1.call-done = bf16[8192,1024]{1,0:T(8,128)(2,1)} async-done(((bf16[256,1024]{1,0:T(8,128)(2,1)}), bf16[8192,1024]{1,0:T(8,128)(2,1)}) %all-gather.2.cloned.1.call-update) | async-done | bytes 16777232 | tf_op jit(solution)/shard_map/all_gather | solution.py:33
  206.5 23.8 %fusion.7 = bf16[1024,1024]{1,0:T(8,128)(2,1)} fusion(bf16[8192,1024]{1,0:T(8,128)(2,1)} %all-gather.2.cloned.1.call-done, bf16[8192,1024]{1,0:T(8,128)(2,1)} %gather_fusion, pred[8192]{0:T(1024)(128)(4,1)S(1)} %compare_and_fusion), kind=kOutput, calls=%fused_computation.11 | convolution fusion | flops 17189306368 | bytes 35659776 | tf_op jit(solution)/shard_map/dot_general | solution.py:41
  (5 shorter events, 0.1 us)
Async XLA Ops:
  7.2 81.0 %copy-start.1 = (f32[256,1024]{1,0:T(8,128)S(1)}, f32[256,1024]{1,0:T(8,128)}, u32[]{:S(2)}) copy-start(f32[256,1024]{1,0:T(8,128)} %param.12) | copy-start | bytes 3145732
  7.2 81.0 %copy-start.2 = (f32[256,1024]{1,0:T(8,128)S(1)}, f32[256,1024]{1,0:T(8,128)}, u32[]{:S(2)}) copy-start(f32[256,1024]{1,0:T(8,128)} %param.13) | copy-start | bytes 3145732
  7.2 81.0 %reduce-scatter.2.cloned.1.call-start = ((), (), s32[]{:S(2)}) async-start(), calls=%async_computation.1 | async-start | bytes 9437184 | tf_op jit(solution)/shard_map/reduce_scatter | solution.py:25
  15.6 190.9 %all-gather.2.cloned.1.call-start = ((), (), s32[]{:S(2)}) async-start(), calls=%async_computation.2 | async-start | bytes 17301504 | tf_op jit(solution)/shard_map/all_gather | solution.py:33
  91.3 22.5 %copy-start.3 = (bf16[8192]{0:T(1024)(128)(2,1)S(1)}, bf16[8192]{0:T(1024)(128)(2,1)}, u32[]{:S(2)}) copy-start(bf16[8192]{0:T(1024)(128)(2,1)} %param.8) | copy-start | bytes 49156
  113.8 11.4 %copy-start = (bf16[1024,8192]{0,1:T(8,128)(2,1)S(1)}, bf16[1024,8192]{0,1:T(8,128)(2,1)}, u32[]{:S(2)}) copy-start(bf16[1024,8192]{0,1:T(8,128)(2,1)} %copy.12) | copy-start | bytes 50331652
Sparse Core Ops, SparseCore 0:
  15.7 72.4 reduce-scatter.1
  92.2 114.2 all-gather.1
where the time goes:
time: 240 us; the launch traced here: 237 us
  waiting for transfers between devices  97.2 us (40%)
  local copies, waits for them, and re-layouts  71.9 us (30%)
  other arithmetic  30.1 us (13%)
  matrix products  23.8 us (10%)
  between operations  14.1 us (6%)
    reduce_scatter x1, waiting for transfers between devices, on_device(): lax.psum_scatter(weighted, 'rep', scatter_dimension=0, tiled=True)  72.5 us
    gather x1, local copies, waits for them, and re-layouts, on_device(): columns = jnp.take(normed, column_ids, axis=1)  48.6 us
    all_gather x1, waiting for transfers between devices, on_device(): piece = lax.all_gather(layer, ('rep', 'fsdp'), axis=0, tiled=True)  24.6 us
    dot_general x1, matrix products, on_device(): projected = jnp.dot(columns, piece, preferred_element_type=jnp.float32)  23.8 us
    unnamed x9, local copies, waits for them, and re-layouts  23.2 us
    reduce_sum x1, other arithmetic, normalize(): jnp.mean(values * values, axis=1, keepdims=True) + EPSILON  10.5 us
    convert_element_type x1, other arithmetic, normalize(): (values * scale * norm_gain.astype(jnp.float32)[None, :]).astype(jnp.bflo...  8 us
    mul x1, other arithmetic, on_device(): weighted = row_weight[:, None] * deltas[0].astype(jnp.float32)  6.02 us
  transfers between devices with their start and end apart: 2, of which 2 were waited for; matrix products, arithmetic and copies ran while one was open for 38% of the time, Pallas kernels for 0%

commit v1 on v0

v1 whole, which is shorter than its diff:
```python
import functools

import jax
import jax.numpy as jnp
from jax import lax
from jax.experimental import pallas as pl
from jax.experimental.pallas import tpu as pltpu
from jax.sharding import PartitionSpec as P

OUTER_RATE = 0.7
MOMENTUM_KEEP = 0.9
EPSILON = 1e-05
VMEM_BYTES = 48 * 1024 * 1024

CORE, ALONG_X, ALONG_Y = 1, 2, 4


def flip(value, even_bit, odd_bit):
    perm = [(i, i ^ (odd_bit if i & CORE else even_bit)) for i in range(8)]
    return lax.ppermute(value, "rep", perm)


def swap_cores(value):
    return flip(value, CORE, CORE)


def swap_first(value):
    return flip(value, ALONG_X, ALONG_Y)


def swap_second(value):
    return flip(value, ALONG_Y, ALONG_X)


def row_weights(inner_steps, bucket_of_row, replica):
    counts = inner_steps.astype(jnp.float32)
    share = counts / jnp.sum(counts, axis=0, keepdims=True)
    own = lax.dynamic_index_in_dim(share, replica, 0, keepdims=False)
    bucket_ids = jnp.arange(counts.shape[1], dtype=jnp.int32)
    one_hot = (bucket_of_row[:, None] == bucket_ids[None, :]).astype(jnp.float32)
    return jnp.sum(one_hot * own[None, :], axis=1)


def outer_step(averaged, master, momentum):
    momentum_new = MOMENTUM_KEEP * momentum + averaged
    master_new = master - OUTER_RATE * (averaged + MOMENTUM_KEEP * momentum_new)
    return master_new, momentum_new


def normalize_kernel(order, tokens, gain, *outs, width):
    values = tokens[...].astype(jnp.float32)
    scale = lax.rsqrt(jnp.mean(values * values, axis=1, keepdims=True) + EPSILON)
    per_out = outs[0].shape[1] // width
    for at, out in enumerate(outs):
        for j in range(per_out):
            source = pl.ds(pl.multiple_of(order[at * per_out + j] * width, width), width)
            part = tokens[:, source].astype(jnp.float32) * scale * gain[:, source].astype(jnp.float32)
            out[:, j * width:(j + 1) * width] = part.astype(out.dtype)


def normalize_in_order(tokens, gain, order, width, parts):
    rows, features = tokens.shape
    tile = 128
    return pl.pallas_call(
        functools.partial(normalize_kernel, width=width),
        grid_spec=pltpu.PrefetchScalarGridSpec(
            num_scalar_prefetch=1,
            grid=(rows // tile,),
            in_specs=[
                pl.BlockSpec((tile, features), lambda i, order: (i, 0)),
                pl.BlockSpec((1, features), lambda i, order: (0, 0)),
            ],
            out_specs=[pl.BlockSpec((tile, features // parts), lambda i, order: (i, 0))] * parts,
        ),
        out_shape=[jax.ShapeDtypeStruct((rows, features // parts), tokens.dtype)] * parts,
        compiler_params=pltpu.CompilerParams(vmem_limit_bytes=VMEM_BYTES),
        cost_estimate=pl.CostEstimate(
            flops=rows * features * 6, bytes_accessed=rows * features * 4, transcendentals=rows
        ),
        name="normalize_in_order",
    )(order, tokens, gain.reshape(1, features))


def project_kernel(first, last, normed, *refs):
    total = None
    pieces = refs[: len(refs) - (1 if first else 2)]
    start = 0
    for piece in pieces:
        depth = piece.shape[0]
        term = jnp.dot(
            normed[:, start:start + depth], piece[...], preferred_element_type=jnp.float32
        )
        total = term if total is None else total + term
        start += depth
    if not first:
        total = total + refs[-2][...]
    refs[-1][...] = total.astype(refs[-1].dtype)


def project(normed, pieces, total, last):
    rows, depth = normed.shape
    cols = pieces[0].shape[1]
    tile = 256
    first = total is None
    row_spec = pl.BlockSpec((tile, cols), lambda i: (i, 0))
    return pl.pallas_call(
        functools.partial(project_kernel, first, last),
        grid=(rows // tile,),
        in_specs=[pl.BlockSpec((tile, depth), lambda i: (i, 0))]
        + [pl.BlockSpec(piece.shape, lambda i: (0, 0)) for piece in pieces]
        + ([] if first else [row_spec]),
        out_specs=row_spec,
        out_shape=jax.ShapeDtypeStruct((rows, cols), normed.dtype if last else jnp.float32),
        compiler_params=pltpu.CompilerParams(vmem_limit_bytes=VMEM_BYTES),
        cost_estimate=pl.CostEstimate(
            flops=2 * rows * depth * cols,
            bytes_accessed=2 * (rows * depth + depth * cols) + 8 * rows * cols,
            transcendentals=0,
        ),
        name="project",
    )(normed, *pieces, *([] if first else [total]))


def gather_along_line(own):
    place = lax.axis_index("fsdp")
    outer = (place == 0) | (place == 3)
    pair = lax.ppermute(own, "fsdp", [(0, 1), (1, 0), (2, 3), (3, 2)])
    inner_near = lax.ppermute(own, "fsdp", [(1, 2), (2, 1)])
    inner_far = lax.ppermute(pair, "fsdp", [(1, 2), (2, 1)])
    outer_near = lax.ppermute(inner_near, "fsdp", [(1, 0), (2, 3)])
    outer_far = lax.ppermute(inner_far, "fsdp", [(1, 0), (2, 3)])
    near = jnp.where(outer, outer_near, inner_near)
    far = jnp.where(outer, outer_far, inner_far)
    return [own, pair, near, far]


def on_block(tokens, norm_gain, deltas, inner_steps, bucket_of_row, master, momentum):
    rep, place = lax.axis_index("rep"), lax.axis_index("fsdp")
    core = rep & 1
    sibling = rep ^ CORE
    first_bit = jnp.where(core == 0, ALONG_X, ALONG_Y)
    second_bit = jnp.where(core == 0, ALONG_Y, ALONG_X)
    rows, cols = master.shape
    order8 = jnp.stack([
        rep, rep ^ first_bit, rep ^ second_bit, rep ^ 6,
        sibling, sibling ^ second_bit, sibling ^ first_bit, sibling ^ 6,
    ])
    low = place < 2
    order4 = jnp.stack([place, place ^ 1, jnp.where(low, 2, 1), jnp.where(low, 3, 0)])
    order = (order4[:, None] * 8 + order8[None, :]).reshape(-1).astype(jnp.int32)

    own_delta = deltas[0].reshape(4, 2, rows, cols)
    received = swap_cores(lax.dynamic_index_in_dim(own_delta, 1 - core, 1, keepdims=False))
    kept = lax.dynamic_index_in_dim(own_delta, core, 1, keepdims=False)
    weights = [
        lax.dynamic_index_in_dim(
            row_weights(inner_steps, bucket_of_row, r).reshape(4, 2, rows), core, 1, keepdims=False
        )
        for r in (rep, sibling)
    ]

    def chip_sum(replica):
        at = replica // 2

        def pick(array):
            return lax.dynamic_index_in_dim(array, at, 0, keepdims=False)

        return (
            pick(weights[0])[:, None] * pick(kept).astype(jnp.float32)
            + pick(weights[1])[:, None] * pick(received).astype(jnp.float32)
        )

    link = deltas.dtype
    away = rep ^ first_bit
    to_first = jnp.concatenate([chip_sum(away), chip_sum(away ^ second_bit)], 0).astype(link)
    from_first = swap_first(to_first)
    to_second = chip_sum(rep ^ second_bit) + from_first[rows:].astype(jnp.float32)
    from_second = swap_second(to_second.astype(link))
    averaged = chip_sum(rep) + from_first[:rows].astype(jnp.float32) + from_second.astype(jnp.float32)
    master_new, momentum_new = outer_step(averaged, master, momentum)
    layer = master_new.astype(link)

    normed = normalize_in_order(tokens, norm_gain, order, rows, 4)
    total = None
    for at, block in enumerate(gather_along_line(layer)):
        half = jnp.concatenate([block, swap_first(block)], 0)
        other = swap_second(half)
        pieces = [half, other, swap_cores(half), swap_cores(other)]
        total = project(normed[at], pieces, total, at == 3)
    return total, master_new, momentum_new


def on_any(tokens, norm_gain, deltas, inner_steps, bucket_of_row, master, momentum):
    weight = row_weights(inner_steps, bucket_of_row, lax.axis_index("rep"))
    weighted = weight[:, None] * deltas[0].astype(jnp.float32)
    averaged = lax.psum_scatter(weighted, "rep", scatter_dimension=0, tiled=True)
    master_new, momentum_new = outer_step(averaged, master, momentum)
    layer = lax.all_gather(master_new.astype(deltas.dtype), ("fsdp", "rep"), axis=0, tiled=True)
    features = tokens.shape[1]
    order = jnp.arange(features // 256, dtype=jnp.int32)
    (normed,) = normalize_in_order(tokens, norm_gain, order, 256, 1)
    keys = jnp.dot(normed, layer, preferred_element_type=jnp.float32).astype(tokens.dtype)
    return keys, master_new, momentum_new


def solution(mesh):
    in_specs = (
        P(("rep", "fsdp"), None),
        P(),
        P("rep", "fsdp", None),
        P(),
        P("fsdp"),
        P(("fsdp", "rep"), None),
        P(("fsdp", "rep"), None),
    )
    out_specs = (P(("rep", "fsdp"), None), P(("fsdp", "rep"), None), P(("fsdp", "rep"), None))
    is_block = mesh.shape["rep"] == 8 and mesh.shape["fsdp"] == 4
    return jax.shard_map(
        on_block if is_block else on_any,
        mesh=mesh, in_specs=in_specs, out_specs=out_specs, check_vma=False,
    )
```

time: 240 us -> 175 us (0.73)
  local copies, waits for them, and re-layouts: 71.9 us -> 5.06 us
  Pallas kernels: 0 us -> 50.9 us
  starting transfers between devices: 0.08 us -> 30.7 us
  matrix products: 23.8 us -> 0 us
  other arithmetic: 30.1 us -> 8.37 us
  waiting for transfers between devices: 97.2 us -> 78.4 us
  between operations: 14.1 us -> 0.93 us
    ppermute x0 -> x24, waiting for transfers between devices: none -> 78.4 us  [the longest x19 57.9 us: flip(): return lax.ppermute(value, 'rep', perm)]
    reduce_scatter x1 -> x0, waiting for transfers between devices: 72.5 us -> none  [on_device(): lax.psum_scatter(weighted, 'rep', scatter_dimension=0, tiled=True)]
    pallas_call x0 -> x5, Pallas kernels: none -> 50.9 us  [the longest x4 35.4 us: project(): pl.pallas_call(functools.partial(project_kernel, first, last), grid=(rows...]
    gather x1 -> x0, local copies, waits for them, and re-layouts: 48.6 us -> none  [on_device(): columns = jnp.take(normed, column_ids, axis=1)]
    ppermute x0 -> x24, starting transfers between devices: none -> 30.7 us  [the longest x19 20.4 us: flip(): return lax.ppermute(value, 'rep', perm)]
    all_gather x1 -> x0, waiting for transfers between devices: 24.6 us -> none  [on_device(): piece = lax.all_gather(layer, ('rep', 'fsdp'), axis=0, tiled=True)]
    dot_general x1 -> x0, matrix products: 23.8 us -> none  [on_device(): projected = jnp.dot(columns, piece, preferred_element_type=jnp.float32)]
    unnamed x9 -> x21, local copies, waits for them, and re-layouts: 23.2 us -> 3.01 us
  transfers between devices with their start and end apart: 2 -> 24, of which waited for: 2 -> 10; matrix products, arithmetic and copies ran while one was open for 38% -> 1% of each run, Pallas kernels for 0% -> 24%
where the time goes in v1:
time: 175 us; the launch traced here: 174 us
  waiting for transfers between devices  78.4 us (45%)
  Pallas kernels  50.9 us (29%)
  starting transfers between devices  30.7 us (18%)
  other arithmetic  8.37 us (5%)
  local copies, waits for them, and re-layouts  5.06 us (3%)
    ppermute x19, waiting for transfers between devices, flip(): return lax.ppermute(value, 'rep', perm)  57.9 us
    pallas_call x4, Pallas kernels, project(): pl.pallas_call(functools.partial(project_kernel, first, last), grid=(rows...  35.4 us
    ppermute x19, starting transfers between devices, flip(): return lax.ppermute(value, 'rep', perm)  20.4 us
    pallas_call x1, Pallas kernels, normalize_in_order(): pl.pallas_call(functools.partial(normalize_kernel, width=width), grid_spe...  15.5 us
    ppermute x1, waiting for transfers between devices, gather_along_line(): inner_far = lax.ppermute(pair, 'fsdp', [(1, 2), (2, 1)])  8.53 us
    ppermute x1, waiting for transfers between devices, gather_along_line(): pair = lax.ppermute(own, 'fsdp', [(0, 1), (1, 0), (2, 3), (3, 2)])  6.84 us
    ppermute x1, waiting for transfers between devices, gather_along_line(): outer_far = lax.ppermute(inner_far, 'fsdp', [(1, 0), (2, 3)])  5.07 us
    ppermute x1, starting transfers between devices, gather_along_line(): inner_near = lax.ppermute(own, 'fsdp', [(1, 2), (2, 1)])  4.49 us
  transfers between devices with their start and end apart: 24, of which 10 were waited for; matrix products, arithmetic and copies ran while one was open for 1% of the time, Pallas kernels for 24%

profile of v1, /device:TPU:9, one launch (start us, length us, event | category | flops | bytes accessed | tf_op | source)
XLA Modules:
  0.0 174.3 jit_solution(10784318234813394057)
XLA Ops:
  0.7 1.8 %dynamic-slice_bitcast_fusion = bf16[4,256,1024]{2,1,0:T(8,128)(2,1)S(1)} fusion(bf16[4,2,256,1024]{3,2,1,0:T(8,128)(2,1)} %bitcast.63, s32[]{:T(128)S(6)} %select_n.104), kind=kLoop, calls=%fused_computation | loop fusion | bytes 4194308 | tf_op jit(solution)/shard_map/jit(dynamic_index_in_dim)/squeeze | solution.py:153
  2.4 0.7 collective-permute-start
  3.2 0.1 select_reduce_fusion.1
  3.4 3.7 %collective-permute-done = bf16[4,256,1024]{2,1,0:T(8,128)(2,1)} collective-permute-done((bf16[4,256,1024]{2,1,0:T(8,128)(2,1)S(1)}, bf16[4,256,1024]{2,1,0:T(8,128)(2,1)}, u32[]{:S(2)}, u32[]{:S(2)}) %collective-permute-start) | collective-permute-done | bytes 2097184 | tf_op jit(solution)/shard_map/ppermute | solution.py:20
  7.1 1.9 %fusion.6 = (bf16[256,1024]{1,0:T(8,128)(2,1)S(1)}, bf16[256,1024]{1,0:T(8,128)(2,1)S(1)}) fusion(bf16[4,256,1024]{2,1,0:T(8,128)(2,1)} %collective-permute-done, s32[]{:T(128)S(6)} %select_n.106, f32[256]{0:T(256)S(1)} %bitcast.70, bf16[4,2,256,1024]{3,2,1,0:T(8,128)(2,1)} %bitcast.64, s32[]{:T(128)S(6)} %select_n.107, s32[]{:T(128)S(6)} %select_n.102, ...), kind=kLoop, calls=%fused_computation.16 | loop fusion | flops 3145728 | bytes 3149844 | tf_op jit(solution)/shard_map/convert.8
  9.2 1.3 collective-permute-start.1
  10.5 12.7 %collective-permute-done.1 = bf16[512,1024]{1,0:T(8,128)(2,1)S(1)} collective-permute-done((bf16[512,1024]{1,0:T(8,128)(2,1)S(1)}, bf16[512,1024]{1,0:T(8,128)(2,1)S(1)}, u32[]{:S(2)}, u32[]{:S(2)}) %collective-permute-start.1) | collective-permute-done | bytes 1048608 | tf_op jit(solution)/shard_map/ppermute | solution.py:20
  23.2 1.5 fusion.2
  24.7 1.3 collective-permute-start.2
  26.0 7.1 %collective-permute-done.2 = bf16[256,1024]{1,0:T(8,128)(2,1)S(1)} collective-permute-done((bf16[256,1024]{1,0:T(8,128)(2,1)S(1)}, bf16[256,1024]{1,0:T(8,128)(2,1)S(1)}, u32[]{:S(2)}, u32[]{:S(2)}) %collective-permute-start.2) | collective-permute-done | bytes 524320 | tf_op jit(solution)/shard_map/ppermute | solution.py:20
  33.1 3.2 %fusion.12 = (bf16[256,1024]{1,0:T(8,128)(2,1)S(1)}, f32[256,1024]{1,0:T(8,128)}, f32[256,1024]{1,0:T(8,128)}) fusion(f32[256,1024]{1,0:T(8,128)S(1)} %copy-done.5, bf16[256,1024]{1,0:T(8,128)(2,1)S(1)} %collective-permute-done.2, bf16[512,1024]{1,0:T(8,128)(2,1)S(1)} %collective-permute-done.1, bf16[4,256,1024]{2,1,0:T(8,128)(2,1)} %collective-permute-done, ...), kind=kLoop, calls=%fused_computation.48 | loop fusion | flops 4194304 | bytes 6817804 | tf_op jit(solution)/shard_map/convert_element_type | solution.py:181
  36.3 4.5 %collective-permute-start.10 = (bf16[256,1024]{1,0:T(8,128)(2,1)S(1)}, bf16[256,1024]{1,0:T(8,128)(2,1)S(1)}, u32[]{:S(2)}, u32[]{:S(2)}) collective-permute-start(bf16[256,1024]{1,0:T(8,128)(2,1)S(1)} %get-tuple-element.13), channel_id=1, source_target_pairs={{1,2},{2,1},{5,6},{6,5},{9,10},{10,9},{13,14},{14,13},{17,18},{18,... | collective-permute-start | bytes 1572872 | tf_op jit(solution)/shard_map/ppermute | solution.py:128
  40.8 6.8 %collective-permute-done.3 = bf16[256,1024]{1,0:T(8,128)(2,1)S(1)} collective-permute-done((bf16[256,1024]{1,0:T(8,128)(2,1)S(1)}, bf16[256,1024]{1,0:T(8,128)(2,1)S(1)}, u32[]{:S(2)}, u32[]{:S(2)}) %collective-permute-start.3) | collective-permute-done | bytes 524320 | tf_op jit(solution)/shard_map/ppermute | solution.py:127
  47.6 3.2 %collective-permute-start.4 = (bf16[256,1024]{1,0:T(8,128)(2,1)S(1)}, bf16[256,1024]{1,0:T(8,128)(2,1)S(1)}, u32[]{:S(2)}, u32[]{:S(2)}) collective-permute-start(bf16[256,1024]{1,0:T(8,128)(2,1)S(1)} %collective-permute-done.3), channel_id=1, source_target_pairs={{1,2},{2,1},{5,6},{6,5},{9,10},{10,9},{13,14},{14,13},{17,18},{18,... | collective-permute-start | bytes 1572872 | tf_op jit(solution)/shard_map/ppermute | solution.py:129
  50.8 1.3 collective-permute-start.20
  52.1 1.3 collective-permute-start.11
  53.4 8.5 %collective-permute-done.4 = bf16[256,1024]{1,0:T(8,128)(2,1)S(1)} collective-permute-done((bf16[256,1024]{1,0:T(8,128)(2,1)S(1)}, bf16[256,1024]{1,0:T(8,128)(2,1)S(1)}, u32[]{:S(2)}, u32[]{:S(2)}) %collective-permute-start.4) | collective-permute-done | bytes 524320 | tf_op jit(solution)/shard_map/ppermute | solution.py:129
  62.0 1.3 collective-permute-start.5
  63.3 0.1 pad_maximum_fusion.3.refs_0_
  63.4 1.3 collective-permute-start.21
  64.7 3.2 %collective-permute-start.22 = (bf16[512,1024]{1,0:T(8,128)(2,1)S(1)}, bf16[512,1024]{1,0:T(8,128)(2,1)S(1)}, u32[]{:S(2)}, u32[]{:S(2)}) collective-permute-start(bf16[512,1024]{1,0:T(8,128)(2,1)S(1)} %pad_maximum_fusion.3.refs_0_), channel_id=1, source_target_pairs={{0,4},{4,0},{8,12},{12,8},{16,20},{20,16},{24,28},{28,24},{1,5},{5... | collective-permute-start | bytes 3145736 | tf_op jit(solution)/shard_map/ppermute | solution.py:20
  67.9 0.2 collective-permute-start.16
  68.2 1.3 collective-permute-start.12
  69.5 5.1 %collective-permute-done.5 = bf16[256,1024]{1,0:T(8,128)(2,1)S(1)} collective-permute-done((bf16[256,1024]{1,0:T(8,128)(2,1)S(1)}, bf16[256,1024]{1,0:T(8,128)(2,1)S(1)}, u32[]{:S(2)}, u32[]{:S(2)}) %collective-permute-start.5) | collective-permute-done | bytes 524320 | tf_op jit(solution)/shard_map/ppermute | solution.py:131
  74.6 0.1 broadcast_select_fusion.1
  74.7 0.1 collective-permute-start.6
  74.7 7.2 %collective-permute-done.16 = bf16[256,1024]{1,0:T(8,128)(2,1)S(1)} collective-permute-done((bf16[256,1024]{1,0:T(8,128)(2,1)S(1)}, bf16[256,1024]{1,0:T(8,128)(2,1)S(1)}, u32[]{:S(2)}, u32[]{:S(2)}) %collective-permute-start.16) | collective-permute-done | bytes 524320 | tf_op jit(solution)/shard_map/ppermute | solution.py:20
  82.0 1.3 collective-permute-start.17
  83.2 9.8 %collective-permute-done.12 = bf16[256,1024]{1,0:T(8,128)(2,1)S(1)} collective-permute-done((bf16[256,1024]{1,0:T(8,128)(2,1)S(1)}, bf16[256,1024]{1,0:T(8,128)(2,1)S(1)}, u32[]{:S(2)}, u32[]{:S(2)}) %collective-permute-start.12) | collective-permute-done | bytes 524320 | tf_op jit(solution)/shard_map/ppermute | solution.py:20
  93.1 1.3 collective-permute-start.13
  94.4 9.9 %collective-permute-done.6 = bf16[256,1024]{1,0:T(8,128)(2,1)S(1)} collective-permute-done((bf16[256,1024]{1,0:T(8,128)(2,1)S(1)}, bf16[256,1024]{1,0:T(8,128)(2,1)S(1)}, u32[]{:S(2)}, u32[]{:S(2)}) %collective-permute-start.6) | collective-permute-done | bytes 524320 | tf_op jit(solution)/shard_map/ppermute | solution.py:20
  104.3 1.1 pad_maximum_fusion.1.refs_0_
  105.4 1.0 copy-done.3
  106.4 1.2 collective-permute-start.7
  107.6 1.7 collective-permute-start.19
  109.2 7.6 %collective-permute-done.13.refs_1_ = bf16[512,1024]{1,0:T(8,128)(2,1)} collective-permute-done((bf16[512,1024]{1,0:T(8,128)(2,1)S(1)}, bf16[512,1024]{1,0:T(8,128)(2,1)}, u32[]{:S(2)}, u32[]{:S(2)}) %collective-permute-start.13) | collective-permute-done | bytes 1048608 | tf_op jit(solution)/shard_map/ppermute | solution.py:20
  116.8 3.7 %collective-permute-start.15 = (bf16[512,1024]{1,0:T(8,128)(2,1)}, bf16[512,1024]{1,0:T(8,128)(2,1)}, u32[]{:S(2)}, u32[]{:S(2)}) collective-permute-start(bf16[512,1024]{1,0:T(8,128)(2,1)} %collective-permute-done.13.refs_1_), channel_id=1, source_target_pairs={{0,4},{4,0},{8,12},{12,8},{16,20},{20,16},{24,28},{28,24},{1,5},{5... | collective-permute-start | bytes 3145736 | tf_op jit(solution)/shard_map/ppermute | solution.py:20
  120.6 0.1 add_multiply_fusion
  120.6 0.1 stack.55
  120.7 0.1 broadcast_add_fusion
  120.8 0.1 add.135.order
  120.9 15.5 %normalize_in_order.1 = (bf16[1024,2048]{1,0:T(8,128)(2,1)S(1)}, bf16[1024,2048]{1,0:T(8,128)(2,1)}, bf16[1024,2048]{1,0:T(8,128)(2,1)}, bf16[1024,2048]{1,0:T(8,128)(2,1)}) custom-call(s32[32]{0:T(128)S(1)} %add.135.order, bf16[1024,8192]{1,0:T(8,128)(2,1)} %tokens.1, bf16[1,8192]{1,0:T(2,128)(2,1)S(1)} %reshape.112.gain), custom_call_target="tpu_custom_call" | custom-call | flops 50331648 | bytes 33554432 | tf_op jit(solution)/shard_map/normalize_in_order/pallas_call | solution.py:64
  136.5 1.9 %copy-done.2 = bf16[1024,2048]{1,0:T(8,128)(2,1)} copy-done((bf16[1024,2048]{1,0:T(8,128)(2,1)}, bf16[1024,2048]{1,0:T(8,128)(2,1)S(1)}, u32[]{:S(2)}) %copy-start.2) | copy-done | bytes 4194328
  138.5 0.5 collective-permute-start.9
  139.0 8.3 %project.4.refs_4_ = f32[1024,1024]{1,0:T(8,128)} custom-call(bf16[1024,2048]{1,0:T(8,128)(2,1)} %copy-done.2, bf16[512,1024]{1,0:T(8,128)(2,1)S(1)} %copy-done.1, bf16[512,1024]{1,0:T(8,128)(2,1)} %collective-permute-done.21.refs_1_, bf16[512,1024]{1,0:T(8,128)(2,1)S(1)} %copy-done.4, bf16[512,1024]{1,0:T(8,128)(2,1)} %collective-permute-done.23.refs_3_), custom_call_target="tpu_custom_call" | custom-call | flops 4294967296 | bytes 16777216 | tf_op jit(solution)/shard_map/project/pallas_call | solution.py:106
  147.2 9.1 %project.5.refs_4_ = f32[1024,1024]{1,0:T(8,128)} custom-call(bf16[1024,2048]{1,0:T(8,128)(2,1)} %get-tuple-element.9.normed, bf16[512,1024]{1,0:T(8,128)(2,1)S(1)} %constant_dynamic-update-slice_fusion.refs_0_, bf16[512,1024]{1,0:T(8,128)(2,1)S(1)} %collective-permute-done.17.refs_1_, bf16[512,1024]{1,0:T(8,128)(2,1)} %collective-permute-done.18.refs_2_, ...), custom_call_target="tpu_custom_call" | custom-call | flops 4294967296 | bytes 16777216 | tf_op jit(solution)/shard_map/project/pallas_call | solution.py:106
  156.3 9.4 %project.6.refs_4_ = f32[1024,1024]{1,0:T(8,128)} custom-call(bf16[1024,2048]{1,0:T(8,128)(2,1)} %get-tuple-element.8.normed, bf16[512,1024]{1,0:T(8,128)(2,1)S(1)} %pad_maximum_fusion.2.refs_0_, bf16[512,1024]{1,0:T(8,128)(2,1)} %collective-permute-done.13.refs_1_, bf16[512,1024]{1,0:T(8,128)(2,1)} %collective-permute-done.14.refs_2_, ...), custom_call_target="tpu_custom_call" | custom-call | flops 4294967296 | bytes 16777216 | tf_op jit(solution)/shard_map/project/pallas_call | solution.py:106
  165.7 8.6 %project.7 = bf16[1024,1024]{1,0:T(8,128)(2,1)} custom-call(bf16[1024,2048]{1,0:T(8,128)(2,1)} %get-tuple-element.7.normed, bf16[512,1024]{1,0:T(8,128)(2,1)} %pad_maximum_fusion.1.refs_0_, bf16[512,1024]{1,0:T(8,128)(2,1)} %collective-permute-done.7.refs_1_, bf16[512,1024]{1,0:T(8,128)(2,1)S(1)} %collective-permute-done.8.refs_2_, ...), custom_call_target="tpu_custom_call" | custom-call | flops 4294967296 | bytes 16777216 | tf_op jit(solution)/shard_map/project/pallas_call | solution.py:106
  (49 shorter events, 0.5 us)
Async XLA Ops:
  0.6 2.5 %copy-start.8 = (s32[8,16]{1,0:T(8,128)S(1)}, s32[8,16]{1,0:T(8,128)}, u32[]{:S(2)}) copy-start(s32[8,16]{1,0:T(8,128)} %param.10) | copy-start | bytes 1540
  0.6 2.6 %copy-start.9 = (s32[2048]{0:T(1024)S(1)}, s32[2048]{0:T(1024)}, u32[]{:S(2)}) copy-start(s32[2048]{0:T(1024)} %param.11) | copy-start | bytes 24580
  2.4 4.7 %collective-permute-start = (bf16[4,256,1024]{2,1,0:T(8,128)(2,1)S(1)}, bf16[4,256,1024]{2,1,0:T(8,128)(2,1)}, u32[]{:S(2)}, u32[]{:S(2)}) collective-permute-start(bf16[4,256,1024]{2,1,0:T(8,128)(2,1)S(1)} %dynamic-slice_bitcast_fusion), channel_id=1, source_target_pairs={{0,4},{4,0},{8,12},{12,8},{16,20},{20,16},{24,28},{28,24},{1,5},{5... | collective-permute-start | bytes 6291464 | tf_op jit(solution)/shard_map/ppermute | solution.py:20
  9.1 24.0 %copy-start.5 = (f32[256,1024]{1,0:T(8,128)S(1)}, f32[256,1024]{1,0:T(8,128)}, u32[]{:S(2)}) copy-start(f32[256,1024]{1,0:T(8,128)} %param.12) | copy-start | bytes 3145732
  9.1 24.0 %copy-start.6 = (f32[256,1024]{1,0:T(8,128)S(1)}, f32[256,1024]{1,0:T(8,128)}, u32[]{:S(2)}) copy-start(f32[256,1024]{1,0:T(8,128)} %param.13) | copy-start | bytes 3145732
  9.2 14.0 %collective-permute-start.1 = (bf16[512,1024]{1,0:T(8,128)(2,1)S(1)}, bf16[512,1024]{1,0:T(8,128)(2,1)S(1)}, u32[]{:S(2)}, u32[]{:S(2)}) collective-permute-start(bf16[512,1024]{1,0:T(8,128)(2,1)S(1)} %pad_maximum_fusion), channel_id=1, source_target_pairs={{0,8},{4,20},{8,0},{12,28},{16,24},{20,4},{24,16},{28,12},{1,9},{5... | collective-permute-start | bytes 3145736 | tf_op jit(solution)/shard_map/ppermute | solution.py:20
  24.7 8.4 %collective-permute-start.2 = (bf16[256,1024]{1,0:T(8,128)(2,1)S(1)}, bf16[256,1024]{1,0:T(8,128)(2,1)S(1)}, u32[]{:S(2)}, u32[]{:S(2)}) collective-permute-start(bf16[256,1024]{1,0:T(8,128)(2,1)S(1)} %fusion.2), channel_id=1, source_target_pairs={{0,16},{4,12},{8,24},{12,4},{16,0},{20,28},{24,8},{28,20},{1,17},{... | collective-permute-start | bytes 1572872 | tf_op jit(solution)/shard_map/ppermute | solution.py:20
  36.3 11.3 %collective-permute-start.3 = (bf16[256,1024]{1,0:T(8,128)(2,1)S(1)}, bf16[256,1024]{1,0:T(8,128)(2,1)S(1)}, u32[]{:S(2)}, u32[]{:S(2)}) collective-permute-start(bf16[256,1024]{1,0:T(8,128)(2,1)S(1)} %get-tuple-element.13), channel_id=1, source_target_pairs={{0,1},{1,0},{2,3},{3,2},{4,5},{5,4},{6,7},{7,6},{8,9},{9,8},{10,11... | collective-permute-start | bytes 1572872 | tf_op jit(solution)/shard_map/ppermute | solution.py:127
  36.3 15.8 %collective-permute-start.10 = (bf16[256,1024]{1,0:T(8,128)(2,1)S(1)}, bf16[256,1024]{1,0:T(8,128)(2,1)S(1)}, u32[]{:S(2)}, u32[]{:S(2)}) collective-permute-start(bf16[256,1024]{1,0:T(8,128)(2,1)S(1)} %get-tuple-element.13), channel_id=1, source_target_pairs={{1,2},{2,1},{5,6},{6,5},{9,10},{10,9},{13,14},{14,13},{17,18},{18,... | collective-permute-start | bytes 1572872 | tf_op jit(solution)/shard_map/ppermute | solution.py:128
  47.6 14.4 %collective-permute-start.4 = (bf16[256,1024]{1,0:T(8,128)(2,1)S(1)}, bf16[256,1024]{1,0:T(8,128)(2,1)S(1)}, u32[]{:S(2)}, u32[]{:S(2)}) collective-permute-start(bf16[256,1024]{1,0:T(8,128)(2,1)S(1)} %collective-permute-done.3), channel_id=1, source_target_pairs={{1,2},{2,1},{5,6},{6,5},{9,10},{10,9},{13,14},{14,13},{17,18},{18,... | collective-permute-start | bytes 1572872 | tf_op jit(solution)/shard_map/ppermute | solution.py:129
  50.8 12.5 %collective-permute-start.20 = (bf16[256,1024]{1,0:T(8,128)(2,1)S(1)}, bf16[256,1024]{1,0:T(8,128)(2,1)S(1)}, u32[]{:S(2)}, u32[]{:S(2)}) collective-permute-start(bf16[256,1024]{1,0:T(8,128)(2,1)S(1)} %get-tuple-element.13), channel_id=1, source_target_pairs={{0,8},{4,20},{8,0},{12,28},{16,24},{20,4},{24,16},{28,12},{1,9},{5... | collective-permute-start | bytes 1572872 | tf_op jit(solution)/shard_map/ppermute | solution.py:20
  52.1 16.0 %collective-permute-start.11 = (bf16[256,1024]{1,0:T(8,128)(2,1)S(1)}, bf16[256,1024]{1,0:T(8,128)(2,1)S(1)}, u32[]{:S(2)}, u32[]{:S(2)}) collective-permute-start(bf16[256,1024]{1,0:T(8,128)(2,1)S(1)} %collective-permute-done.10), channel_id=1, source_target_pairs={{1,0},{2,3},{5,4},{6,7},{9,8},{10,11},{13,12},{14,15},{17,16},{18,... | collective-permute-start | bytes 1572872 | tf_op jit(solution)/shard_map/ppermute | solution.py:130
  62.0 12.6 %collective-permute-start.5 = (bf16[256,1024]{1,0:T(8,128)(2,1)S(1)}, bf16[256,1024]{1,0:T(8,128)(2,1)S(1)}, u32[]{:S(2)}, u32[]{:S(2)}) collective-permute-start(bf16[256,1024]{1,0:T(8,128)(2,1)S(1)} %collective-permute-done.4), channel_id=1, source_target_pairs={{1,0},{2,3},{5,4},{6,7},{9,8},{10,11},{13,12},{14,15},{17,16},{18,... | collective-permute-start | bytes 1572872 | tf_op jit(solution)/shard_map/ppermute | solution.py:131
  63.4 11.3 %copy-start = (bf16[512,1024]{1,0:T(8,128)(2,1)}, bf16[512,1024]{1,0:T(8,128)(2,1)S(1)}, u32[]{:S(2)}) copy-start(bf16[512,1024]{1,0:T(8,128)(2,1)S(1)} %pad_maximum_fusion.3.refs_0_) | copy-start | bytes 3145732
  63.4 29.7 %collective-permute-start.21 = (bf16[512,1024]{1,0:T(8,128)(2,1)S(1)}, bf16[512,1024]{1,0:T(8,128)(2,1)}, u32[]{:S(2)}, u32[]{:S(2)}) collective-permute-start(bf16[512,1024]{1,0:T(8,128)(2,1)S(1)} %pad_maximum_fusion.3.refs_0_), channel_id=1, source_target_pairs={{0,16},{4,12},{8,24},{12,4},{16,0},{20,28},{24,8},{28,20},{1,17},{... | collective-permute-start | bytes 3145736 | tf_op jit(solution)/shard_map/ppermute | solution.py:20
  64.7 40.7 %collective-permute-start.22 = (bf16[512,1024]{1,0:T(8,128)(2,1)S(1)}, bf16[512,1024]{1,0:T(8,128)(2,1)S(1)}, u32[]{:S(2)}, u32[]{:S(2)}) collective-permute-start(bf16[512,1024]{1,0:T(8,128)(2,1)S(1)} %pad_maximum_fusion.3.refs_0_), channel_id=1, source_target_pairs={{0,4},{4,0},{8,12},{12,8},{16,20},{20,16},{24,28},{28,24},{1,5},{5... | collective-permute-start | bytes 3145736 | tf_op jit(solution)/shard_map/ppermute | solution.py:20
  67.9 14.1 %collective-permute-start.16 = (bf16[256,1024]{1,0:T(8,128)(2,1)S(1)}, bf16[256,1024]{1,0:T(8,128)(2,1)S(1)}, u32[]{:S(2)}, u32[]{:S(2)}) collective-permute-start(bf16[256,1024]{1,0:T(8,128)(2,1)S(1)} %collective-permute-done.3), channel_id=1, source_target_pairs={{0,8},{4,20},{8,0},{12,28},{16,24},{20,4},{24,16},{28,12},{1,9},{5... | collective-permute-start | bytes 1572872 | tf_op jit(solution)/shard_map/ppermute | solution.py:20
  68.2 24.8 %collective-permute-start.12 = (bf16[256,1024]{1,0:T(8,128)(2,1)S(1)}, bf16[256,1024]{1,0:T(8,128)(2,1)S(1)}, u32[]{:S(2)}, u32[]{:S(2)}) collective-permute-start(bf16[256,1024]{1,0:T(8,128)(2,1)S(1)} %broadcast_select_fusion), channel_id=1, source_target_pairs={{0,8},{4,20},{8,0},{12,28},{16,24},{20,4},{24,16},{28,12},{1,9},{5... | collective-permute-start | bytes 1572872 | tf_op jit(solution)/shard_map/ppermute | solution.py:20
  74.7 29.6 %collective-permute-start.6 = (bf16[256,1024]{1,0:T(8,128)(2,1)S(1)}, bf16[256,1024]{1,0:T(8,128)(2,1)S(1)}, u32[]{:S(2)}, u32[]{:S(2)}) collective-permute-start(bf16[256,1024]{1,0:T(8,128)(2,1)S(1)} %broadcast_select_fusion.1), channel_id=1, source_target_pairs={{0,8},{4,20},{8,0},{12,28},{16,24},{20,4},{24,16},{28,12},{1,9},{5... | collective-permute-start | bytes 1572872 | tf_op jit(solution)/shard_map/ppermute | solution.py:20
  82.0 38.9 %copy-start.7 = (bf16[8192]{0:T(1024)(128)(2,1)S(1)}, bf16[8192]{0:T(1024)(128)(2,1)}, u32[]{:S(2)}) copy-start(bf16[8192]{0:T(1024)(128)(2,1)} %param.8) | copy-start | bytes 49156
  82.0 25.6 %collective-permute-start.17 = (bf16[512,1024]{1,0:T(8,128)(2,1)S(1)}, bf16[512,1024]{1,0:T(8,128)(2,1)S(1)}, u32[]{:S(2)}, u32[]{:S(2)}) collective-permute-start(bf16[512,1024]{1,0:T(8,128)(2,1)S(1)} %constant_dynamic-update-slice_fusion.refs_0_), channel_id=1, source_target_pairs={{0,16},{4,12},{8,24},{12,4},{16,0},{20,28},{24,8},{28,20},{1,17},{... | collective-permute-start | bytes 3145736 | tf_op jit(solution)/shard_map/ppermute | solution.py:20
  93.0 16.2 %collective-permute-start.18 = (bf16[512,1024]{1,0:T(8,128)(2,1)S(1)}, bf16[512,1024]{1,0:T(8,128)(2,1)}, u32[]{:S(2)}, u32[]{:S(2)}) collective-permute-start(bf16[512,1024]{1,0:T(8,128)(2,1)S(1)} %constant_dynamic-update-slice_fusion.refs_0_), channel_id=1, source_target_pairs={{0,4},{4,0},{8,12},{12,8},{16,20},{20,16},{24,28},{28,24},{1,5},{5... | collective-permute-start | bytes 3145736 | tf_op jit(solution)/shard_map/ppermute | solution.py:20
  93.1 23.7 %collective-permute-start.13 = (bf16[512,1024]{1,0:T(8,128)(2,1)S(1)}, bf16[512,1024]{1,0:T(8,128)(2,1)}, u32[]{:S(2)}, u32[]{:S(2)}) collective-permute-start(bf16[512,1024]{1,0:T(8,128)(2,1)S(1)} %pad_maximum_fusion.2.refs_0_), channel_id=1, source_target_pairs={{0,16},{4,12},{8,24},{12,4},{16,0},{20,28},{24,8},{28,20},{1,17},{... | collective-permute-start | bytes 3145736 | tf_op jit(solution)/shard_map/ppermute | solution.py:20
  104.3 34.2 %collective-permute-start.23 = (bf16[512,1024]{1,0:T(8,128)(2,1)}, bf16[512,1024]{1,0:T(8,128)(2,1)}, u32[]{:S(2)}, u32[]{:S(2)}) collective-permute-start(bf16[512,1024]{1,0:T(8,128)(2,1)} %collective-permute-done.21.refs_1_), channel_id=1, source_target_pairs={{0,4},{4,0},{8,12},{12,8},{16,20},{20,16},{24,28},{28,24},{1,5},{5... | collective-permute-start | bytes 3145736 | tf_op jit(solution)/shard_map/ppermute | solution.py:20
  105.4 1.0 copy-start.3
  106.4 32.1 %collective-permute-start.7 = (bf16[512,1024]{1,0:T(8,128)(2,1)}, bf16[512,1024]{1,0:T(8,128)(2,1)}, u32[]{:S(2)}, u32[]{:S(2)}) collective-permute-start(bf16[512,1024]{1,0:T(8,128)(2,1)} %pad_maximum_fusion.1.refs_0_), channel_id=1, source_target_pairs={{0,16},{4,12},{8,24},{12,4},{16,0},{20,28},{24,8},{28,20},{1,17},{... | collective-permute-start | bytes 3145736 | tf_op jit(solution)/shard_map/ppermute | solution.py:20
  107.6 39.7 %collective-permute-start.19 = (bf16[512,1024]{1,0:T(8,128)(2,1)S(1)}, bf16[512,1024]{1,0:T(8,128)(2,1)}, u32[]{:S(2)}, u32[]{:S(2)}) collective-permute-start(bf16[512,1024]{1,0:T(8,128)(2,1)S(1)} %collective-permute-done.17.refs_1_), channel_id=1, source_target_pairs={{0,4},{4,0},{8,12},{12,8},{16,20},{20,16},{24,28},{28,24},{1,5},{5... | collective-permute-start | bytes 3145736 | tf_op jit(solution)/shard_map/ppermute | solution.py:20
  109.2 47.1 %collective-permute-start.14 = (bf16[512,1024]{1,0:T(8,128)(2,1)S(1)}, bf16[512,1024]{1,0:T(8,128)(2,1)}, u32[]{:S(2)}, u32[]{:S(2)}) collective-permute-start(bf16[512,1024]{1,0:T(8,128)(2,1)S(1)} %pad_maximum_fusion.2.refs_0_), channel_id=1, source_target_pairs={{0,4},{4,0},{8,12},{12,8},{16,20},{20,16},{24,28},{28,24},{1,5},{5... | collective-permute-start | bytes 3145736 | tf_op jit(solution)/shard_map/ppermute | solution.py:20
  116.8 39.5 %collective-permute-start.15 = (bf16[512,1024]{1,0:T(8,128)(2,1)}, bf16[512,1024]{1,0:T(8,128)(2,1)}, u32[]{:S(2)}, u32[]{:S(2)}) collective-permute-start(bf16[512,1024]{1,0:T(8,128)(2,1)} %collective-permute-done.13.refs_1_), channel_id=1, source_target_pairs={{0,4},{4,0},{8,12},{12,8},{16,20},{20,16},{24,28},{28,24},{1,5},{5... | collective-permute-start | bytes 3145736 | tf_op jit(solution)/shard_map/ppermute | solution.py:20
  120.9 18.0 %copy-start.1 = (bf16[512,1024]{1,0:T(8,128)(2,1)S(1)}, bf16[512,1024]{1,0:T(8,128)(2,1)}, u32[]{:S(2)}) copy-start(bf16[512,1024]{1,0:T(8,128)(2,1)} %copy-done) | copy-start | bytes 3145732
  120.9 18.0 %copy-start.4 = (bf16[512,1024]{1,0:T(8,128)(2,1)S(1)}, bf16[512,1024]{1,0:T(8,128)(2,1)}, u32[]{:S(2)}) copy-start(bf16[512,1024]{1,0:T(8,128)(2,1)} %copy-done.3) | copy-start | bytes 3145732
  136.5 1.9 %copy-start.2 = (bf16[1024,2048]{1,0:T(8,128)(2,1)}, bf16[1024,2048]{1,0:T(8,128)(2,1)S(1)}, u32[]{:S(2)}) copy-start(bf16[1024,2048]{1,0:T(8,128)(2,1)S(1)} %get-tuple-element.10.normed) | copy-start | bytes 12582916
  138.4 27.3 %collective-permute-start.8 = (bf16[512,1024]{1,0:T(8,128)(2,1)}, bf16[512,1024]{1,0:T(8,128)(2,1)S(1)}, u32[]{:S(2)}, u32[]{:S(2)}) collective-permute-start(bf16[512,1024]{1,0:T(8,128)(2,1)} %pad_maximum_fusion.1.refs_0_), channel_id=1, source_target_pairs={{0,4},{4,0},{8,12},{12,8},{16,20},{20,16},{24,28},{28,24},{1,5},{5... | collective-permute-start | bytes 3145736 | tf_op jit(solution)/shard_map/ppermute | solution.py:20
  138.5 27.2 %collective-permute-start.9 = (bf16[512,1024]{1,0:T(8,128)(2,1)}, bf16[512,1024]{1,0:T(8,128)(2,1)S(1)}, u32[]{:S(2)}, u32[]{:S(2)}) collective-permute-start(bf16[512,1024]{1,0:T(8,128)(2,1)} %collective-permute-done.7.refs_1_), channel_id=1, source_target_pairs={{0,4},{4,0},{8,12},{12,8},{16,20},{20,16},{24,28},{28,24},{1,5},{5... | collective-permute-start | bytes 3145736 | tf_op jit(solution)/shard_map/ppermute | solution.py:20

commit v2 on v1

v2 whole, which is shorter than its diff:
```python
import functools

import jax
import jax.numpy as jnp
from jax import lax
from jax.experimental import pallas as pl
from jax.experimental.pallas import tpu as pltpu
from jax.sharding import PartitionSpec as P

OUTER_RATE = 0.7
MOMENTUM_KEEP = 0.9
EPSILON = 1e-05
VMEM_BYTES = 24 * 1024 * 1024

CORE, ALONG_X, ALONG_Y = 1, 2, 4


def flip(value, even_bit, odd_bit):
    perm = [(i, i ^ (odd_bit if i & CORE else even_bit)) for i in range(8)]
    return lax.ppermute(value, "rep", perm)


def swap_cores(value):
    return flip(value, CORE, CORE)


def swap_first(value):
    return flip(value, ALONG_X, ALONG_Y)


def swap_second(value):
    return flip(value, ALONG_Y, ALONG_X)


def row_weights(inner_steps, bucket_of_row, replica):
    counts = inner_steps.astype(jnp.float32)
    share = counts / jnp.sum(counts, axis=0, keepdims=True)
    own = lax.dynamic_index_in_dim(share, replica, 0, keepdims=False)
    bucket_ids = jnp.arange(counts.shape[1], dtype=jnp.int32)
    one_hot = (bucket_of_row[:, None] == bucket_ids[None, :]).astype(jnp.float32)
    return jnp.sum(one_hot * own[None, :], axis=1)


def outer_step(averaged, master, momentum):
    momentum_new = MOMENTUM_KEEP * momentum + averaged
    master_new = master - OUTER_RATE * (averaged + MOMENTUM_KEEP * momentum_new)
    return master_new, momentum_new


def normalize_kernel(order, tokens, gain, *refs, width, parts):
    outs = refs[len(refs) - parts - 1:-1]
    refs[-1][...] = jnp.zeros_like(refs[-1])
    values = tokens[...].astype(jnp.float32)
    scale = lax.rsqrt(jnp.mean(values * values, axis=1, keepdims=True) + EPSILON)
    at = 0
    for out in outs:
        for j in range(out.shape[1] // width):
            source = pl.ds(pl.multiple_of(order[at] * width, width), width)
            at += 1
            part = tokens[:, source].astype(jnp.float32) * scale * gain[:, source].astype(jnp.float32)
            out[:, j * width:(j + 1) * width] = part.astype(out.dtype)


def normalize_in_order(tokens, gain, order, width, parts, first=0, count=None, earlier=()):
    rows, features = tokens.shape
    tile = 128
    count = rows // tile if count is None else count
    return list(pl.pallas_call(
        functools.partial(normalize_kernel, width=width, parts=len(parts)),
        grid_spec=pltpu.PrefetchScalarGridSpec(
            num_scalar_prefetch=1,
            grid=(count,),
            in_specs=[
                pl.BlockSpec((tile, features), lambda i, order: (i + first, 0)),
                pl.BlockSpec((1, features), lambda i, order: (0, 0)),
            ] + [pl.BlockSpec(memory_space=pl.ANY)] * len(earlier),
            out_specs=[pl.BlockSpec((tile, part), lambda i, order: (i + first, 0)) for part in parts]
            + [pl.BlockSpec((8, 128), lambda i, order: (0, 0))],
        ),
        out_shape=[pltpu.HBM((rows, part), tokens.dtype) for part in parts]
        + [jax.ShapeDtypeStruct((8, 128), jnp.float32)],
        input_output_aliases={3 + i: i for i in range(len(earlier))},
        compiler_params=pltpu.CompilerParams(vmem_limit_bytes=VMEM_BYTES),
        cost_estimate=pl.CostEstimate(
            flops=count * tile * features * 6,
            bytes_accessed=count * tile * features * 4,
            transcendentals=count * tile,
        ),
        name="normalize_in_order",
    )(order, tokens, gain.reshape(1, features), *earlier))


def project_kernel(depths, normed, *refs):
    total = None
    start = 0
    for depth, piece in zip(depths, refs):
        term = jnp.dot(
            normed[:, start:start + depth], piece[...], preferred_element_type=jnp.float32
        )
        total = term if total is None else total + term
        start += depth
    if refs[-2].shape == total.shape:
        total = total + refs[-2][...]
    refs[-1][...] = total.astype(refs[-1].dtype)


def project(normed, pieces, total, last=False):
    rows = normed.shape[0]
    cols = pieces[0].shape[1]
    depths = [piece.shape[0] for piece in pieces]
    depth = sum(depths)
    tile = 256
    first = total.shape != (rows, cols)
    row_spec = pl.BlockSpec((tile, cols), lambda i: (i, 0))
    return pl.pallas_call(
        functools.partial(project_kernel, depths),
        grid=(rows // tile,),
        in_specs=[pl.BlockSpec((tile, depth), lambda i: (i, 0))]
        + [pl.BlockSpec(memory_space=pltpu.VMEM) for piece in pieces]
        + [pl.BlockSpec(memory_space=pl.ANY) if first else row_spec],
        out_specs=row_spec,
        out_shape=jax.ShapeDtypeStruct((rows, cols), normed.dtype if last else jnp.float32),
        compiler_params=pltpu.CompilerParams(vmem_limit_bytes=VMEM_BYTES),
        cost_estimate=pl.CostEstimate(
            flops=2 * rows * depth * cols,
            bytes_accessed=2 * (rows * depth + depth * cols) + 8 * rows * cols,
            transcendentals=0,
        ),
        name="project",
    )(normed, *pieces, total)


def together(*values):
    return lax.optimization_barrier(values)


def to_pair(value):
    return lax.ppermute(value, "fsdp", [(0, 1), (1, 0), (2, 3), (3, 2)])


def inwards(value):
    return lax.ppermute(value, "fsdp", [(1, 2), (2, 1)])


def outwards(value):
    return lax.ppermute(value, "fsdp", [(1, 0), (2, 3)])


def on_block(tokens, norm_gain, deltas, inner_steps, bucket_of_row, master, momentum):
    rep, place = lax.axis_index("rep"), lax.axis_index("fsdp")
    core = rep & 1
    sibling = rep ^ CORE
    first_bit = jnp.where(core == 0, ALONG_X, ALONG_Y)
    second_bit = jnp.where(core == 0, ALONG_Y, ALONG_X)
    rows, cols = master.shape
    tokens = pltpu.with_memory_space_constraint(tokens, pltpu.HBM)
    order8 = jnp.stack([
        rep, rep ^ first_bit, sibling, sibling ^ second_bit,
        rep ^ second_bit, rep ^ 6, sibling ^ first_bit, sibling ^ 6,
    ])
    low = place < 2
    order4 = jnp.stack([place, place ^ 1, jnp.where(low, 2, 1), jnp.where(low, 3, 0)])
    order = (order4[:, None] * 8 + order8[None, :]).reshape(-1).astype(jnp.int32)
    parts = [4 * rows, 8 * rows, 8 * rows, 8 * rows, 4 * rows]

    link = deltas.dtype
    half_rows = rows // 2
    own_delta = deltas[0].reshape(4, 2, 2, half_rows, cols)
    weights = [
        row_weights(inner_steps, bucket_of_row, r).reshape(4, 2, 2, half_rows) for r in (rep, sibling)
    ]

    def pick(array, *index):
        starts = index + (0,) * (array.ndim - len(index))
        sizes = (1,) * len(index) + array.shape[len(index):]
        return lax.dynamic_slice(array, starts, sizes).reshape(array.shape[len(index):])

    def chip_sum(replica, part, received):
        at = replica // 2
        return (
            pick(weights[0], at, core, part)[:, None]
            * pick(own_delta, at, core, part).astype(jnp.float32)
            + pick(weights[1], at, core, part)[:, None] * pick(received, at).astype(jnp.float32)
        )

    received = []
    for part in range(2):
        theirs = lax.dynamic_slice(own_delta, (0, 1 - core, part, 0, 0), (4, 1, 1, half_rows, cols))
        received.append(swap_cores(theirs.reshape(4, half_rows, cols)))
    away = rep ^ first_bit
    from_first = []
    for part in range(2):
        to_first = jnp.concatenate(
            [chip_sum(block, part, received[part]) for block in (away, away ^ second_bit)], 0
        ).astype(link)
        from_first.append(swap_first(to_first))
        received, order, to_first = together(received, order, to_first)
    normed = normalize_in_order(tokens, norm_gain, order, rows, parts, 0, 4)
    own_sum = [chip_sum(rep, part, received[part]) for part in range(2)]
    next_sum = [chip_sum(rep ^ second_bit, part, received[part]) for part in range(2)]
    from_first[0], own_sum, next_sum, normed[-1] = together(from_first[0], own_sum, next_sum, normed[-1])
    from_second = []
    for part in range(2):
        next_sum[part] += from_first[part][half_rows:].astype(jnp.float32)
        own_sum[part] += from_first[part][:half_rows].astype(jnp.float32)
        to_second = next_sum[part].astype(link)
        from_second.append(swap_second(to_second))
        order, to_second = together(order, to_second)
    normed = normalize_in_order(tokens, norm_gain, order, rows, parts, 4, 4, normed)
    from_second[0], normed[-1] = together(from_second[0], normed[-1])
    from_second, own_sum = together(from_second, own_sum)
    averaged = jnp.concatenate(
        [own_sum[part] + from_second[part].astype(jnp.float32) for part in range(2)], 0
    )
    master_new, momentum_new = outer_step(averaged, master, momentum)
    layer = master_new.astype(link)

    outer = (place == 0) | (place == 3)
    pair, near_in = to_pair(layer), inwards(layer)
    beside = swap_first(layer)
    half = jnp.concatenate([layer, beside], 0)
    other = swap_second(half)
    pieces = [half, swap_cores(half)]
    far_in, near_out = inwards(pair), outwards(near_in)
    beside = swap_first(pair)

    beside, other, far_in, near_out = together(beside, other, far_in, near_out)
    half = jnp.concatenate([pair, beside], 0)
    far_out = outwards(far_in)
    near = jnp.where(outer, near_out, near_in)
    last = [other, swap_cores(other)]
    other = swap_second(half)
    beside = swap_first(near)
    half, pieces = together(half, pieces)
    total = project(normed[0], pieces, normed[-1])
    pieces = last + [half, swap_cores(half)]
    far = jnp.where(outer, far_out, far_in)

    beside, other, total = together(beside, other, total)
    half = jnp.concatenate([near, beside], 0)
    last = [other, swap_cores(other)]
    other = swap_second(half)
    beside = swap_first(far)
    half, pieces = together(half, pieces)
    total = project(normed[1], pieces, total)
    pieces = last + [half, swap_cores(half)]

    beside, other, total = together(beside, other, total)
    half = jnp.concatenate([far, beside], 0)
    last = [other, swap_cores(other)]
    other = swap_second(half)
    half, pieces = together(half, pieces)
    total = project(normed[2], pieces, total)
    pieces = last + [half, swap_cores(half)]
    other, total = together(other, total)
    total = project(normed[3], pieces, total)
    last = [other, swap_cores(other)]
    total = project(normed[4], last, total, True)
    return total, master_new, momentum_new


def on_any(tokens, norm_gain, deltas, inner_steps, bucket_of_row, master, momentum):
    weight = row_weights(inner_steps, bucket_of_row, lax.axis_index("rep"))
    weighted = weight[:, None] * deltas[0].astype(jnp.float32)
    averaged = lax.psum_scatter(weighted, "rep", scatter_dimension=0, tiled=True)
    master_new, momentum_new = outer_step(averaged, master, momentum)
    layer = lax.all_gather(master_new.astype(deltas.dtype), ("fsdp", "rep"), axis=0, tiled=True)
    features = tokens.shape[1]
    order = jnp.arange(features // 256, dtype=jnp.int32)
    normed, _ = normalize_in_order(tokens, norm_gain, order, 256, [features])
    keys = jnp.dot(normed, layer, preferred_element_type=jnp.float32).astype(tokens.dtype)
    return keys, master_new, momentum_new


def solution(mesh):
    in_specs = (
        P(("rep", "fsdp"), None),
        P(),
        P("rep", "fsdp", None),
        P(),
        P("fsdp"),
        P(("fsdp", "rep"), None),
        P(("fsdp", "rep"), None),
    )
    out_specs = (P(("rep", "fsdp"), None), P(("fsdp", "rep"), None), P(("fsdp", "rep"), None))
    is_block = mesh.shape["rep"] == 8 and mesh.shape["fsdp"] == 4
    return jax.shard_map(
        on_block if is_block else on_any,
        mesh=mesh, in_specs=in_specs, out_specs=out_specs, check_vma=False,
    )
```

time: 175 us -> 133 us (0.76)
  waiting for transfers between devices: 78.4 us -> 38.2 us
  Pallas kernels: 50.9 us -> 43.5 us
  starting transfers between devices: 30.7 us -> 36 us
    ppermute x19 -> x22, waiting for transfers between devices: 57.9 us -> 28.8 us  [flip(): return lax.ppermute(value, 'rep', perm)]
    ppermute x5, waiting for transfers between devices: 20.4 us -> 9.33 us  [the longest x2 9.07 us: inwards(): return lax.ppermute(value, 'fsdp', [(1, 2), (2, 1)])]
    pallas_call x5 -> x7, Pallas kernels: 50.9 us -> 43.5 us  [the longest x5 25.8 us: project(): pl.pallas_call(functools.partial(project_kernel, depths), grid=(rows // t...]
    ppermute x19 -> x22, starting transfers between devices: 20.4 us -> 26.8 us  [flip(): return lax.ppermute(value, 'rep', perm)]
    add x0 -> x5, other arithmetic: none -> 2.18 us  [the longest x1 1.75 us: chip_sum(): pick(weights[0], at, core, part)[:, None]]
    select_n x2, other arithmetic: 0.13 us -> 2.2 us  [the longest x1 1.1 us: on_block(): near = jnp.where(outer, near_out, near_in)]
    squeeze x1 -> x0, local copies, waits for them, and re-layouts: 1.77 us -> none  [on_block(): lax.dynamic_index_in_dim(own_delta, 1 - core, 1, keepdims=False)]
  transfers between devices with their start and end apart: 24 -> 27, of which waited for: 10 -> 11; matrix products, arithmetic and copies ran while one was open for 1% -> 7% of each run, Pallas kernels for 24% -> 30%
where the time goes in v2:
time: 133 us
  Pallas kernels  43.5 us (33%)
  waiting for transfers between devices  38.2 us (29%)
  starting transfers between devices  36 us (27%)
  other arithmetic  9.47 us (7%)
  local copies, waits for them, and re-layouts  4.65 us (3%)
    ppermute x22, waiting for transfers between devices, flip(): return lax.ppermute(value, 'rep', perm)  28.8 us
    ppermute x22, starting transfers between devices, flip(): return lax.ppermute(value, 'rep', perm)  26.8 us
    pallas_call x5, Pallas kernels, project(): pl.pallas_call(functools.partial(project_kernel, depths), grid=(rows // t...  25.8 us
    pallas_call x2, Pallas kernels, normalize_in_order(): pl.pallas_call(functools.partial(normalize_kernel, width=width, parts=len...  17.6 us
    ppermute x2, waiting for transfers between devices, inwards(): return lax.ppermute(value, 'fsdp', [(1, 2), (2, 1)])  9.07 us
    ppermute x2, starting transfers between devices, inwards(): return lax.ppermute(value, 'fsdp', [(1, 2), (2, 1)])  6.39 us
    ppermute x2, starting transfers between devices, outwards(): return lax.ppermute(value, 'fsdp', [(1, 0), (2, 3)])  2.76 us
    another operation x2, other arithmetic  2.72 us
  transfers between devices with their start and end apart: 27, of which 11 were waited for; matrix products, arithmetic and copies ran while one was open for 7% of the time, Pallas kernels for 30%

profile of v2, /device:TPU:9, one launch (start us, length us, event | category | flops | bytes accessed | tf_op | source)
XLA Modules:
  0.0 132.8 jit_solution(13398824693382935709)
XLA Ops:
  0.7 1.7 %dynamic-slice_bitcast_fusion = (bf16[4,128,1024]{2,1,0:T(8,128)(2,1)S(1)}, bf16[4,128,1024]{2,1,0:T(8,128)(2,1)S(1)}) fusion(bf16[4,2,2,128,1024]{4,3,2,1,0:T(8,128)(2,1)} %bitcast.103, s32[]{:T(128)S(6)} %select_n.60), kind=kLoop, calls=%fused_computation.6 | loop fusion | bytes 4194308 | tf_op jit(solution)/shard_map/reshape | solution.py:189
  2.4 0.7 collective-permute-start
  3.8 2.3 %collective-permute-done = bf16[4,128,1024]{2,1,0:T(8,128)(2,1)S(1)} collective-permute-done((bf16[4,128,1024]{2,1,0:T(8,128)(2,1)S(1)}, bf16[4,128,1024]{2,1,0:T(8,128)(2,1)S(1)}, u32[]{:S(2)}, u32[]{:S(2)}) %collective-permute-start) | collective-permute-done | bytes 1048608 | tf_op jit(solution)/shard_map/ppermute | solution.py:20
  6.1 1.3 fusion.11
  7.5 1.3 collective-permute-start.2
  8.8 1.4 %fusion.7 = (bf16[128,1024]{1,0:T(8,128)(2,1)S(1)}, bf16[128,1024]{1,0:T(8,128)(2,1)S(1)}) fusion(bf16[4,128,1024]{2,1,0:T(8,128)(2,1)} %collective-permute-done.1, s32[]{:T(128)S(6)} %select_n.127, f32[128]{0:T(128)S(1)} %get-tuple-element.151, bf16[4,2,2,128,1024]{4,3,2,1,0:T(8,128)(2,1)} %bitcast.105, s32[]{:T(128)S(6)} %select_n.128, ...), kind=kLoop, calls=%fused_computation.28 | loop fusion | flops 1572864 | bytes 1574924 | tf_op jit(solution)/shard_map/convert.16
  10.3 0.3 collective-permute-start.3
  10.6 8.8 %normalize_in_order.2 = (bf16[1024,1024]{1,0:T(8,128)(2,1)}, bf16[1024,2048]{1,0:T(8,128)(2,1)}, bf16[1024,2048]{1,0:T(8,128)(2,1)}, bf16[1024,2048]{1,0:T(8,128...) custom-call(s32[32]{0:T(128)S(1)} %add.70.order, bf16[1024,8192]{1,0:T(8,128)(2,1)} %tokens.3, ...), custom_call_target="tpu_custom_call" | custom-call | flops 25165824 | bytes 16777216 | tf_op jit(solution)/shard_map/normalize_in_order/pallas_call | solution.py:68
  19.3 1.8 %fusion = (f32[128,1024]{1,0:T(8,128)S(1)}, f32[128,1024]{1,0:T(8,128)S(1)}, f32[128,1024]{1,0:T(8,128)S(1)}, f32[128,1024]{1,0:T(8,128)S(1)}) fusion(bf16[4,128,1024]{2,1,0:T(8,128)(2,1)} %collective-permute-done.1, s32[]{:T(128)S(6)} %select_n.135, f32[128]{0:T(128)S(1)} %get-tuple-element.146, bf16[4,2,2,128,1024]{4,3,2,1,0:T(8,128)(2,1)} %bitcast.106, ...), kind=kLoop, calls=%fused_computation.11 | loop fusion | flops 2621440 | bytes 4198412 | tf_op jit(solution)/shard_map/add | solution.py:181
  21.2 1.3 collective-permute-start.4
  22.7 0.3 collective-permute-start.5
  23.0 8.8 %normalize_in_order.3 = (bf16[1024,1024]{1,0:T(8,128)(2,1)}, bf16[1024,2048]{1,0:T(8,128)(2,1)}, bf16[1024,2048]{1,0:T(8,128)(2,1)}, bf16[1024,2048]{1,0:T(8,128...) custom-call(s32[32]{0:T(128)S(1)} %add.70.order, ...), custom_call_target="tpu_custom_call", output_to_operand_aliasing={{0}: (3, {}), {1}: (4, {}), {2}: (5, {}), {3}: (6, {}), {4}... | custom-call | flops 25165824 | bytes 16777216 | tf_op jit(solution)/shard_map/normalize_in_order/pallas_call | solution.py:68
  32.0 1.8 %fusion.30 = (bf16[256,1024]{1,0:T(8,128)(2,1)S(1)}, f32[256,1024]{1,0:T(8,128)}, f32[256,1024]{1,0:T(8,128)}) fusion(f32[256,1024]{1,0:T(8,128)S(1)} %copy-done.7, f32[128,1024]{1,0:T(8,128)S(1)} %convert_add_fusion, f32[128,1024]{1,0:T(8,128)S(1)} %convert_add_fusion.1, f32[256,1024]{1,0:T(8,128)S(1)} %copy-done.8), kind=kLoop, calls=%fused_computation.91 | loop fusion | flops 2097152 | bytes 5767168 | tf_op jit(solution)/shard_map/convert_element_type | solution.py:216
  33.8 1.3 collective-permute-start.8
  35.1 3.2 %collective-permute-start.11 = (bf16[256,1024]{1,0:T(8,128)(2,1)S(1)}, bf16[256,1024]{1,0:T(8,128)(2,1)S(1)}, u32[]{:S(2)}, u32[]{:S(2)}) collective-permute-start(bf16[256,1024]{1,0:T(8,128)(2,1)S(1)} %get-tuple-element.119), channel_id=1, source_target_pairs={{1,2},{2,1},{5,6},{6,5},{9,10},{10,9},{13,14},{14,13},{17,18},{18,... | collective-permute-start | bytes 1572872 | tf_op jit(solution)/shard_map/ppermute | solution.py:142
  38.4 3.8 %collective-permute-done.8 = bf16[256,1024]{1,0:T(8,128)(2,1)S(1)} collective-permute-done((bf16[256,1024]{1,0:T(8,128)(2,1)S(1)}, bf16[256,1024]{1,0:T(8,128)(2,1)S(1)}, u32[]{:S(2)}, u32[]{:S(2)}) %collective-permute-start.8) | collective-permute-done | bytes 524320 | tf_op jit(solution)/shard_map/ppermute | solution.py:20
  42.2 1.3 collective-permute-start.9
  43.5 5.1 %collective-permute-done.11 = bf16[256,1024]{1,0:T(8,128)(2,1)S(1)} collective-permute-done((bf16[256,1024]{1,0:T(8,128)(2,1)S(1)}, bf16[256,1024]{1,0:T(8,128)(2,1)S(1)}, u32[]{:S(2)}, u32[]{:S(2)}) %collective-permute-start.11) | collective-permute-done | bytes 524320 | tf_op jit(solution)/shard_map/ppermute | solution.py:142
  48.7 1.3 collective-permute-start.12
  50.0 3.2 %collective-permute-start.10 = (bf16[256,1024]{1,0:T(8,128)(2,1)S(1)}, bf16[256,1024]{1,0:T(8,128)(2,1)}, u32[]{:S(2)}, u32[]{:S(2)}) collective-permute-start(bf16[256,1024]{1,0:T(8,128)(2,1)S(1)} %collective-permute-done.6), channel_id=1, source_target_pairs={{1,2},{2,1},{5,6},{6,5},{9,10},{10,9},{13,14},{14,13},{17,18},{18,... | collective-permute-start | bytes 1572872 | tf_op jit(solution)/shard_map/ppermute | solution.py:142
  53.3 4.4 %collective-permute-start.17 = (bf16[512,1024]{1,0:T(8,128)(2,1)S(1)}, bf16[512,1024]{1,0:T(8,128)(2,1)}, u32[]{:S(2)}, u32[]{:S(2)}) collective-permute-start(bf16[512,1024]{1,0:T(8,128)(2,1)S(1)} %pad_maximum_fusion.1.refs_0_), channel_id=1, source_target_pairs={{0,4},{4,0},{8,12},{12,8},{16,20},{20,16},{24,28},{28,24},{1,5},{5... | collective-permute-start | bytes 3145736 | tf_op jit(solution)/shard_map/ppermute | solution.py:20
  57.7 0.8 constant_dynamic-update-slice_fusion.1
  58.8 3.9 %collective-permute-done.10 = bf16[256,1024]{1,0:T(8,128)(2,1)} collective-permute-done((bf16[256,1024]{1,0:T(8,128)(2,1)S(1)}, bf16[256,1024]{1,0:T(8,128)(2,1)}, u32[]{:S(2)}, u32[]{:S(2)}) %collective-permute-start.10) | collective-permute-done | bytes 524320 | tf_op jit(solution)/shard_map/ppermute | solution.py:142
  62.7 2.1 %collective-permute-done.7 = bf16[256,1024]{1,0:T(8,128)(2,1)S(1)} collective-permute-done((bf16[256,1024]{1,0:T(8,128)(2,1)S(1)}, bf16[256,1024]{1,0:T(8,128)(2,1)S(1)}, u32[]{:S(2)}, u32[]{:S(2)}) %collective-permute-start.7) | collective-permute-done | bytes 524320 | tf_op jit(solution)/shard_map/ppermute | solution.py:20
  64.8 1.0 copy-done.5
  65.8 0.8 constant_dynamic-update-slice_fusion.refs_2_
  66.6 1.3 collective-permute-start.16
  67.9 1.1 broadcast_select_fusion
  69.0 1.4 %collective-permute-start.15 = (bf16[256,1024]{1,0:T(8,128)(2,1)S(1)}, bf16[256,1024]{1,0:T(8,128)(2,1)S(1)}, u32[]{:S(2)}, u32[]{:S(2)}) collective-permute-start(bf16[256,1024]{1,0:T(8,128)(2,1)S(1)} %broadcast_select_fusion), channel_id=1, source_target_pairs={{0,8},{4,20},{8,0},{12,28},{16,24},{20,4},{24,16},{28,12},{1,9},{5... | collective-permute-start | bytes 1572872 | tf_op jit(solution)/shard_map/ppermute | solution.py:20
  70.3 1.3 %collective-permute-start.20 = (bf16[512,1024]{1,0:T(8,128)(2,1)}, bf16[512,1024]{1,0:T(8,128)(2,1)S(1)}, u32[]{:S(2)}, u32[]{:S(2)}) collective-permute-start(bf16[512,1024]{1,0:T(8,128)(2,1)} %constant_dynamic-update-slice_fusion.refs_2_), channel_id=1, source_target_pairs={{0,4},{4,0},{8,12},{12,8},{16,20},{20,16},{24,28},{28,24},{1,5},{5... | collective-permute-start | bytes 3145736 | tf_op jit(solution)/shard_map/ppermute | solution.py:20
  71.6 1.5 %collective-permute-start.13 = (bf16[256,1024]{1,0:T(8,128)(2,1)}, bf16[256,1024]{1,0:T(8,128)(2,1)S(1)}, u32[]{:S(2)}, u32[]{:S(2)}) collective-permute-start(bf16[256,1024]{1,0:T(8,128)(2,1)} %collective-permute-done.10), channel_id=1, source_target_pairs={{1,0},{2,3},{5,4},{6,7},{9,8},{10,11},{13,12},{14,15},{17,16},{18,... | collective-permute-start | bytes 1572872 | tf_op jit(solution)/shard_map/ppermute | solution.py:146
  73.1 4.2 %project.5.refs_4_ = f32[1024,1024]{1,0:T(8,128)S(1)} custom-call(bf16[1024,1024]{1,0:T(8,128)(2,1)S(1)} %copy-done.4, bf16[512,1024]{1,0:T(8,128)(2,1)S(1)} %pad_maximum_fusion.1.refs_0_, bf16[512,1024]{1,0:T(8,128)(2,1)} %collective-permute-done.17.refs_1_, f32[8,128]{1,0:T(8,128)S(1)} %get-tuple-element.93.refs_2_), custom_call_target="tpu_custom_call" | custom-call | flops 2147483648 | bytes 12582912 | tf_op jit(solution)/shard_map/project/pallas_call | solution.py:115
  77.4 5.7 %collective-permute-done.15 = bf16[256,1024]{1,0:T(8,128)(2,1)S(1)} collective-permute-done((bf16[256,1024]{1,0:T(8,128)(2,1)S(1)}, bf16[256,1024]{1,0:T(8,128)(2,1)S(1)}, u32[]{:S(2)}, u32[]{:S(2)}) %collective-permute-start.15) | collective-permute-done | bytes 524320 | tf_op jit(solution)/shard_map/ppermute | solution.py:20
  83.1 3.4 %collective-permute-done.16.refs_0_ = bf16[512,1024]{1,0:T(8,128)(2,1)} collective-permute-done((bf16[512,1024]{1,0:T(8,128)(2,1)}, bf16[512,1024]{1,0:T(8,128)(2,1)}, u32[]{:S(2)}, u32[]{:S(2)}) %collective-permute-start.16) | collective-permute-done | bytes 1048608 | tf_op jit(solution)/shard_map/ppermute | solution.py:20
  86.5 1.3 collective-permute-start.18
  87.9 1.1 broadcast_select_fusion.1
  89.0 1.4 %collective-permute-start.14 = (bf16[256,1024]{1,0:T(8,128)(2,1)S(1)}, bf16[256,1024]{1,0:T(8,128)(2,1)S(1)}, u32[]{:S(2)}, u32[]{:S(2)}) collective-permute-start(bf16[256,1024]{1,0:T(8,128)(2,1)S(1)} %broadcast_select_fusion.1), channel_id=1, source_target_pairs={{0,8},{4,20},{8,0},{12,28},{16,24},{20,4},{24,16},{28,12},{1,9},{5... | collective-permute-start | bytes 1572872 | tf_op jit(solution)/shard_map/ppermute | solution.py:20
  90.3 1.9 %collective-permute-start.22 = (bf16[512,1024]{1,0:T(8,128)(2,1)}, bf16[512,1024]{1,0:T(8,128)(2,1)S(1)}, u32[]{:S(2)}, u32[]{:S(2)}) collective-permute-start(bf16[512,1024]{1,0:T(8,128)(2,1)} %collective-permute-done.16.refs_0_), channel_id=1, source_target_pairs={{0,4},{4,0},{8,12},{12,8},{16,20},{20,16},{24,28},{28,24},{1,5},{5... | collective-permute-start | bytes 3145736 | tf_op jit(solution)/shard_map/ppermute | solution.py:20
  92.4 6.4 %project.6.refs_4_ = f32[1024,1024]{1,0:T(8,128)S(1)} custom-call(bf16[1024,2048]{1,0:T(8,128)(2,1)S(1)} %copy-done, bf16[512,1024]{1,0:T(8,128)(2,1)S(1)} %copy-done.6, bf16[512,1024]{1,0:T(8,128)(2,1)S(1)} %collective-permute-done.19.refs_1_, bf16[512,1024]{1,0:T(8,128)(2,1)} %constant_dynamic-update-slice_fusion.refs_2_, ...), custom_call_target="tpu_custom_call" | custom-call | flops 4294967296 | bytes 16777216 | tf_op jit(solution)/shard_map/project/pallas_call | solution.py:115
  98.8 3.8 %collective-permute-done.14 = bf16[256,1024]{1,0:T(8,128)(2,1)S(1)} collective-permute-done((bf16[256,1024]{1,0:T(8,128)(2,1)S(1)}, bf16[256,1024]{1,0:T(8,128)(2,1)S(1)}, u32[]{:S(2)}, u32[]{:S(2)}) %collective-permute-start.14) | collective-permute-done | bytes 524320 | tf_op jit(solution)/shard_map/ppermute | solution.py:20
  102.6 3.6 %collective-permute-done.18.refs_0_ = bf16[512,1024]{1,0:T(8,128)(2,1)S(1)} collective-permute-done((bf16[512,1024]{1,0:T(8,128)(2,1)S(1)}, bf16[512,1024]{1,0:T(8,128)(2,1)S(1)}, u32[]{:S(2)}, u32[]{:S(2)}) %collective-permute-start.18) | collective-permute-done | bytes 1048608 | tf_op jit(solution)/shard_map/ppermute | solution.py:20
  106.2 1.3 collective-permute-start.21
  107.6 2.0 %collective-permute-start.25 = (bf16[512,1024]{1,0:T(8,128)(2,1)S(1)}, bf16[512,1024]{1,0:T(8,128)(2,1)S(1)}, u32[]{:S(2)}, u32[]{:S(2)}) collective-permute-start(bf16[512,1024]{1,0:T(8,128)(2,1)S(1)} %collective-permute-done.18.refs_0_), channel_id=1, source_target_pairs={{0,4},{4,0},{8,12},{12,8},{16,20},{20,16},{24,28},{28,24},{1,5},{5... | collective-permute-start | bytes 3145736 | tf_op jit(solution)/shard_map/ppermute | solution.py:20
  109.7 6.4 %project.7.refs_4_ = f32[1024,1024]{1,0:T(8,128)S(1)} custom-call(bf16[1024,2048]{1,0:T(8,128)(2,1)S(1)} %copy-done.1, bf16[512,1024]{1,0:T(8,128)(2,1)} %collective-permute-done.16.refs_0_, bf16[512,1024]{1,0:T(8,128)(2,1)S(1)} %collective-permute-done.22.refs_1_, bf16[512,1024]{1,0:T(8,128)(2,1)S(1)} %pad_maximum_fusion.2.refs_2_, ...), custom_call_target="tpu_custom_call" | custom-call | flops 4294967296 | bytes 16777216 | tf_op jit(solution)/shard_map/project/pallas_call | solution.py:115
  116.1 4.2 %collective-permute-done.21.refs_0_ = bf16[512,1024]{1,0:T(8,128)(2,1)S(1)} collective-permute-done((bf16[512,1024]{1,0:T(8,128)(2,1)S(1)}, bf16[512,1024]{1,0:T(8,128)(2,1)S(1)}, u32[]{:S(2)}, u32[]{:S(2)}) %collective-permute-start.21) | collective-permute-done | bytes 1048608 | tf_op jit(solution)/shard_map/ppermute | solution.py:20
  120.3 3.7 %collective-permute-start.24 = (bf16[512,1024]{1,0:T(8,128)(2,1)S(1)}, bf16[512,1024]{1,0:T(8,128)(2,1)S(1)}, u32[]{:S(2)}, u32[]{:S(2)}) collective-permute-start(bf16[512,1024]{1,0:T(8,128)(2,1)S(1)} %collective-permute-done.21.refs_0_), channel_id=1, source_target_pairs={{0,4},{4,0},{8,12},{12,8},{16,20},{20,16},{24,28},{28,24},{1,5},{5... | collective-permute-start | bytes 3145736 | tf_op jit(solution)/shard_map/ppermute | solution.py:20
  124.0 5.0 %project.8.refs_2_ = f32[1024,1024]{1,0:T(8,128)S(1)} custom-call(bf16[1024,2048]{1,0:T(8,128)(2,1)S(1)} %copy-done.2, bf16[512,1024]{1,0:T(8,128)(2,1)S(1)} %collective-permute-done.18.refs_0_, bf16[512,1024]{1,0:T(8,128)(2,1)S(1)} %collective-permute-done.25.refs_1_, bf16[512,1024]{1,0:T(8,128)(2,1)S(1)} %pad_maximum_fusion.3.refs_2_, ...), custom_call_target="tpu_custom_call" | custom-call | flops 4294967296 | bytes 16777216 | tf_op jit(solution)/shard_map/project/pallas_call | solution.py:115
  129.0 3.8 %project.9 = bf16[1024,1024]{1,0:T(8,128)(2,1)} custom-call(bf16[1024,1024]{1,0:T(8,128)(2,1)S(1)} %copy-done.3, bf16[512,1024]{1,0:T(8,128)(2,1)S(1)} %collective-permute-done.21.refs_0_, bf16[512,1024]{1,0:T(8,128)(2,1)S(1)} %collective-permute-done.24.refs_1_, f32[1024,1024]{1,0:T(8,128)S(1)} %project.8.refs_2_), custom_call_target="tpu_custom_call" | custom-call | flops 2147483648 | bytes 12582912 | tf_op jit(solution)/shard_map/project/pallas_call | solution.py:115
  (69 shorter events, 1.9 us)
Async XLA Ops:
  0.6 2.9 %copy-start.11 = (bf16[8192]{0:T(1024)(128)(2,1)S(1)}, bf16[8192]{0:T(1024)(128)(2,1)}, u32[]{:S(2)}) copy-start(bf16[8192]{0:T(1024)(128)(2,1)} %param.8) | copy-start | bytes 49156
  0.6 3.0 %copy-start.12 = (s32[8,16]{1,0:T(8,128)S(1)}, s32[8,16]{1,0:T(8,128)}, u32[]{:S(2)}) copy-start(s32[8,16]{1,0:T(8,128)} %param.10) | copy-start | bytes 1540
  0.7 3.0 %copy-start.13 = (s32[2048]{0:T(1024)S(1)}, s32[2048]{0:T(1024)}, u32[]{:S(2)}) copy-start(s32[2048]{0:T(1024)} %param.11) | copy-start | bytes 24580
  2.4 3.7 %collective-permute-start = (bf16[4,128,1024]{2,1,0:T(8,128)(2,1)S(1)}, bf16[4,128,1024]{2,1,0:T(8,128)(2,1)S(1)}, u32[]{:S(2)}, u32[]{:S(2)}) collective-permute-start(bf16[4,128,1024]{2,1,0:T(8,128)(2,1)S(1)} %get-tuple-element.133), channel_id=1, source_target_pairs={{0,4},{4,0},{8,12},{12,8},{16,20},{20,16},{24,28},{28,24},{1,5},{5... | collective-permute-start | bytes 3145736 | tf_op jit(solution)/shard_map/ppermute | solution.py:20
  3.1 5.6 %collective-permute-start.1 = (bf16[4,128,1024]{2,1,0:T(8,128)(2,1)S(1)}, bf16[4,128,1024]{2,1,0:T(8,128)(2,1)}, u32[]{:S(2)}, u32[]{:S(2)}) collective-permute-start(bf16[4,128,1024]{2,1,0:T(8,128)(2,1)S(1)} %get-tuple-element.132), channel_id=1, source_target_pairs={{0,4},{4,0},{8,12},{12,8},{16,20},{20,16},{24,28},{28,24},{1,5},{5... | collective-permute-start | bytes 3145736 | tf_op jit(solution)/shard_map/ppermute | solution.py:20
  7.5 13.6 %collective-permute-start.2 = (bf16[256,1024]{1,0:T(8,128)(2,1)S(1)}, bf16[256,1024]{1,0:T(8,128)(2,1)S(1)}, u32[]{:S(2)}, u32[]{:S(2)}) collective-permute-start(bf16[256,1024]{1,0:T(8,128)(2,1)S(1)} %pad_maximum_fusion.4), channel_id=1, source_target_pairs={{0,8},{4,20},{8,0},{12,28},{16,24},{20,4},{24,16},{28,12},{1,9},{5... | collective-permute-start | bytes 1572872 | tf_op jit(solution)/shard_map/ppermute | solution.py:20
  10.3 12.3 %collective-permute-start.3 = (bf16[256,1024]{1,0:T(8,128)(2,1)S(1)}, bf16[256,1024]{1,0:T(8,128)(2,1)S(1)}, u32[]{:S(2)}, u32[]{:S(2)}) collective-permute-start(bf16[256,1024]{1,0:T(8,128)(2,1)S(1)} %pad_maximum_fusion.5), channel_id=1, source_target_pairs={{0,8},{4,20},{8,0},{12,28},{16,24},{20,4},{24,16},{28,12},{1,9},{5... | collective-permute-start | bytes 1572872 | tf_op jit(solution)/shard_map/ppermute | solution.py:20
  21.2 10.6 %collective-permute-start.4 = (bf16[128,1024]{1,0:T(8,128)(2,1)S(1)}, bf16[128,1024]{1,0:T(8,128)(2,1)S(1)}, u32[]{:S(2)}, u32[]{:S(2)}) collective-permute-start(bf16[128,1024]{1,0:T(8,128)(2,1)S(1)} %get-tuple-element.137), channel_id=1, source_target_pairs={{0,16},{4,12},{8,24},{12,4},{16,0},{20,28},{24,8},{28,20},{1,17},{... | collective-permute-start | bytes 786440 | tf_op jit(solution)/shard_map/ppermute | solution.py:20
  22.7 9.2 %collective-permute-start.5 = (bf16[128,1024]{1,0:T(8,128)(2,1)S(1)}, bf16[128,1024]{1,0:T(8,128)(2,1)S(1)}, u32[]{:S(2)}, u32[]{:S(2)}) collective-permute-start(bf16[128,1024]{1,0:T(8,128)(2,1)S(1)} %get-tuple-element.135), channel_id=1, source_target_pairs={{0,16},{4,12},{8,24},{12,4},{16,0},{20,28},{24,8},{28,20},{1,17},{... | collective-permute-start | bytes 786440 | tf_op jit(solution)/shard_map/ppermute | solution.py:20
  23.0 9.0 %copy-start.7 = (f32[256,1024]{1,0:T(8,128)S(1)}, f32[256,1024]{1,0:T(8,128)}, u32[]{:S(2)}) copy-start(f32[256,1024]{1,0:T(8,128)} %param.12) | copy-start | bytes 3145732
  23.0 9.0 %copy-start.8 = (f32[256,1024]{1,0:T(8,128)S(1)}, f32[256,1024]{1,0:T(8,128)}, u32[]{:S(2)}) copy-start(f32[256,1024]{1,0:T(8,128)} %param.13) | copy-start | bytes 3145732
  33.8 39.3 %copy-start.4 = (bf16[1024,1024]{1,0:T(8,128)(2,1)S(1)}, bf16[1024,1024]{1,0:T(8,128)(2,1)}, u32[]{:S(2)}) copy-start(bf16[1024,1024]{1,0:T(8,128)(2,1)} %get-tuple-element.90.normed) | copy-start | bytes 6291460
  33.8 8.3 %collective-permute-start.8 = (bf16[256,1024]{1,0:T(8,128)(2,1)S(1)}, bf16[256,1024]{1,0:T(8,128)(2,1)S(1)}, u32[]{:S(2)}, u32[]{:S(2)}) collective-permute-start(bf16[256,1024]{1,0:T(8,128)(2,1)S(1)} %get-tuple-element.119), channel_id=1, source_target_pairs={{0,8},{4,20},{8,0},{12,28},{16,24},{20,4},{24,16},{28,12},{1,9},{5... | collective-permute-start | bytes 1572872 | tf_op jit(solution)/shard_map/ppermute | solution.py:20
  35.1 13.5 %collective-permute-start.11 = (bf16[256,1024]{1,0:T(8,128)(2,1)S(1)}, bf16[256,1024]{1,0:T(8,128)(2,1)S(1)}, u32[]{:S(2)}, u32[]{:S(2)}) collective-permute-start(bf16[256,1024]{1,0:T(8,128)(2,1)S(1)} %get-tuple-element.119), channel_id=1, source_target_pairs={{1,2},{2,1},{5,6},{6,5},{9,10},{10,9},{13,14},{14,13},{17,18},{18,... | collective-permute-start | bytes 1572872 | tf_op jit(solution)/shard_map/ppermute | solution.py:142
  38.3 11.7 %collective-permute-start.6 = (bf16[256,1024]{1,0:T(8,128)(2,1)S(1)}, bf16[256,1024]{1,0:T(8,128)(2,1)S(1)}, u32[]{:S(2)}, u32[]{:S(2)}) collective-permute-start(bf16[256,1024]{1,0:T(8,128)(2,1)S(1)} %get-tuple-element.119), channel_id=1, source_target_pairs={{0,1},{1,0},{2,3},{3,2},{4,5},{5,4},{6,7},{7,6},{8,9},{9,8},{10,11... | collective-permute-start | bytes 1572872 | tf_op jit(solution)/shard_map/ppermute | solution.py:138
  42.2 22.6 %collective-permute-start.9 = (bf16[512,1024]{1,0:T(8,128)(2,1)S(1)}, bf16[512,1024]{1,0:T(8,128)(2,1)S(1)}, u32[]{:S(2)}, u32[]{:S(2)}) collective-permute-start(bf16[512,1024]{1,0:T(8,128)(2,1)S(1)} %pad_maximum_fusion.1.refs_0_), channel_id=1, source_target_pairs={{0,16},{4,12},{8,24},{12,4},{16,0},{20,28},{24,8},{28,20},{1,17},{... | collective-permute-start | bytes 3145736 | tf_op jit(solution)/shard_map/ppermute | solution.py:20
  48.7 17.9 %copy-start.9 = (bf16[256,1024]{1,0:T(8,128)(2,1)}, bf16[256,1024]{1,0:T(8,128)(2,1)S(1)}, u32[]{:S(2)}) copy-start(bf16[256,1024]{1,0:T(8,128)(2,1)S(1)} %collective-permute-done.11) | copy-start | bytes 1572868
  48.7 10.1 %collective-permute-start.12 = (bf16[256,1024]{1,0:T(8,128)(2,1)S(1)}, bf16[256,1024]{1,0:T(8,128)(2,1)S(1)}, u32[]{:S(2)}, u32[]{:S(2)}) collective-permute-start(bf16[256,1024]{1,0:T(8,128)(2,1)S(1)} %collective-permute-done.11), channel_id=1, source_target_pairs={{1,0},{2,3},{5,4},{6,7},{9,8},{10,11},{13,12},{14,15},{17,16},{18,... | collective-permute-start | bytes 1572872 | tf_op jit(solution)/shard_map/ppermute | solution.py:146
  50.0 12.7 %collective-permute-start.10 = (bf16[256,1024]{1,0:T(8,128)(2,1)S(1)}, bf16[256,1024]{1,0:T(8,128)(2,1)}, u32[]{:S(2)}, u32[]{:S(2)}) collective-permute-start(bf16[256,1024]{1,0:T(8,128)(2,1)S(1)} %collective-permute-done.6), channel_id=1, source_target_pairs={{1,2},{2,1},{5,6},{6,5},{9,10},{10,9},{13,14},{14,13},{17,18},{18,... | collective-permute-start | bytes 1572872 | tf_op jit(solution)/shard_map/ppermute | solution.py:142
  53.2 11.6 %collective-permute-start.7 = (bf16[256,1024]{1,0:T(8,128)(2,1)S(1)}, bf16[256,1024]{1,0:T(8,128)(2,1)S(1)}, u32[]{:S(2)}, u32[]{:S(2)}) collective-permute-start(bf16[256,1024]{1,0:T(8,128)(2,1)S(1)} %collective-permute-done.6), channel_id=1, source_target_pairs={{0,8},{4,20},{8,0},{12,28},{16,24},{20,4},{24,16},{28,12},{1,9},{5... | collective-permute-start | bytes 1572872 | tf_op jit(solution)/shard_map/ppermute | solution.py:20
  53.3 17.0 %collective-permute-start.17 = (bf16[512,1024]{1,0:T(8,128)(2,1)S(1)}, bf16[512,1024]{1,0:T(8,128)(2,1)}, u32[]{:S(2)}, u32[]{:S(2)}) collective-permute-start(bf16[512,1024]{1,0:T(8,128)(2,1)S(1)} %pad_maximum_fusion.1.refs_0_), channel_id=1, source_target_pairs={{0,4},{4,0},{8,12},{12,8},{16,20},{20,16},{24,28},{28,24},{1,5},{5... | collective-permute-start | bytes 3145736 | tf_op jit(solution)/shard_map/ppermute | solution.py:20
  58.8 7.8 %copy-start.10 = (bf16[256,1024]{1,0:T(8,128)(2,1)}, bf16[256,1024]{1,0:T(8,128)(2,1)S(1)}, u32[]{:S(2)}) copy-start(bf16[256,1024]{1,0:T(8,128)(2,1)S(1)} %collective-permute-done.12) | copy-start | bytes 1572868
  64.8 1.0 copy-start.5
  66.6 19.9 %collective-permute-start.16 = (bf16[512,1024]{1,0:T(8,128)(2,1)}, bf16[512,1024]{1,0:T(8,128)(2,1)}, u32[]{:S(2)}, u32[]{:S(2)}) collective-permute-start(bf16[512,1024]{1,0:T(8,128)(2,1)} %constant_dynamic-update-slice_fusion.refs_2_), channel_id=1, source_target_pairs={{0,16},{4,12},{8,24},{12,4},{16,0},{20,28},{24,8},{28,20},{1,17},{... | collective-permute-start | bytes 3145736 | tf_op jit(solution)/shard_map/ppermute | solution.py:20
  69.0 14.1 %collective-permute-start.15 = (bf16[256,1024]{1,0:T(8,128)(2,1)S(1)}, bf16[256,1024]{1,0:T(8,128)(2,1)S(1)}, u32[]{:S(2)}, u32[]{:S(2)}) collective-permute-start(bf16[256,1024]{1,0:T(8,128)(2,1)S(1)} %broadcast_select_fusion), channel_id=1, source_target_pairs={{0,8},{4,20},{8,0},{12,28},{16,24},{20,4},{24,16},{28,12},{1,9},{5... | collective-permute-start | bytes 1572872 | tf_op jit(solution)/shard_map/ppermute | solution.py:20
  70.3 22.0 %collective-permute-start.20 = (bf16[512,1024]{1,0:T(8,128)(2,1)}, bf16[512,1024]{1,0:T(8,128)(2,1)S(1)}, u32[]{:S(2)}, u32[]{:S(2)}) collective-permute-start(bf16[512,1024]{1,0:T(8,128)(2,1)} %constant_dynamic-update-slice_fusion.refs_2_), channel_id=1, source_target_pairs={{0,4},{4,0},{8,12},{12,8},{16,20},{20,16},{24,28},{28,24},{1,5},{5... | collective-permute-start | bytes 3145736 | tf_op jit(solution)/shard_map/ppermute | solution.py:20
  71.6 20.6 %collective-permute-start.19 = (bf16[512,1024]{1,0:T(8,128)(2,1)}, bf16[512,1024]{1,0:T(8,128)(2,1)S(1)}, u32[]{:S(2)}, u32[]{:S(2)}) collective-permute-start(bf16[512,1024]{1,0:T(8,128)(2,1)} %copy-done.5), channel_id=1, source_target_pairs={{0,4},{4,0},{8,12},{12,8},{16,20},{20,16},{24,28},{28,24},{1,5},{5... | collective-permute-start | bytes 3145736 | tf_op jit(solution)/shard_map/ppermute | solution.py:20
  71.6 16.2 %collective-permute-start.13 = (bf16[256,1024]{1,0:T(8,128)(2,1)}, bf16[256,1024]{1,0:T(8,128)(2,1)S(1)}, u32[]{:S(2)}, u32[]{:S(2)}) collective-permute-start(bf16[256,1024]{1,0:T(8,128)(2,1)} %collective-permute-done.10), channel_id=1, source_target_pairs={{1,0},{2,3},{5,4},{6,7},{9,8},{10,11},{13,12},{14,15},{17,16},{18,... | collective-permute-start | bytes 1572872 | tf_op jit(solution)/shard_map/ppermute | solution.py:146
  73.1 19.2 %copy-start = (bf16[1024,2048]{1,0:T(8,128)(2,1)S(1)}, bf16[1024,2048]{1,0:T(8,128)(2,1)}, u32[]{:S(2)}) copy-start(bf16[1024,2048]{1,0:T(8,128)(2,1)} %get-tuple-element.95.normed) | copy-start | bytes 12582916
  73.1 19.2 %copy-start.6 = (bf16[512,1024]{1,0:T(8,128)(2,1)S(1)}, bf16[512,1024]{1,0:T(8,128)(2,1)}, u32[]{:S(2)}) copy-start(bf16[512,1024]{1,0:T(8,128)(2,1)} %copy-done.5) | copy-start | bytes 3145732
  86.5 19.6 %collective-permute-start.18 = (bf16[512,1024]{1,0:T(8,128)(2,1)S(1)}, bf16[512,1024]{1,0:T(8,128)(2,1)S(1)}, u32[]{:S(2)}, u32[]{:S(2)}) collective-permute-start(bf16[512,1024]{1,0:T(8,128)(2,1)S(1)} %pad_maximum_fusion.2.refs_2_), channel_id=1, source_target_pairs={{0,16},{4,12},{8,24},{12,4},{16,0},{20,28},{24,8},{28,20},{1,17},{... | collective-permute-start | bytes 3145736 | tf_op jit(solution)/shard_map/ppermute | solution.py:20
  89.0 13.6 %collective-permute-start.14 = (bf16[256,1024]{1,0:T(8,128)(2,1)S(1)}, bf16[256,1024]{1,0:T(8,128)(2,1)S(1)}, u32[]{:S(2)}, u32[]{:S(2)}) collective-permute-start(bf16[256,1024]{1,0:T(8,128)(2,1)S(1)} %broadcast_select_fusion.1), channel_id=1, source_target_pairs={{0,8},{4,20},{8,0},{12,28},{16,24},{20,4},{24,16},{28,12},{1,9},{5... | collective-permute-start | bytes 1572872 | tf_op jit(solution)/shard_map/ppermute | solution.py:20
  90.3 19.3 %collective-permute-start.22 = (bf16[512,1024]{1,0:T(8,128)(2,1)}, bf16[512,1024]{1,0:T(8,128)(2,1)S(1)}, u32[]{:S(2)}, u32[]{:S(2)}) collective-permute-start(bf16[512,1024]{1,0:T(8,128)(2,1)} %collective-permute-done.16.refs_0_), channel_id=1, source_target_pairs={{0,4},{4,0},{8,12},{12,8},{16,20},{20,16},{24,28},{28,24},{1,5},{5... | collective-permute-start | bytes 3145736 | tf_op jit(solution)/shard_map/ppermute | solution.py:20
  92.3 17.3 %collective-permute-start.23 = (bf16[512,1024]{1,0:T(8,128)(2,1)S(1)}, bf16[512,1024]{1,0:T(8,128)(2,1)S(1)}, u32[]{:S(2)}, u32[]{:S(2)}) collective-permute-start(bf16[512,1024]{1,0:T(8,128)(2,1)S(1)} %pad_maximum_fusion.2.refs_2_), channel_id=1, source_target_pairs={{0,4},{4,0},{8,12},{12,8},{16,20},{20,16},{24,28},{28,24},{1,5},{5... | collective-permute-start | bytes 3145736 | tf_op jit(solution)/shard_map/ppermute | solution.py:20
  92.3 17.3 %copy-start.1 = (bf16[1024,2048]{1,0:T(8,128)(2,1)S(1)}, bf16[1024,2048]{1,0:T(8,128)(2,1)}, u32[]{:S(2)}) copy-start(bf16[1024,2048]{1,0:T(8,128)(2,1)} %get-tuple-element.104.normed) | copy-start | bytes 12582916
  106.2 14.0 %collective-permute-start.21 = (bf16[512,1024]{1,0:T(8,128)(2,1)S(1)}, bf16[512,1024]{1,0:T(8,128)(2,1)S(1)}, u32[]{:S(2)}, u32[]{:S(2)}) collective-permute-start(bf16[512,1024]{1,0:T(8,128)(2,1)S(1)} %pad_maximum_fusion.3.refs_2_), channel_id=1, source_target_pairs={{0,16},{4,12},{8,24},{12,4},{16,0},{20,28},{24,8},{28,20},{1,17},{... | collective-permute-start | bytes 3145736 | tf_op jit(solution)/shard_map/ppermute | solution.py:20
  107.6 16.4 %collective-permute-start.25 = (bf16[512,1024]{1,0:T(8,128)(2,1)S(1)}, bf16[512,1024]{1,0:T(8,128)(2,1)S(1)}, u32[]{:S(2)}, u32[]{:S(2)}) collective-permute-start(bf16[512,1024]{1,0:T(8,128)(2,1)S(1)} %collective-permute-done.18.refs_0_), channel_id=1, source_target_pairs={{0,4},{4,0},{8,12},{12,8},{16,20},{20,16},{24,28},{28,24},{1,5},{5... | collective-permute-start | bytes 3145736 | tf_op jit(solution)/shard_map/ppermute | solution.py:20
  109.6 14.3 %collective-permute-start.26 = (bf16[512,1024]{1,0:T(8,128)(2,1)S(1)}, bf16[512,1024]{1,0:T(8,128)(2,1)S(1)}, u32[]{:S(2)}, u32[]{:S(2)}) collective-permute-start(bf16[512,1024]{1,0:T(8,128)(2,1)S(1)} %pad_maximum_fusion.3.refs_2_), channel_id=1, source_target_pairs={{0,4},{4,0},{8,12},{12,8},{16,20},{20,16},{24,28},{28,24},{1,5},{5... | collective-permute-start | bytes 3145736 | tf_op jit(solution)/shard_map/ppermute | solution.py:20
  109.7 14.3 %copy-start.2 = (bf16[1024,2048]{1,0:T(8,128)(2,1)S(1)}, bf16[1024,2048]{1,0:T(8,128)(2,1)}, u32[]{:S(2)}) copy-start(bf16[1024,2048]{1,0:T(8,128)(2,1)} %get-tuple-element.113.normed) | copy-start | bytes 12582916
  120.3 8.7 %collective-permute-start.24 = (bf16[512,1024]{1,0:T(8,128)(2,1)S(1)}, bf16[512,1024]{1,0:T(8,128)(2,1)S(1)}, u32[]{:S(2)}, u32[]{:S(2)}) collective-permute-start(bf16[512,1024]{1,0:T(8,128)(2,1)S(1)} %collective-permute-done.21.refs_0_), channel_id=1, source_target_pairs={{0,4},{4,0},{8,12},{12,8},{16,20},{20,16},{24,28},{28,24},{1,5},{5... | collective-permute-start | bytes 3145736 | tf_op jit(solution)/shard_map/ppermute | solution.py:20
  123.9 5.1 %copy-start.3 = (bf16[1024,1024]{1,0:T(8,128)(2,1)S(1)}, bf16[1024,1024]{1,0:T(8,128)(2,1)}, u32[]{:S(2)}) copy-start(bf16[1024,1024]{1,0:T(8,128)(2,1)} %get-tuple-element.78.normed) | copy-start | bytes 6291460

commit v3 on v2

--- a/solution.py
+++ b/solution.py
@@ -154,14 +154,21 @@
     second_bit = jnp.where(core == 0, ALONG_Y, ALONG_X)
     rows, cols = master.shape
     tokens = pltpu.with_memory_space_constraint(tokens, pltpu.HBM)
-    order8 = jnp.stack([
-        rep, rep ^ first_bit, sibling, sibling ^ second_bit,
-        rep ^ second_bit, rep ^ 6, sibling ^ first_bit, sibling ^ 6,
-    ])
     low = place < 2
-    order4 = jnp.stack([place, place ^ 1, jnp.where(low, 2, 1), jnp.where(low, 3, 0)])
-    order = (order4[:, None] * 8 + order8[None, :]).reshape(-1).astype(jnp.int32)
-    parts = [4 * rows, 8 * rows, 8 * rows, 8 * rows, 4 * rows]
+    block_place = [place, place ^ 1, jnp.where(low, 2, 1), jnp.where(low, 3, 0)]
+    half_reps = [rep, rep ^ first_bit, sibling, sibling ^ second_bit]
+    other_reps = [rep ^ second_bit, rep ^ 6, sibling ^ first_bit, sibling ^ 6]
+    sequence = [
+        [(0, half_reps)],
+        [(0, other_reps), (1, half_reps)],
+        [(2, half_reps), (2, other_reps)],
+        [(3, half_reps)],
+        [(1, other_reps), (3, other_reps)],
+    ]
+    order = jnp.stack([
+        block_place[at] * 8 + r for group in sequence for at, reps in group for r in reps
+    ]).astype(jnp.int32)
+    parts = [4 * rows * len(group) for group in sequence]
 
     link = deltas.dtype
     half_rows = rows // 2
@@ -184,9 +191,12 @@
         )
 
     received = []
+    not_mine = 1 - core
     for part in range(2):
-        theirs = lax.dynamic_slice(own_delta, (0, 1 - core, part, 0, 0), (4, 1, 1, half_rows, cols))
-        received.append(swap_cores(theirs.reshape(4, half_rows, cols)))
+        theirs = lax.dynamic_slice(own_delta, (0, not_mine, part, 0, 0), (4, 1, 1, half_rows, cols))
+        theirs = theirs.reshape(4, half_rows, cols)
+        received.append(swap_cores(theirs))
+        not_mine, theirs = together(not_mine, theirs)
     away = rep ^ first_bit
     from_first = []
     for part in range(2):
@@ -195,7 +205,7 @@
         ).astype(link)
         from_first.append(swap_first(to_first))
         received, order, to_first = together(received, order, to_first)
-    normed = normalize_in_order(tokens, norm_gain, order, rows, parts, 0, 4)
+    normed = normalize_in_order(tokens, norm_gain, order, rows, parts, 0, 2)
     own_sum = [chip_sum(rep, part, received[part]) for part in range(2)]
     next_sum = [chip_sum(rep ^ second_bit, part, received[part]) for part in range(2)]
     from_first[0], own_sum, next_sum, normed[-1] = together(from_first[0], own_sum, next_sum, normed[-1])
@@ -206,7 +216,7 @@
         to_second = next_sum[part].astype(link)
         from_second.append(swap_second(to_second))
         order, to_second = together(order, to_second)
-    normed = normalize_in_order(tokens, norm_gain, order, rows, parts, 4, 4, normed)
+    normed = normalize_in_order(tokens, norm_gain, order, rows, parts, 2, 2, normed)
     from_second[0], normed[-1] = together(from_second[0], normed[-1])
     from_second, own_sum = together(from_second, own_sum)
     averaged = jnp.concatenate(
@@ -217,44 +227,45 @@
 
     outer = (place == 0) | (place == 3)
     pair, near_in = to_pair(layer), inwards(layer)
+    pair, near_in = together(pair, near_in)
     beside = swap_first(layer)
-    half = jnp.concatenate([layer, beside], 0)
-    other = swap_second(half)
-    pieces = [half, swap_cores(half)]
+    half0 = jnp.concatenate([layer, beside], 0)
+    other0 = swap_second(half0)
+    half0 = [half0, swap_cores(half0)]
     far_in, near_out = inwards(pair), outwards(near_in)
     beside = swap_first(pair)
 
-    beside, other, far_in, near_out = together(beside, other, far_in, near_out)
-    half = jnp.concatenate([pair, beside], 0)
+    order, pair = together(order, pair)
+    normed = normalize_in_order(tokens, norm_gain, order, rows, parts, 4, 4, normed)
+    beside, other0, near_out, normed[-1] = together(beside, other0, near_out, normed[-1])
+    near = jnp.where(outer, near_out, near_in)
+    half1 = jnp.concatenate([pair, beside], 0)
+    beside = swap_first(near)
     far_out = outwards(far_in)
-    near = jnp.where(outer, near_out, near_in)
-    last = [other, swap_cores(other)]
-    other = swap_second(half)
-    beside = swap_first(near)
-    half, pieces = together(half, pieces)
-    total = project(normed[0], pieces, normed[-1])
-    pieces = last + [half, swap_cores(half)]
+    half1, half0 = together(half1, half0)
+    total = project(normed[0], half0, normed[-1])
+    ready = [other0, swap_cores(other0), half1, swap_cores(half1)]
+
+    beside, total = together(beside, total)
+    half2 = jnp.concatenate([near, beside], 0)
+    other2 = swap_second(half2)
     far = jnp.where(outer, far_out, far_in)
-
-    beside, other, total = together(beside, other, total)
-    half = jnp.concatenate([near, beside], 0)
-    last = [other, swap_cores(other)]
-    other = swap_second(half)
+    far, pair_source = together(far, other0)
     beside = swap_first(far)
-    half, pieces = together(half, pieces)
-    total = project(normed[1], pieces, total)
-    pieces = last + [half, swap_cores(half)]
-
-    beside, other, total = together(beside, other, total)
-    half = jnp.concatenate([far, beside], 0)
-    last = [other, swap_cores(other)]
-    other = swap_second(half)
-    half, pieces = together(half, pieces)
-    total = project(normed[2], pieces, total)
-    pieces = last + [half, swap_cores(half)]
-    other, total = together(other, total)
-    total = project(normed[3], pieces, total)
-    last = [other, swap_cores(other)]
+    other1 = to_pair(pair_source)
+    half2, ready = together(half2, ready)
+    total = project(normed[1], ready, total)
+
+    beside, other2, total = together(beside, other2, total)
+    half3 = jnp.concatenate([far, beside], 0)
+    other3 = swap_second(half3)
+    ready = [half2, swap_cores(half2), other2, swap_cores(other2)]
+    half3, ready = together(half3, ready)
+    total = project(normed[2], ready, total)
+    half3 = [half3, swap_cores(half3)]
+    other3, total = together(other3, total)
+    total = project(normed[3], half3, total)
+    last = [other1, swap_cores(other1), other3, swap_cores(other3)]
     total = project(normed[4], last, total, True)
     return total, master_new, momentum_new
 

time: 133 us -> 125 us (0.940)
  the two profiles are of different devices: /device:TPU:9 before, /device:TPU:0 now
where the time goes in v3:
time: 125 us
  waiting for transfers between devices  45.4 us (36%)
  Pallas kernels  41.2 us (33%)
  starting transfers between devices  22.8 us (18%)
  other arithmetic  9.48 us (8%)
  local copies, waits for them, and re-layouts  4.46 us (4%)
    pallas_call x5, Pallas kernels, project(): pl.pallas_call(functools.partial(project_kernel, depths), grid=(rows // t...  21.7 us
    pallas_call x3, Pallas kernels, normalize_in_order(): pl.pallas_call(functools.partial(normalize_kernel, width=width, parts=len...  19.5 us
    ppermute x21, waiting for transfers between devices, flip(): return lax.ppermute(value, 'rep', perm)  18 us
    ppermute x21, starting transfers between devices, flip(): return lax.ppermute(value, 'rep', perm)  16.5 us
    ppermute x2, waiting for transfers between devices, to_pair(): return lax.ppermute(value, 'fsdp', [(0, 1), (1, 0), (2, 3), (3, 2)])  15.3 us
    ppermute x2, waiting for transfers between devices, outwards(): return lax.ppermute(value, 'fsdp', [(1, 0), (2, 3)])  12.1 us
    another operation x2, other arithmetic  2.72 us
    reshape x2, local copies, waits for them, and re-layouts, on_block(): theirs = theirs.reshape(4, half_rows, cols)  2.6 us
  transfers between devices with their start and end apart: 27, of which 10 were waited for; matrix products, arithmetic and copies ran while one was open for 7% of the time, Pallas kernels for 28%

profile of v3, /device:TPU:0, one launch (start us, length us, event | category | flops | bytes accessed | tf_op | source)
XLA Modules:
  0.0 124.5 jit_solution(17485712684060257840)
XLA Ops:
  0.7 1.3 %dynamic-slice_bitcast_fusion.1 = bf16[4,128,1024]{2,1,0:T(8,128)(2,1)S(1)} fusion(bf16[4,2,2,128,1024]{4,3,2,1,0:T(8,128)(2,1)} %bitcast.123, s32[]{:T(128)S(6)} %select_n.62), kind=kLoop, calls=%fused_computation.7 | loop fusion | bytes 2097156 | tf_op jit(solution)/shard_map/reshape | solution.py:197
  2.0 0.5 collective-permute-start
  2.5 1.3 %dynamic-slice_bitcast_fusion = bf16[4,128,1024]{2,1,0:T(8,128)(2,1)S(1)} fusion(bf16[4,2,2,128,1024]{4,3,2,1,0:T(8,128)(2,1)} %bitcast.124, s32[]{:T(128)S(6)} %select_n.63), kind=kLoop, calls=%fused_computation.6 | loop fusion | bytes 2097156 | tf_op jit(solution)/shard_map/reshape | solution.py:197
  4.4 0.4 collective-permute-done
  4.8 1.3 %fusion.11 = (bf16[128,1024]{1,0:T(8,128)(2,1)S(1)}, bf16[128,1024]{1,0:T(8,128)(2,1)S(1)}) fusion(bf16[4,128,1024]{2,1,0:T(8,128)(2,1)S(1)} %collective-permute-done, s32[]{:T(128)S(6)} %select_n.130, f32[128]{0:T(128)S(1)} %get-tuple-element.178, bf16[4,2,2,128,1024]{4,3,2,1,0:T(8,128)(2,1)} %bitcast.125, s32[]{:T(128)S(6)} %select_n.131, ...), kind=kLoop, calls=%fused_computation.36 | loop fusion | flops 1572864 | bytes 1574924 | tf_op jit(solution)/shard_map/convert.18
  6.1 2.9 %collective-permute-start.2 = (bf16[256,1024]{1,0:T(8,128)(2,1)S(1)}, bf16[256,1024]{1,0:T(8,128)(2,1)S(1)}, u32[]{:S(2)}, u32[]{:S(2)}) collective-permute-start(bf16[256,1024]{1,0:T(8,128)(2,1)S(1)} %pad_maximum_fusion.4), channel_id=1, source_target_pairs={{0,8},{4,20},{8,0},{12,28},{16,24},{20,4},{24,16},{28,12},{1,9},{5... | collective-permute-start | bytes 1572872 | tf_op jit(solution)/shard_map/ppermute | solution.py:20
  9.0 1.4 %fusion.7 = (bf16[128,1024]{1,0:T(8,128)(2,1)S(1)}, bf16[128,1024]{1,0:T(8,128)(2,1)S(1)}) fusion(bf16[4,128,1024]{2,1,0:T(8,128)(2,1)} %collective-permute-done.1, s32[]{:T(128)S(6)} %select_n.130, f32[128]{0:T(128)S(1)} %get-tuple-element.180, bf16[4,2,2,128,1024]{4,3,2,1,0:T(8,128)(2,1)} %bitcast.126, s32[]{:T(128)S(6)} %select_n.131, ...), kind=kLoop, calls=%fused_computation.28 | loop fusion | flops 1572864 | bytes 1574924 | tf_op jit(solution)/shard_map/convert.16
  10.5 0.3 collective-permute-start.3
  10.8 5.2 %normalize_in_order.3 = (bf16[1024,1024]{1,0:T(8,128)(2,1)}, bf16[1024,2048]{1,0:T(8,128)(2,1)}, bf16[1024,2048]{1,0:T(8,128)(2,1)}, bf16[1024,1024]{1,0:T(8,128...) custom-call(s32[32]{0:T(128)S(1)} %stack.131.order, bf16[1024,8192]{1,0:T(8,128)(2,1)} %tokens.5, ...), custom_call_target="tpu_custom_call" | custom-call | flops 12582912 | bytes 8388608 | tf_op jit(solution)/shard_map/normalize_in_order/pallas_call | solution.py:68
  16.0 1.8 %fusion = (f32[128,1024]{1,0:T(8,128)S(1)}, f32[128,1024]{1,0:T(8,128)S(1)}, f32[128,1024]{1,0:T(8,128)S(1)}, f32[128,1024]{1,0:T(8,128)S(1)}) fusion(bf16[4,128,1024]{2,1,0:T(8,128)(2,1)} %collective-permute-done.1, s32[]{:T(128)S(6)} %select_n.138, f32[128]{0:T(128)S(1)} %get-tuple-element.185, bf16[4,2,2,128,1024]{4,3,2,1,0:T(8,128)(2,1)} %bitcast.127, ...), kind=kLoop, calls=%fused_computation.11 | loop fusion | flops 2621440 | bytes 4198412 | tf_op jit(solution)/shard_map/add | solution.py:188
  17.8 0.1 convert_add_fusion.3
  17.9 1.9 %collective-permute-start.4 = (bf16[128,1024]{1,0:T(8,128)(2,1)S(1)}, bf16[128,1024]{1,0:T(8,128)(2,1)S(1)}, u32[]{:S(2)}, u32[]{:S(2)}) collective-permute-start(bf16[128,1024]{1,0:T(8,128)(2,1)S(1)} %get-tuple-element.159), channel_id=1, source_target_pairs={{0,16},{4,12},{8,24},{12,4},{16,0},{20,28},{24,8},{28,20},{1,17},{... | collective-permute-start | bytes 786440 | tf_op jit(solution)/shard_map/ppermute | solution.py:20
  19.8 3.1 %collective-permute-done.3 = bf16[256,1024]{1,0:T(8,128)(2,1)S(1)} collective-permute-done((bf16[256,1024]{1,0:T(8,128)(2,1)S(1)}, bf16[256,1024]{1,0:T(8,128)(2,1)S(1)}, u32[]{:S(2)}, u32[]{:S(2)}) %collective-permute-start.3) | collective-permute-done | bytes 524320 | tf_op jit(solution)/shard_map/ppermute | solution.py:20
  22.9 0.1 convert_add_fusion.2
  23.1 2.8 %collective-permute-start.5 = (bf16[128,1024]{1,0:T(8,128)(2,1)S(1)}, bf16[128,1024]{1,0:T(8,128)(2,1)S(1)}, u32[]{:S(2)}, u32[]{:S(2)}) collective-permute-start(bf16[128,1024]{1,0:T(8,128)(2,1)S(1)} %get-tuple-element.157), channel_id=1, source_target_pairs={{0,16},{4,12},{8,24},{12,4},{16,0},{20,28},{24,8},{28,20},{1,17},{... | collective-permute-start | bytes 786440 | tf_op jit(solution)/shard_map/ppermute | solution.py:20
  25.9 5.3 %normalize_in_order.4 = (bf16[1024,1024]{1,0:T(8,128)(2,1)}, bf16[1024,2048]{1,0:T(8,128)(2,1)}, bf16[1024,2048]{1,0:T(8,128)(2,1)}, bf16[1024,1024]{1,0:T(8,128...) custom-call(s32[32]{0:T(128)S(1)} %stack.131.order, ...), custom_call_target="tpu_custom_call", output_to_operand_aliasing={{0}: (3, {}), {1}: (4, {}), {2}: (5, {}), {3}: (6, {}), {4}... | custom-call | flops 12582912 | bytes 8388608 | tf_op jit(solution)/shard_map/normalize_in_order/pallas_call | solution.py:68
  31.4 1.8 %fusion.30 = (bf16[256,1024]{1,0:T(8,128)(2,1)S(1)}, f32[256,1024]{1,0:T(8,128)}, f32[256,1024]{1,0:T(8,128)}) fusion(f32[256,1024]{1,0:T(8,128)S(1)} %copy-done.5, f32[128,1024]{1,0:T(8,128)S(1)} %convert_add_fusion, f32[128,1024]{1,0:T(8,128)S(1)} %convert_add_fusion.1, f32[256,1024]{1,0:T(8,128)S(1)} %copy-done.6), kind=kLoop, calls=%fused_computation.89 | loop fusion | flops 2097152 | bytes 5767168 | tf_op jit(solution)/shard_map/convert_element_type | solution.py:226
  33.2 1.5 %collective-permute-start.11 = (bf16[256,1024]{1,0:T(8,128)(2,1)S(1)}, bf16[256,1024]{1,0:T(8,128)(2,1)S(1)}, u32[]{:S(2)}, u32[]{:S(2)}) collective-permute-start(bf16[256,1024]{1,0:T(8,128)(2,1)S(1)} %get-tuple-element.143), channel_id=1, source_target_pairs={{0,8},{4,20},{8,0},{12,28},{16,24},{20,4},{24,16},{28,12},{1,9},{5... | collective-permute-start | bytes 1572872 | tf_op jit(solution)/shard_map/ppermute | solution.py:20
  34.7 1.6 %collective-permute-start.6 = (bf16[256,1024]{1,0:T(8,128)(2,1)S(1)}, bf16[256,1024]{1,0:T(8,128)(2,1)}, u32[]{:S(2)}, u32[]{:S(2)}) collective-permute-start(bf16[256,1024]{1,0:T(8,128)(2,1)S(1)} %get-tuple-element.143), channel_id=1, source_target_pairs={{0,1},{1,0},{2,3},{3,2},{4,5},{5,4},{6,7},{7,6},{8,9},{9,8},{10,11... | collective-permute-start | bytes 1572872 | tf_op jit(solution)/shard_map/ppermute | solution.py:138
  36.3 1.5 %collective-permute-start.7 = (bf16[256,1024]{1,0:T(8,128)(2,1)S(1)}, bf16[256,1024]{1,0:T(8,128)(2,1)}, u32[]{:S(2)}, u32[]{:S(2)}) collective-permute-start(bf16[256,1024]{1,0:T(8,128)(2,1)S(1)} %get-tuple-element.143), channel_id=1, source_target_pairs={{1,2},{2,1},{5,6},{6,5},{9,10},{10,9},{13,14},{14,13},{17,18},{18,... | collective-permute-start | bytes 1572872 | tf_op jit(solution)/shard_map/ppermute | solution.py:142
  37.7 5.4 %collective-permute-done.11 = bf16[256,1024]{1,0:T(8,128)(2,1)S(1)} collective-permute-done((bf16[256,1024]{1,0:T(8,128)(2,1)S(1)}, bf16[256,1024]{1,0:T(8,128)(2,1)S(1)}, u32[]{:S(2)}, u32[]{:S(2)}) %collective-permute-start.11) | collective-permute-done | bytes 524320 | tf_op jit(solution)/shard_map/ppermute | solution.py:20
  43.2 0.7 collective-permute-start.12
  43.8 1.7 %collective-permute-done.6 = bf16[256,1024]{1,0:T(8,128)(2,1)} collective-permute-done((bf16[256,1024]{1,0:T(8,128)(2,1)S(1)}, bf16[256,1024]{1,0:T(8,128)(2,1)}, u32[]{:S(2)}, u32[]{:S(2)}) %collective-permute-start.6) | collective-permute-done | bytes 524320 | tf_op jit(solution)/shard_map/ppermute | solution.py:138
  45.5 1.2 collective-permute-start.10
  46.7 1.3 %collective-permute-start.13 = (bf16[256,1024]{1,0:T(8,128)(2,1)}, bf16[256,1024]{1,0:T(8,128)(2,1)}, u32[]{:S(2)}, u32[]{:S(2)}) collective-permute-start(bf16[256,1024]{1,0:T(8,128)(2,1)} %collective-permute-done.7), channel_id=1, source_target_pairs={{1,0},{2,3},{5,4},{6,7},{9,8},{10,11},{13,12},{14,15},{17,16},{18,... | collective-permute-start | bytes 1572872 | tf_op jit(solution)/shard_map/ppermute | solution.py:146
  48.0 0.7 collective-permute-start.8
  48.7 9.0 %normalize_in_order.5 = (bf16[1024,1024]{1,0:T(8,128)(2,1)}, bf16[1024,2048]{1,0:T(8,128)(2,1)}, bf16[1024,2048]{1,0:T(8,128)(2,1)}, bf16[1024,1024]{1,0:T(8,128...) custom-call(s32[32]{0:T(128)S(1)} %stack.131.order, ...), custom_call_target="tpu_custom_call", output_to_operand_aliasing={{0}: (3, {}), {1}: (4, {}), {2}: (5, {}), {3}: (6, {}), {4}... | custom-call | flops 25165824 | bytes 16777216 | tf_op jit(solution)/shard_map/normalize_in_order/pallas_call | solution.py:68
  57.7 1.6 %collective-permute-done.10 = bf16[256,1024]{1,0:T(8,128)(2,1)} collective-permute-done((bf16[256,1024]{1,0:T(8,128)(2,1)}, bf16[256,1024]{1,0:T(8,128)(2,1)}, u32[]{:S(2)}, u32[]{:S(2)}) %collective-permute-start.10) | collective-permute-done | bytes 524320 | tf_op jit(solution)/shard_map/ppermute | solution.py:20
  59.3 2.2 %collective-permute-done.13 = bf16[256,1024]{1,0:T(8,128)(2,1)} collective-permute-done((bf16[256,1024]{1,0:T(8,128)(2,1)}, bf16[256,1024]{1,0:T(8,128)(2,1)}, u32[]{:S(2)}, u32[]{:S(2)}) %collective-permute-start.13) | collective-permute-done | bytes 524320 | tf_op jit(solution)/shard_map/ppermute | solution.py:146
  61.5 3.4 %collective-permute-done.12.refs_0_ = bf16[512,1024]{1,0:T(8,128)(2,1)S(1)} collective-permute-done((bf16[512,1024]{1,0:T(8,128)(2,1)S(1)}, bf16[512,1024]{1,0:T(8,128)(2,1)S(1)}, u32[]{:S(2)}, u32[]{:S(2)}) %collective-permute-start.12) | collective-permute-done | bytes 1048608 | tf_op jit(solution)/shard_map/ppermute | solution.py:20
  64.9 1.1 broadcast_select_fusion
  66.0 1.9 %collective-permute-start.17 = (bf16[256,1024]{1,0:T(8,128)(2,1)S(1)}, bf16[256,1024]{1,0:T(8,128)(2,1)S(1)}, u32[]{:S(2)}, u32[]{:S(2)}) collective-permute-start(bf16[256,1024]{1,0:T(8,128)(2,1)S(1)} %broadcast_select_fusion), channel_id=1, source_target_pairs={{0,8},{4,20},{8,0},{12,28},{16,24},{20,4},{24,16},{28,12},{1,9},{5... | collective-permute-start | bytes 1572872 | tf_op jit(solution)/shard_map/ppermute | solution.py:20
  67.9 1.3 %pad_maximum_fusion.2.refs_2_ = bf16[512,1024]{1,0:T(8,128)(2,1)S(1)} fusion(bf16[256,1024]{1,0:T(8,128)(2,1)} %collective-permute-done.10, bf16[256,1024]{1,0:T(8,128)(2,1)} %collective-permute-done.6), kind=kLoop, calls=%fused_computation.2 | loop fusion | flops 2097152 | bytes 2097152 | tf_op jit(solution)/shard_map/concatenate | solution.py:242
  69.3 0.5 collective-permute-start.21
  69.8 1.3 %collective-permute-start.9 = (bf16[256,1024]{1,0:T(8,128)(2,1)S(1)}, bf16[256,1024]{1,0:T(8,128)(2,1)S(1)}, u32[]{:S(2)}, u32[]{:S(2)}) collective-permute-start(bf16[256,1024]{1,0:T(8,128)(2,1)S(1)} %collective-permute-done.8), channel_id=1, source_target_pairs={{1,0},{2,3},{5,4},{6,7},{9,8},{10,11},{13,12},{14,15},{17,16},{18,... | collective-permute-start | bytes 1572872 | tf_op jit(solution)/shard_map/ppermute | solution.py:146
  71.1 1.6 %copy-done.2 = bf16[1024,1024]{1,0:T(8,128)(2,1)S(1)} copy-done((bf16[1024,1024]{1,0:T(8,128)(2,1)S(1)}, bf16[1024,1024]{1,0:T(8,128)(2,1)}, u32[]{:S(2)}) %copy-start.2) | copy-done | bytes 2097176
  72.7 2.9 %project.5.refs_4_ = f32[1024,1024]{1,0:T(8,128)S(1)} custom-call(bf16[1024,1024]{1,0:T(8,128)(2,1)S(1)} %copy-done.2, bf16[512,1024]{1,0:T(8,128)(2,1)S(1)} %pad_maximum_fusion.1.refs_0_, bf16[512,1024]{1,0:T(8,128)(2,1)S(1)} %collective-permute-done.18.refs_1_, f32[8,128]{1,0:T(8,128)S(1)} %get-tuple-element.119.refs_2_), custom_call_target="tpu_custom_call" | custom-call | flops 2147483648 | bytes 12582912 | tf_op jit(solution)/shard_map/project/pallas_call | solution.py:115
  75.7 9.8 %collective-permute-done.9 = bf16[256,1024]{1,0:T(8,128)(2,1)S(1)} collective-permute-done((bf16[256,1024]{1,0:T(8,128)(2,1)S(1)}, bf16[256,1024]{1,0:T(8,128)(2,1)S(1)}, u32[]{:S(2)}, u32[]{:S(2)}) %collective-permute-start.9) | collective-permute-done | bytes 524320 | tf_op jit(solution)/shard_map/ppermute | solution.py:146
  85.6 0.3 collective-permute-start.16
  86.0 5.1 %project.6.refs_4_ = f32[1024,1024]{1,0:T(8,128)S(1)} custom-call(bf16[1024,2048]{1,0:T(8,128)(2,1)S(1)} %copy-done, bf16[512,1024]{1,0:T(8,128)(2,1)S(1)} %collective-permute-done.12.refs_0_, bf16[512,1024]{1,0:T(8,128)(2,1)S(1)} %collective-permute-done.20.refs_1_, bf16[512,1024]{1,0:T(8,128)(2,1)S(1)} %pad_maximum_fusion.2.refs_2_, ...), custom_call_target="tpu_custom_call" | custom-call | flops 4294967296 | bytes 16777216 | tf_op jit(solution)/shard_map/project/pallas_call | solution.py:115
  91.1 4.1 %collective-permute-done.16 = bf16[256,1024]{1,0:T(8,128)(2,1)S(1)} collective-permute-done((bf16[256,1024]{1,0:T(8,128)(2,1)S(1)}, bf16[256,1024]{1,0:T(8,128)(2,1)S(1)}, u32[]{:S(2)}, u32[]{:S(2)}) %collective-permute-start.16) | collective-permute-done | bytes 524320 | tf_op jit(solution)/shard_map/ppermute | solution.py:20
  95.2 1.0 collective-permute-start.24
  96.4 13.7 %collective-permute-done.14.refs_0_ = bf16[512,1024]{1,0:T(8,128)(2,1)S(1)} collective-permute-done((bf16[512,1024]{1,0:T(8,128)(2,1)S(1)}, bf16[512,1024]{1,0:T(8,128)(2,1)S(1)}, u32[]{:S(2)}, u32[]{:S(2)}) %collective-permute-start.14) | collective-permute-done | bytes 1048608 | tf_op jit(solution)/shard_map/ppermute | solution.py:138
  110.1 0.5 collective-permute-start.26
  110.6 5.0 %project.7.refs_2_ = f32[1024,1024]{1,0:T(8,128)S(1)} custom-call(bf16[1024,2048]{1,0:T(8,128)(2,1)S(1)} %copy-done.1, bf16[512,1024]{1,0:T(8,128)(2,1)S(1)} %pad_maximum_fusion.3.refs_0_, bf16[512,1024]{1,0:T(8,128)(2,1)S(1)} %collective-permute-done.23.refs_1_, bf16[512,1024]{1,0:T(8,128)(2,1)S(1)} %collective-permute-done.19.refs_2_, ...), custom_call_target="tpu_custom_call" | custom-call | flops 4294967296 | bytes 16777216 | tf_op jit(solution)/shard_map/project/pallas_call | solution.py:115
  115.6 0.1 collective-permute-start.25
  115.8 2.9 %project.8.refs_4_ = f32[1024,1024]{1,0:T(8,128)S(1)} custom-call(bf16[1024,1024]{1,0:T(8,128)(2,1)S(1)} %copy-done.3, bf16[512,1024]{1,0:T(8,128)(2,1)S(1)} %constant_dynamic-update-slice_fusion.refs_0_, bf16[512,1024]{1,0:T(8,128)(2,1)S(1)} %collective-permute-done.26.refs_1_, f32[1024,1024]{1,0:T(8,128)S(1)} %project.7.refs_2_), custom_call_target="tpu_custom_call" | custom-call | flops 2147483648 | bytes 12582912 | tf_op jit(solution)/shard_map/project/pallas_call | solution.py:115
  118.7 5.8 %project.9 = bf16[1024,1024]{1,0:T(8,128)(2,1)} custom-call(bf16[1024,2048]{1,0:T(8,128)(2,1)S(1)} %copy-done.4, bf16[512,1024]{1,0:T(8,128)(2,1)S(1)} %collective-permute-done.14.refs_0_, bf16[512,1024]{1,0:T(8,128)(2,1)S(1)} %collective-permute-done.15.refs_1_, bf16[512,1024]{1,0:T(8,128)(2,1)S(1)} %collective-permute-done.22.refs_2_, ...), custom_call_target="tpu_custom_call" | custom-call | flops 4294967296 | bytes 16777216 | tf_op jit(solution)/shard_map/project/pallas_call | solution.py:115
  (60 shorter events, 1.3 us)
Async XLA Ops:
  0.6 3.4 %copy-start.7 = (bf16[8192]{0:T(1024)(128)(2,1)S(1)}, bf16[8192]{0:T(1024)(128)(2,1)}, u32[]{:S(2)}) copy-start(bf16[8192]{0:T(1024)(128)(2,1)} %param.8) | copy-start | bytes 49156
  0.6 3.6 %copy-start.8 = (s32[8,16]{1,0:T(8,128)S(1)}, s32[8,16]{1,0:T(8,128)}, u32[]{:S(2)}) copy-start(s32[8,16]{1,0:T(8,128)} %param.10) | copy-start | bytes 1540
  0.7 3.6 %copy-start.9 = (s32[2048]{0:T(1024)S(1)}, s32[2048]{0:T(1024)}, u32[]{:S(2)}) copy-start(s32[2048]{0:T(1024)} %param.11) | copy-start | bytes 24580
  2.0 2.8 %collective-permute-start = (bf16[4,128,1024]{2,1,0:T(8,128)(2,1)S(1)}, bf16[4,128,1024]{2,1,0:T(8,128)(2,1)S(1)}, u32[]{:S(2)}, u32[]{:S(2)}) collective-permute-start(bf16[4,128,1024]{2,1,0:T(8,128)(2,1)S(1)} %dynamic-slice_bitcast_fusion.1), channel_id=1, source_target_pairs={{0,4},{4,0},{8,12},{12,8},{16,20},{20,16},{24,28},{28,24},{1,5},{5... | collective-permute-start | bytes 3145736 | tf_op jit(solution)/shard_map/ppermute | solution.py:20
  3.8 5.3 %collective-permute-start.1 = (bf16[4,128,1024]{2,1,0:T(8,128)(2,1)S(1)}, bf16[4,128,1024]{2,1,0:T(8,128)(2,1)}, u32[]{:S(2)}, u32[]{:S(2)}) collective-permute-start(bf16[4,128,1024]{2,1,0:T(8,128)(2,1)S(1)} %dynamic-slice_bitcast_fusion), channel_id=1, source_target_pairs={{0,4},{4,0},{8,12},{12,8},{16,20},{20,16},{24,28},{28,24},{1,5},{5... | collective-permute-start | bytes 3145736 | tf_op jit(solution)/shard_map/ppermute | solution.py:20
  6.1 11.6 %collective-permute-start.2 = (bf16[256,1024]{1,0:T(8,128)(2,1)S(1)}, bf16[256,1024]{1,0:T(8,128)(2,1)S(1)}, u32[]{:S(2)}, u32[]{:S(2)}) collective-permute-start(bf16[256,1024]{1,0:T(8,128)(2,1)S(1)} %pad_maximum_fusion.4), channel_id=1, source_target_pairs={{0,8},{4,20},{8,0},{12,28},{16,24},{20,4},{24,16},{28,12},{1,9},{5... | collective-permute-start | bytes 1572872 | tf_op jit(solution)/shard_map/ppermute | solution.py:20
  10.5 12.4 %collective-permute-start.3 = (bf16[256,1024]{1,0:T(8,128)(2,1)S(1)}, bf16[256,1024]{1,0:T(8,128)(2,1)S(1)}, u32[]{:S(2)}, u32[]{:S(2)}) collective-permute-start(bf16[256,1024]{1,0:T(8,128)(2,1)S(1)} %pad_maximum_fusion.5), channel_id=1, source_target_pairs={{0,8},{4,20},{8,0},{12,28},{16,24},{20,4},{24,16},{28,12},{1,9},{5... | collective-permute-start | bytes 1572872 | tf_op jit(solution)/shard_map/ppermute | solution.py:20
  17.9 13.3 %collective-permute-start.4 = (bf16[128,1024]{1,0:T(8,128)(2,1)S(1)}, bf16[128,1024]{1,0:T(8,128)(2,1)S(1)}, u32[]{:S(2)}, u32[]{:S(2)}) collective-permute-start(bf16[128,1024]{1,0:T(8,128)(2,1)S(1)} %get-tuple-element.159), channel_id=1, source_target_pairs={{0,16},{4,12},{8,24},{12,4},{16,0},{20,28},{24,8},{28,20},{1,17},{... | collective-permute-start | bytes 786440 | tf_op jit(solution)/shard_map/ppermute | solution.py:20
  23.1 8.1 %collective-permute-start.5 = (bf16[128,1024]{1,0:T(8,128)(2,1)S(1)}, bf16[128,1024]{1,0:T(8,128)(2,1)S(1)}, u32[]{:S(2)}, u32[]{:S(2)}) collective-permute-start(bf16[128,1024]{1,0:T(8,128)(2,1)S(1)} %get-tuple-element.157), channel_id=1, source_target_pairs={{0,16},{4,12},{8,24},{12,4},{16,0},{20,28},{24,8},{28,20},{1,17},{... | collective-permute-start | bytes 786440 | tf_op jit(solution)/shard_map/ppermute | solution.py:20
  25.9 5.5 %copy-start.5 = (f32[256,1024]{1,0:T(8,128)S(1)}, f32[256,1024]{1,0:T(8,128)}, u32[]{:S(2)}) copy-start(f32[256,1024]{1,0:T(8,128)} %param.12) | copy-start | bytes 3145732
  25.9 5.5 %copy-start.6 = (f32[256,1024]{1,0:T(8,128)S(1)}, f32[256,1024]{1,0:T(8,128)}, u32[]{:S(2)}) copy-start(f32[256,1024]{1,0:T(8,128)} %param.13) | copy-start | bytes 3145732
  33.2 9.9 %collective-permute-start.11 = (bf16[256,1024]{1,0:T(8,128)(2,1)S(1)}, bf16[256,1024]{1,0:T(8,128)(2,1)S(1)}, u32[]{:S(2)}, u32[]{:S(2)}) collective-permute-start(bf16[256,1024]{1,0:T(8,128)(2,1)S(1)} %get-tuple-element.143), channel_id=1, source_target_pairs={{0,8},{4,20},{8,0},{12,28},{16,24},{20,4},{24,16},{28,12},{1,9},{5... | collective-permute-start | bytes 1572872 | tf_op jit(solution)/shard_map/ppermute | solution.py:20
  34.7 10.8 %collective-permute-start.6 = (bf16[256,1024]{1,0:T(8,128)(2,1)S(1)}, bf16[256,1024]{1,0:T(8,128)(2,1)}, u32[]{:S(2)}, u32[]{:S(2)}) collective-permute-start(bf16[256,1024]{1,0:T(8,128)(2,1)S(1)} %get-tuple-element.143), channel_id=1, source_target_pairs={{0,1},{1,0},{2,3},{3,2},{4,5},{5,4},{6,7},{7,6},{8,9},{9,8},{10,11... | collective-permute-start | bytes 1572872 | tf_op jit(solution)/shard_map/ppermute | solution.py:138
  36.3 9.3 %collective-permute-start.7 = (bf16[256,1024]{1,0:T(8,128)(2,1)S(1)}, bf16[256,1024]{1,0:T(8,128)(2,1)}, u32[]{:S(2)}, u32[]{:S(2)}) collective-permute-start(bf16[256,1024]{1,0:T(8,128)(2,1)S(1)} %get-tuple-element.143), channel_id=1, source_target_pairs={{1,2},{2,1},{5,6},{6,5},{9,10},{10,9},{13,14},{14,13},{17,18},{18,... | collective-permute-start | bytes 1572872 | tf_op jit(solution)/shard_map/ppermute | solution.py:142
  43.2 21.8 %collective-permute-start.12 = (bf16[512,1024]{1,0:T(8,128)(2,1)S(1)}, bf16[512,1024]{1,0:T(8,128)(2,1)S(1)}, u32[]{:S(2)}, u32[]{:S(2)}) collective-permute-start(bf16[512,1024]{1,0:T(8,128)(2,1)S(1)} %pad_maximum_fusion.1.refs_0_), channel_id=1, source_target_pairs={{0,16},{4,12},{8,24},{12,4},{16,0},{20,28},{24,8},{28,20},{1,17},{... | collective-permute-start | bytes 3145736 | tf_op jit(solution)/shard_map/ppermute | solution.py:20
  43.8 25.3 %collective-permute-start.18 = (bf16[512,1024]{1,0:T(8,128)(2,1)S(1)}, bf16[512,1024]{1,0:T(8,128)(2,1)S(1)}, u32[]{:S(2)}, u32[]{:S(2)}) collective-permute-start(bf16[512,1024]{1,0:T(8,128)(2,1)S(1)} %pad_maximum_fusion.1.refs_0_), channel_id=1, source_target_pairs={{0,4},{4,0},{8,12},{12,8},{16,20},{20,16},{24,28},{28,24},{1,5},{5... | collective-permute-start | bytes 3145736 | tf_op jit(solution)/shard_map/ppermute | solution.py:20
  45.5 13.8 %collective-permute-start.10 = (bf16[256,1024]{1,0:T(8,128)(2,1)}, bf16[256,1024]{1,0:T(8,128)(2,1)}, u32[]{:S(2)}, u32[]{:S(2)}) collective-permute-start(bf16[256,1024]{1,0:T(8,128)(2,1)} %collective-permute-done.6), channel_id=1, source_target_pairs={{0,8},{4,20},{8,0},{12,28},{16,24},{20,4},{24,16},{28,12},{1,9},{5... | collective-permute-start | bytes 1572872 | tf_op jit(solution)/shard_map/ppermute | solution.py:20
  46.7 14.8 %collective-permute-start.13 = (bf16[256,1024]{1,0:T(8,128)(2,1)}, bf16[256,1024]{1,0:T(8,128)(2,1)}, u32[]{:S(2)}, u32[]{:S(2)}) collective-permute-start(bf16[256,1024]{1,0:T(8,128)(2,1)} %collective-permute-done.7), channel_id=1, source_target_pairs={{1,0},{2,3},{5,4},{6,7},{9,8},{10,11},{13,12},{14,15},{17,16},{18,... | collective-permute-start | bytes 1572872 | tf_op jit(solution)/shard_map/ppermute | solution.py:146
  48.0 21.7 %collective-permute-start.8 = (bf16[256,1024]{1,0:T(8,128)(2,1)}, bf16[256,1024]{1,0:T(8,128)(2,1)S(1)}, u32[]{:S(2)}, u32[]{:S(2)}) collective-permute-start(bf16[256,1024]{1,0:T(8,128)(2,1)} %collective-permute-done.6), channel_id=1, source_target_pairs={{1,2},{2,1},{5,6},{6,5},{9,10},{10,9},{13,14},{14,13},{17,18},{18,... | collective-permute-start | bytes 1572872 | tf_op jit(solution)/shard_map/ppermute | solution.py:142
  66.0 9.5 %collective-permute-start.17 = (bf16[256,1024]{1,0:T(8,128)(2,1)S(1)}, bf16[256,1024]{1,0:T(8,128)(2,1)S(1)}, u32[]{:S(2)}, u32[]{:S(2)}) collective-permute-start(bf16[256,1024]{1,0:T(8,128)(2,1)S(1)} %broadcast_select_fusion), channel_id=1, source_target_pairs={{0,8},{4,20},{8,0},{12,28},{16,24},{20,4},{24,16},{28,12},{1,9},{5... | collective-permute-start | bytes 1572872 | tf_op jit(solution)/shard_map/ppermute | solution.py:20
  69.2 16.7 %collective-permute-start.20 = (bf16[512,1024]{1,0:T(8,128)(2,1)S(1)}, bf16[512,1024]{1,0:T(8,128)(2,1)S(1)}, u32[]{:S(2)}, u32[]{:S(2)}) collective-permute-start(bf16[512,1024]{1,0:T(8,128)(2,1)S(1)} %collective-permute-done.12.refs_0_), channel_id=1, source_target_pairs={{0,4},{4,0},{8,12},{12,8},{16,20},{20,16},{24,28},{28,24},{1,5},{5... | collective-permute-start | bytes 3145736 | tf_op jit(solution)/shard_map/ppermute | solution.py:20
  69.3 16.7 %collective-permute-start.21 = (bf16[512,1024]{1,0:T(8,128)(2,1)S(1)}, bf16[512,1024]{1,0:T(8,128)(2,1)S(1)}, u32[]{:S(2)}, u32[]{:S(2)}) collective-permute-start(bf16[512,1024]{1,0:T(8,128)(2,1)S(1)} %pad_maximum_fusion.2.refs_2_), channel_id=1, source_target_pairs={{0,4},{4,0},{8,12},{12,8},{16,20},{20,16},{24,28},{28,24},{1,5},{5... | collective-permute-start | bytes 3145736 | tf_op jit(solution)/shard_map/ppermute | solution.py:20
  69.8 15.8 %collective-permute-start.9 = (bf16[256,1024]{1,0:T(8,128)(2,1)S(1)}, bf16[256,1024]{1,0:T(8,128)(2,1)S(1)}, u32[]{:S(2)}, u32[]{:S(2)}) collective-permute-start(bf16[256,1024]{1,0:T(8,128)(2,1)S(1)} %collective-permute-done.8), channel_id=1, source_target_pairs={{1,0},{2,3},{5,4},{6,7},{9,8},{10,11},{13,12},{14,15},{17,16},{18,... | collective-permute-start | bytes 1572872 | tf_op jit(solution)/shard_map/ppermute | solution.py:146
  71.1 1.6 %copy-start.2 = (bf16[1024,1024]{1,0:T(8,128)(2,1)S(1)}, bf16[1024,1024]{1,0:T(8,128)(2,1)}, u32[]{:S(2)}) copy-start(bf16[1024,1024]{1,0:T(8,128)(2,1)} %get-tuple-element.114.normed) | copy-start | bytes 6291460
  72.6 13.4 %copy-start = (bf16[1024,2048]{1,0:T(8,128)(2,1)S(1)}, bf16[1024,2048]{1,0:T(8,128)(2,1)}, u32[]{:S(2)}) copy-start(bf16[1024,2048]{1,0:T(8,128)(2,1)} %get-tuple-element.121.normed) | copy-start | bytes 12582916
  75.6 19.6 %collective-permute-start.19 = (bf16[512,1024]{1,0:T(8,128)(2,1)S(1)}, bf16[512,1024]{1,0:T(8,128)(2,1)S(1)}, u32[]{:S(2)}, u32[]{:S(2)}) collective-permute-start(bf16[512,1024]{1,0:T(8,128)(2,1)S(1)} %pad_maximum_fusion.3.refs_0_), channel_id=1, source_target_pairs={{0,16},{4,12},{8,24},{12,4},{16,0},{20,28},{24,8},{28,20},{1,17},{... | collective-permute-start | bytes 3145736 | tf_op jit(solution)/shard_map/ppermute | solution.py:20
  85.6 9.6 %collective-permute-start.16 = (bf16[256,1024]{1,0:T(8,128)(2,1)S(1)}, bf16[256,1024]{1,0:T(8,128)(2,1)S(1)}, u32[]{:S(2)}, u32[]{:S(2)}) collective-permute-start(bf16[256,1024]{1,0:T(8,128)(2,1)S(1)} %broadcast_select_fusion.1), channel_id=1, source_target_pairs={{0,8},{4,20},{8,0},{12,28},{16,24},{20,4},{24,16},{28,12},{1,9},{5... | collective-permute-start | bytes 1572872 | tf_op jit(solution)/shard_map/ppermute | solution.py:20
  85.9 24.1 %collective-permute-start.14 = (bf16[512,1024]{1,0:T(8,128)(2,1)S(1)}, bf16[512,1024]{1,0:T(8,128)(2,1)S(1)}, u32[]{:S(2)}, u32[]{:S(2)}) collective-permute-start(bf16[512,1024]{1,0:T(8,128)(2,1)S(1)} %collective-permute-done.12.refs_0_), channel_id=1, source_target_pairs={{0,1},{1,0},{2,3},{3,2},{4,5},{5,4},{6,7},{7,6},{8,9},{9,8},{10,11... | collective-permute-start | bytes 3145736 | tf_op jit(solution)/shard_map/ppermute | solution.py:138
  85.9 24.1 %collective-permute-start.23 = (bf16[512,1024]{1,0:T(8,128)(2,1)S(1)}, bf16[512,1024]{1,0:T(8,128)(2,1)S(1)}, u32[]{:S(2)}, u32[]{:S(2)}) collective-permute-start(bf16[512,1024]{1,0:T(8,128)(2,1)S(1)} %pad_maximum_fusion.3.refs_0_), channel_id=1, source_target_pairs={{0,4},{4,0},{8,12},{12,8},{16,20},{20,16},{24,28},{28,24},{1,5},{5... | collective-permute-start | bytes 3145736 | tf_op jit(solution)/shard_map/ppermute | solution.py:20
  86.0 24.6 %copy-start.1 = (bf16[1024,2048]{1,0:T(8,128)(2,1)S(1)}, bf16[1024,2048]{1,0:T(8,128)(2,1)}, u32[]{:S(2)}) copy-start(bf16[1024,2048]{1,0:T(8,128)(2,1)} %get-tuple-element.129.normed) | copy-start | bytes 12582916
  95.2 14.8 %collective-permute-start.24 = (bf16[512,1024]{1,0:T(8,128)(2,1)S(1)}, bf16[512,1024]{1,0:T(8,128)(2,1)S(1)}, u32[]{:S(2)}, u32[]{:S(2)}) collective-permute-start(bf16[512,1024]{1,0:T(8,128)(2,1)S(1)} %collective-permute-done.19.refs_2_), channel_id=1, source_target_pairs={{0,4},{4,0},{8,12},{12,8},{16,20},{20,16},{24,28},{28,24},{1,5},{5... | collective-permute-start | bytes 3145736 | tf_op jit(solution)/shard_map/ppermute | solution.py:20
  96.3 19.3 %collective-permute-start.22 = (bf16[512,1024]{1,0:T(8,128)(2,1)S(1)}, bf16[512,1024]{1,0:T(8,128)(2,1)S(1)}, u32[]{:S(2)}, u32[]{:S(2)}) collective-permute-start(bf16[512,1024]{1,0:T(8,128)(2,1)S(1)} %constant_dynamic-update-slice_fusion.refs_0_), channel_id=1, source_target_pairs={{0,16},{4,12},{8,24},{12,4},{16,0},{20,28},{24,8},{28,20},{1,17},{... | collective-permute-start | bytes 3145736 | tf_op jit(solution)/shard_map/ppermute | solution.py:20
  110.1 8.6 %collective-permute-start.15 = (bf16[512,1024]{1,0:T(8,128)(2,1)S(1)}, bf16[512,1024]{1,0:T(8,128)(2,1)S(1)}, u32[]{:S(2)}, u32[]{:S(2)}) collective-permute-start(bf16[512,1024]{1,0:T(8,128)(2,1)S(1)} %collective-permute-done.14.refs_0_), channel_id=1, source_target_pairs={{0,4},{4,0},{8,12},{12,8},{16,20},{20,16},{24,28},{28,24},{1,5},{5... | collective-permute-start | bytes 3145736 | tf_op jit(solution)/shard_map/ppermute | solution.py:20
  110.1 5.7 %collective-permute-start.26 = (bf16[512,1024]{1,0:T(8,128)(2,1)S(1)}, bf16[512,1024]{1,0:T(8,128)(2,1)S(1)}, u32[]{:S(2)}, u32[]{:S(2)}) collective-permute-start(bf16[512,1024]{1,0:T(8,128)(2,1)S(1)} %constant_dynamic-update-slice_fusion.refs_0_), channel_id=1, source_target_pairs={{0,4},{4,0},{8,12},{12,8},{16,20},{20,16},{24,28},{28,24},{1,5},{5... | collective-permute-start | bytes 3145736 | tf_op jit(solution)/shard_map/ppermute | solution.py:20
  110.6 5.2 %copy-start.3 = (bf16[1024,1024]{1,0:T(8,128)(2,1)S(1)}, bf16[1024,1024]{1,0:T(8,128)(2,1)}, u32[]{:S(2)}) copy-start(bf16[1024,1024]{1,0:T(8,128)(2,1)} %get-tuple-element.138.normed) | copy-start | bytes 6291460
  115.6 3.0 %collective-permute-start.25 = (bf16[512,1024]{1,0:T(8,128)(2,1)S(1)}, bf16[512,1024]{1,0:T(8,128)(2,1)S(1)}, u32[]{:S(2)}, u32[]{:S(2)}) collective-permute-start(bf16[512,1024]{1,0:T(8,128)(2,1)S(1)} %collective-permute-done.22.refs_2_), channel_id=1, source_target_pairs={{0,4},{4,0},{8,12},{12,8},{16,20},{20,16},{24,28},{28,24},{1,5},{5... | collective-permute-start | bytes 3145736 | tf_op jit(solution)/shard_map/ppermute | solution.py:20
  115.8 2.9 %copy-start.4 = (bf16[1024,2048]{1,0:T(8,128)(2,1)S(1)}, bf16[1024,2048]{1,0:T(8,128)(2,1)}, u32[]{:S(2)}) copy-start(bf16[1024,2048]{1,0:T(8,128)(2,1)} %get-tuple-element.107.normed) | copy-start | bytes 12582916

commit v4 on v3

--- a/solution.py
+++ b/solution.py
@@ -160,15 +160,15 @@
     other_reps = [rep ^ second_bit, rep ^ 6, sibling ^ first_bit, sibling ^ 6]
     sequence = [
         [(0, half_reps)],
-        [(0, other_reps), (1, half_reps)],
-        [(2, half_reps), (2, other_reps)],
+        [(0, other_reps), (1, half_reps), (1, other_reps[0::2])],
+        [(2, half_reps), (2, other_reps), (1, other_reps[1::2])],
         [(3, half_reps)],
-        [(1, other_reps), (3, other_reps)],
+        [(3, other_reps)],
     ]
     order = jnp.stack([
         block_place[at] * 8 + r for group in sequence for at, reps in group for r in reps
     ]).astype(jnp.int32)
-    parts = [4 * rows * len(group) for group in sequence]
+    parts = [rows * sum(len(reps) for _, reps in group) for group in sequence]
 
     link = deltas.dtype
     half_rows = rows // 2
@@ -234,17 +234,18 @@
     half0 = [half0, swap_cores(half0)]
     far_in, near_out = inwards(pair), outwards(near_in)
     beside = swap_first(pair)
+    third1 = swap_second(pair)
 
     order, pair = together(order, pair)
     normed = normalize_in_order(tokens, norm_gain, order, rows, parts, 4, 4, normed)
-    beside, other0, near_out, normed[-1] = together(beside, other0, near_out, normed[-1])
+    beside, near_out, normed[-1] = together(beside, near_out, normed[-1])
     near = jnp.where(outer, near_out, near_in)
     half1 = jnp.concatenate([pair, beside], 0)
     beside = swap_first(near)
     far_out = outwards(far_in)
     half1, half0 = together(half1, half0)
     total = project(normed[0], half0, normed[-1])
-    ready = [other0, swap_cores(other0), half1, swap_cores(half1)]
+    ready = [other0, swap_cores(other0), half1, swap_cores(half1), third1, swap_cores(third1)]
 
     beside, total = together(beside, total)
     half2 = jnp.concatenate([near, beside], 0)
@@ -252,20 +253,20 @@
     far = jnp.where(outer, far_out, far_in)
     far, pair_source = together(far, other0)
     beside = swap_first(far)
-    other1 = to_pair(pair_source)
+    fourth1 = to_pair(pair_source[rows:])
     half2, ready = together(half2, ready)
     total = project(normed[1], ready, total)
 
     beside, other2, total = together(beside, other2, total)
     half3 = jnp.concatenate([far, beside], 0)
     other3 = swap_second(half3)
-    ready = [half2, swap_cores(half2), other2, swap_cores(other2)]
+    ready = [half2, swap_cores(half2), other2, swap_cores(other2), fourth1, swap_cores(fourth1)]
     half3, ready = together(half3, ready)
     total = project(normed[2], ready, total)
     half3 = [half3, swap_cores(half3)]
     other3, total = together(other3, total)
     total = project(normed[3], half3, total)
-    last = [other1, swap_cores(other1), other3, swap_cores(other3)]
+    last = [other3, swap_cores(other3)]
     total = project(normed[4], last, total, True)
     return total, master_new, momentum_new
 

time: 125 us -> 122 us (0.976)
  the two profiles are of different devices: /device:TPU:0 before, /device:TPU:9 now
where the time goes in v4:
time: 122 us; the launch traced here: 121 us
  starting transfers between devices  45.4 us (37%)
  Pallas kernels  40.7 us (33%)
  waiting for transfers between devices  20 us (16%)
  other arithmetic  9.54 us (8%)
  local copies, waits for them, and re-layouts  4.28 us (4%)
    ppermute x23, starting transfers between devices, flip(): return lax.ppermute(value, 'rep', perm)  30.5 us
    pallas_call x5, Pallas kernels, project(): pl.pallas_call(functools.partial(project_kernel, depths), grid=(rows // t...  21.8 us
    pallas_call x3, Pallas kernels, normalize_in_order(): pl.pallas_call(functools.partial(normalize_kernel, width=width, parts=len...  18.9 us
    ppermute x23, waiting for transfers between devices, flip(): return lax.ppermute(value, 'rep', perm)  17.6 us
    ppermute x2, starting transfers between devices, inwards(): return lax.ppermute(value, 'fsdp', [(1, 2), (2, 1)])  8.64 us
    ppermute x2, starting transfers between devices, outwards(): return lax.ppermute(value, 'fsdp', [(1, 0), (2, 3)])  3.85 us
    another operation x2, other arithmetic  2.72 us
    reshape x2, local copies, waits for them, and re-layouts, on_block(): theirs = theirs.reshape(4, half_rows, cols)  2.6 us
  transfers between devices with their start and end apart: 29, of which 9 were waited for; matrix products, arithmetic and copies ran while one was open for 8% of the time, Pallas kernels for 30%

profile of v4, /device:TPU:9, one launch (start us, length us, event | category | flops | bytes accessed | tf_op | source)
XLA Modules:
  0.0 121.1 jit_solution(17234105862633581851)
XLA Ops:
  0.7 1.3 %dynamic-slice_bitcast_fusion.1 = bf16[4,128,1024]{2,1,0:T(8,128)(2,1)S(1)} fusion(bf16[4,2,2,128,1024]{4,3,2,1,0:T(8,128)(2,1)} %bitcast.127, s32[]{:T(128)S(6)} %select_n.62), kind=kLoop, calls=%fused_computation.7 | loop fusion | bytes 2097156 | tf_op jit(solution)/shard_map/reshape | solution.py:197
  2.0 0.7 collective-permute-start
  2.7 1.3 %dynamic-slice_bitcast_fusion = bf16[4,128,1024]{2,1,0:T(8,128)(2,1)S(1)} fusion(bf16[4,2,2,128,1024]{4,3,2,1,0:T(8,128)(2,1)} %bitcast.128, s32[]{:T(128)S(6)} %select_n.63), kind=kLoop, calls=%fused_computation.6 | loop fusion | bytes 2097156 | tf_op jit(solution)/shard_map/reshape | solution.py:197
  4.7 0.4 collective-permute-done
  5.0 1.3 %fusion.11 = (bf16[128,1024]{1,0:T(8,128)(2,1)S(1)}, bf16[128,1024]{1,0:T(8,128)(2,1)S(1)}) fusion(bf16[4,128,1024]{2,1,0:T(8,128)(2,1)S(1)} %collective-permute-done, s32[]{:T(128)S(6)} %select_n.130, f32[128]{0:T(128)S(1)} %get-tuple-element.184, bf16[4,2,2,128,1024]{4,3,2,1,0:T(8,128)(2,1)} %bitcast.129, s32[]{:T(128)S(6)} %select_n.131, ...), kind=kLoop, calls=%fused_computation.36 | loop fusion | flops 1572864 | bytes 1574924 | tf_op jit(solution)/shard_map/convert.18
  6.3 1.3 %collective-permute-start.2 = (bf16[256,1024]{1,0:T(8,128)(2,1)S(1)}, bf16[256,1024]{1,0:T(8,128)(2,1)S(1)}, u32[]{:S(2)}, u32[]{:S(2)}) collective-permute-start(bf16[256,1024]{1,0:T(8,128)(2,1)S(1)} %pad_maximum_fusion.4), channel_id=1, source_target_pairs={{0,8},{4,20},{8,0},{12,28},{16,24},{20,4},{24,16},{28,12},{1,9},{5... | collective-permute-start | bytes 1572872 | tf_op jit(solution)/shard_map/ppermute | solution.py:20
  7.7 1.4 %fusion.7 = (bf16[128,1024]{1,0:T(8,128)(2,1)S(1)}, bf16[128,1024]{1,0:T(8,128)(2,1)S(1)}) fusion(bf16[4,128,1024]{2,1,0:T(8,128)(2,1)} %collective-permute-done.1, s32[]{:T(128)S(6)} %select_n.130, f32[128]{0:T(128)S(1)} %get-tuple-element.186, bf16[4,2,2,128,1024]{4,3,2,1,0:T(8,128)(2,1)} %bitcast.130, s32[]{:T(128)S(6)} %select_n.131, ...), kind=kLoop, calls=%fused_computation.28 | loop fusion | flops 1572864 | bytes 1574924 | tf_op jit(solution)/shard_map/convert.16
  9.1 0.5 collective-permute-start.3
  9.7 5.1 %normalize_in_order.3 = (bf16[1024,1024]{1,0:T(8,128)(2,1)}, bf16[1024,2560]{1,0:T(8,128)(2,1)}, bf16[1024,2560]{1,0:T(8,128)(2,1)}, bf16[1024,1024]{1,0:T(8,128...) custom-call(s32[32]{0:T(128)S(1)} %stack.131.order, bf16[1024,8192]{1,0:T(8,128)(2,1)} %tokens.5, ...), custom_call_target="tpu_custom_call" | custom-call | flops 12582912 | bytes 8388608 | tf_op jit(solution)/shard_map/normalize_in_order/pallas_call | solution.py:68
  14.7 1.8 %fusion = (f32[128,1024]{1,0:T(8,128)S(1)}, f32[128,1024]{1,0:T(8,128)S(1)}, f32[128,1024]{1,0:T(8,128)S(1)}, f32[128,1024]{1,0:T(8,128)S(1)}) fusion(bf16[4,128,1024]{2,1,0:T(8,128)(2,1)} %collective-permute-done.1, s32[]{:T(128)S(6)} %select_n.138, f32[128]{0:T(128)S(1)} %get-tuple-element.191, bf16[4,2,2,128,1024]{4,3,2,1,0:T(8,128)(2,1)} %bitcast.131, ...), kind=kLoop, calls=%fused_computation.11 | loop fusion | flops 2621440 | bytes 4198412 | tf_op jit(solution)/shard_map/add | solution.py:188
  16.7 1.3 %collective-permute-start.4 = (bf16[128,1024]{1,0:T(8,128)(2,1)S(1)}, bf16[128,1024]{1,0:T(8,128)(2,1)S(1)}, u32[]{:S(2)}, u32[]{:S(2)}) collective-permute-start(bf16[128,1024]{1,0:T(8,128)(2,1)S(1)} %get-tuple-element.165), channel_id=1, source_target_pairs={{0,16},{4,12},{8,24},{12,4},{16,0},{20,28},{24,8},{28,20},{1,17},{... | collective-permute-start | bytes 786440 | tf_op jit(solution)/shard_map/ppermute | solution.py:20
  17.9 2.4 %collective-permute-done.3 = bf16[256,1024]{1,0:T(8,128)(2,1)S(1)} collective-permute-done((bf16[256,1024]{1,0:T(8,128)(2,1)S(1)}, bf16[256,1024]{1,0:T(8,128)(2,1)S(1)}, u32[]{:S(2)}, u32[]{:S(2)}) %collective-permute-start.3) | collective-permute-done | bytes 524320 | tf_op jit(solution)/shard_map/ppermute | solution.py:20
  20.5 1.3 %collective-permute-start.5 = (bf16[128,1024]{1,0:T(8,128)(2,1)S(1)}, bf16[128,1024]{1,0:T(8,128)(2,1)S(1)}, u32[]{:S(2)}, u32[]{:S(2)}) collective-permute-start(bf16[128,1024]{1,0:T(8,128)(2,1)S(1)} %get-tuple-element.163), channel_id=1, source_target_pairs={{0,16},{4,12},{8,24},{12,4},{16,0},{20,28},{24,8},{28,20},{1,17},{... | collective-permute-start | bytes 786440 | tf_op jit(solution)/shard_map/ppermute | solution.py:20
  21.8 5.1 %normalize_in_order.4 = (bf16[1024,1024]{1,0:T(8,128)(2,1)}, bf16[1024,2560]{1,0:T(8,128)(2,1)}, bf16[1024,2560]{1,0:T(8,128)(2,1)}, bf16[1024,1024]{1,0:T(8,128...) custom-call(s32[32]{0:T(128)S(1)} %stack.131.order, ...), custom_call_target="tpu_custom_call", output_to_operand_aliasing={{0}: (3, {}), {1}: (4, {}), {2}: (5, {}), {3}: (6, {}), {4}... | custom-call | flops 12582912 | bytes 8388608 | tf_op jit(solution)/shard_map/normalize_in_order/pallas_call | solution.py:68
  27.0 1.0 copy-done.3
  28.4 1.7 %fusion.30 = (bf16[256,1024]{1,0:T(8,128)(2,1)S(1)}, f32[256,1024]{1,0:T(8,128)}, f32[256,1024]{1,0:T(8,128)}) fusion(f32[256,1024]{1,0:T(8,128)S(1)} %copy-done.3, f32[128,1024]{1,0:T(8,128)S(1)} %convert_add_fusion, f32[128,1024]{1,0:T(8,128)S(1)} %convert_add_fusion.1, f32[256,1024]{1,0:T(8,128)S(1)} %copy-done.4), kind=kLoop, calls=%fused_computation.89 | loop fusion | flops 2097152 | bytes 5767168 | tf_op jit(solution)/shard_map/convert_element_type | solution.py:226
  30.1 1.2 %collective-permute-start.10 = (bf16[256,1024]{1,0:T(8,128)(2,1)S(1)}, bf16[256,1024]{1,0:T(8,128)(2,1)S(1)}, u32[]{:S(2)}, u32[]{:S(2)}) collective-permute-start(bf16[256,1024]{1,0:T(8,128)(2,1)S(1)} %get-tuple-element.149), channel_id=1, source_target_pairs={{0,8},{4,20},{8,0},{12,28},{16,24},{20,4},{24,16},{28,12},{1,9},{5... | collective-permute-start | bytes 1572872 | tf_op jit(solution)/shard_map/ppermute | solution.py:20
  31.5 4.3 %collective-permute-start.7 = (bf16[256,1024]{1,0:T(8,128)(2,1)S(1)}, bf16[256,1024]{1,0:T(8,128)(2,1)}, u32[]{:S(2)}, u32[]{:S(2)}) collective-permute-start(bf16[256,1024]{1,0:T(8,128)(2,1)S(1)} %get-tuple-element.149), channel_id=1, source_target_pairs={{1,2},{2,1},{5,6},{6,5},{9,10},{10,9},{13,14},{14,13},{17,18},{18,... | collective-permute-start | bytes 1572872 | tf_op jit(solution)/shard_map/ppermute | solution.py:142
  35.8 2.7 %collective-permute-done.10 = bf16[256,1024]{1,0:T(8,128)(2,1)S(1)} collective-permute-done((bf16[256,1024]{1,0:T(8,128)(2,1)S(1)}, bf16[256,1024]{1,0:T(8,128)(2,1)S(1)}, u32[]{:S(2)}, u32[]{:S(2)}) %collective-permute-start.10) | collective-permute-done | bytes 524320 | tf_op jit(solution)/shard_map/ppermute | solution.py:20
  38.6 4.3 %collective-permute-start.16 = (bf16[512,1024]{1,0:T(8,128)(2,1)S(1)}, bf16[512,1024]{1,0:T(8,128)(2,1)S(1)}, u32[]{:S(2)}, u32[]{:S(2)}) collective-permute-start(bf16[512,1024]{1,0:T(8,128)(2,1)S(1)} %pad_maximum_fusion.1.refs_0_), channel_id=1, source_target_pairs={{0,4},{4,0},{8,12},{12,8},{16,20},{20,16},{24,28},{28,24},{1,5},{5... | collective-permute-start | bytes 3145736 | tf_op jit(solution)/shard_map/ppermute | solution.py:20
  42.9 1.2 collective-permute-start.11
  44.1 0.5 collective-permute-start.13
  44.6 2.4 %collective-permute-start.14 = (bf16[256,1024]{1,0:T(8,128)(2,1)}, bf16[256,1024]{1,0:T(8,128)(2,1)}, u32[]{:S(2)}, u32[]{:S(2)}) collective-permute-start(bf16[256,1024]{1,0:T(8,128)(2,1)} %collective-permute-done.7), channel_id=1, source_target_pairs={{1,0},{2,3},{5,4},{6,7},{9,8},{10,11},{13,12},{14,15},{17,16},{18,... | collective-permute-start | bytes 1572872 | tf_op jit(solution)/shard_map/ppermute | solution.py:146
  47.0 4.3 %collective-permute-start.8 = (bf16[256,1024]{1,0:T(8,128)(2,1)}, bf16[256,1024]{1,0:T(8,128)(2,1)S(1)}, u32[]{:S(2)}, u32[]{:S(2)}) collective-permute-start(bf16[256,1024]{1,0:T(8,128)(2,1)} %collective-permute-done.6), channel_id=1, source_target_pairs={{1,2},{2,1},{5,6},{6,5},{9,10},{10,9},{13,14},{14,13},{17,18},{18,... | collective-permute-start | bytes 1572872 | tf_op jit(solution)/shard_map/ppermute | solution.py:142
  51.3 8.8 %normalize_in_order.5 = (bf16[1024,1024]{1,0:T(8,128)(2,1)}, bf16[1024,2560]{1,0:T(8,128)(2,1)}, bf16[1024,2560]{1,0:T(8,128)(2,1)}, bf16[1024,1024]{1,0:T(8,128...) custom-call(s32[32]{0:T(128)S(1)} %stack.131.order, ...), custom_call_target="tpu_custom_call", output_to_operand_aliasing={{0}: (3, {}), {1}: (4, {}), {2}: (5, {}), {3}: (6, {}), {4}... | custom-call | flops 25165824 | bytes 16777216 | tf_op jit(solution)/shard_map/normalize_in_order/pallas_call | solution.py:68
  60.1 1.3 %broadcast_select_fusion = bf16[256,1024]{1,0:T(8,128)(2,1)S(1)} fusion(bf16[256,1024]{1,0:T(8,128)(2,1)} %collective-permute-done.14, bf16[256,1024]{1,0:T(8,128)(2,1)} %collective-permute-done.7, pred[]{:T(512)S(6)} %or.3), kind=kLoop, calls=%fused_computation.44 | loop fusion | flops 262144 | bytes 1572865 | tf_op jit(solution)/shard_map/jit(_where)/select_n | solution.py:242
  61.4 1.5 %collective-permute-start.15 = (bf16[256,1024]{1,0:T(8,128)(2,1)S(1)}, bf16[256,1024]{1,0:T(8,128)(2,1)S(1)}, u32[]{:S(2)}, u32[]{:S(2)}) collective-permute-start(bf16[256,1024]{1,0:T(8,128)(2,1)S(1)} %broadcast_select_fusion), channel_id=1, source_target_pairs={{0,8},{4,20},{8,0},{12,28},{16,24},{20,4},{24,16},{28,12},{1,9},{5... | collective-permute-start | bytes 1572872 | tf_op jit(solution)/shard_map/ppermute | solution.py:20
  63.1 1.3 %pad_maximum_fusion.2.refs_2_ = bf16[512,1024]{1,0:T(8,128)(2,1)S(1)} fusion(bf16[256,1024]{1,0:T(8,128)(2,1)} %collective-permute-done.13, bf16[256,1024]{1,0:T(8,128)(2,1)} %collective-permute-done.6), kind=kLoop, calls=%fused_computation.2 | loop fusion | flops 2097152 | bytes 2097152 | tf_op jit(solution)/shard_map/concatenate | solution.py:243
  64.4 4.1 %collective-permute-start.19 = (bf16[512,1024]{1,0:T(8,128)(2,1)S(1)}, bf16[512,1024]{1,0:T(8,128)(2,1)S(1)}, u32[]{:S(2)}, u32[]{:S(2)}) collective-permute-start(bf16[512,1024]{1,0:T(8,128)(2,1)S(1)} %pad_maximum_fusion.2.refs_2_), channel_id=1, source_target_pairs={{0,4},{4,0},{8,12},{12,8},{16,20},{20,16},{24,28},{28,24},{1,5},{5... | collective-permute-start | bytes 3145736 | tf_op jit(solution)/shard_map/ppermute | solution.py:20
  68.6 1.5 %collective-permute-start.9 = (bf16[256,1024]{1,0:T(8,128)(2,1)S(1)}, bf16[256,1024]{1,0:T(8,128)(2,1)S(1)}, u32[]{:S(2)}, u32[]{:S(2)}) collective-permute-start(bf16[256,1024]{1,0:T(8,128)(2,1)S(1)} %collective-permute-done.8), channel_id=1, source_target_pairs={{1,0},{2,3},{5,4},{6,7},{9,8},{10,11},{13,12},{14,15},{17,16},{18,... | collective-permute-start | bytes 1572872 | tf_op jit(solution)/shard_map/ppermute | solution.py:146
  70.1 2.9 %project.5.refs_6_ = f32[1024,1024]{1,0:T(8,128)S(1)} custom-call(bf16[1024,1024]{1,0:T(8,128)(2,1)S(1)} %copy-done.1, bf16[512,1024]{1,0:T(8,128)(2,1)S(1)} %pad_maximum_fusion.1.refs_0_, bf16[512,1024]{1,0:T(8,128)(2,1)S(1)} %collective-permute-done.16.refs_1_, f32[8,128]{1,0:T(8,128)S(1)} %get-tuple-element.120.refs_2_), custom_call_target="tpu_custom_call" | custom-call | flops 2147483648 | bytes 12582912 | tf_op jit(solution)/shard_map/project/pallas_call | solution.py:115
  73.1 0.3 collective-permute-start.17
  73.5 0.9 collective-permute-done.20.refs_4_
  74.4 4.3 %collective-permute-start.21 = (bf16[256,1024]{1,0:T(8,128)(2,1)S(1)}, bf16[256,1024]{1,0:T(8,128)(2,1)S(1)}, u32[]{:S(2)}, u32[]{:S(2)}) collective-permute-start(bf16[256,1024]{1,0:T(8,128)(2,1)S(1)} %collective-permute-done.20.refs_4_), channel_id=1, source_target_pairs={{0,4},{4,0},{8,12},{12,8},{16,20},{20,16},{24,28},{28,24},{1,5},{5... | collective-permute-start | bytes 1572872 | tf_op jit(solution)/shard_map/ppermute | solution.py:20
  78.7 2.4 %collective-permute-done.9 = bf16[256,1024]{1,0:T(8,128)(2,1)S(1)} collective-permute-done((bf16[256,1024]{1,0:T(8,128)(2,1)S(1)}, bf16[256,1024]{1,0:T(8,128)(2,1)S(1)}, u32[]{:S(2)}, u32[]{:S(2)}) %collective-permute-start.9) | collective-permute-done | bytes 524320 | tf_op jit(solution)/shard_map/ppermute | solution.py:146
  81.1 1.3 %collective-permute-start.12 = (bf16[256,1024]{1,0:T(8,128)(2,1)S(1)}, bf16[256,1024]{1,0:T(8,128)(2,1)S(1)}, u32[]{:S(2)}, u32[]{:S(2)}) collective-permute-start(bf16[256,1024]{1,0:T(8,128)(2,1)S(1)} %broadcast_select_fusion.1), channel_id=1, source_target_pairs={{0,8},{4,20},{8,0},{12,28},{16,24},{20,4},{24,16},{28,12},{1,9},{5... | collective-permute-start | bytes 1572872 | tf_op jit(solution)/shard_map/ppermute | solution.py:20
  82.5 2.3 %collective-permute-start.25 = (bf16[256,1024]{1,0:T(8,128)(2,1)S(1)}, bf16[256,1024]{1,0:T(8,128)(2,1)S(1)}, u32[]{:S(2)}, u32[]{:S(2)}) collective-permute-start(bf16[256,1024]{1,0:T(8,128)(2,1)S(1)} %slice.19), channel_id=1, source_target_pairs={{0,1},{1,0},{2,3},{3,2},{4,5},{5,4},{6,7},{7,6},{8,9},{9,8},{10,11... | collective-permute-start | bytes 1572872 | tf_op jit(solution)/shard_map/ppermute | solution.py:138
  84.8 6.1 %project.6.refs_6_ = f32[1024,1024]{1,0:T(8,128)S(1)} custom-call(bf16[1024,2560]{1,0:T(8,128)(2,1)S(1)} %bitcast.124, bf16[512,1024]{1,0:T(8,128)(2,1)S(1)} %collective-permute-done.11.refs_0_, bf16[512,1024]{1,0:T(8,128)(2,1)S(1)} %collective-permute-done.18.refs_1_, bf16[512,1024]{1,0:T(8,128)(2,1)S(1)} %pad_maximum_fusion.2.refs_2_, ...), custom_call_target="tpu_custom_call" | custom-call | flops 5368709120 | bytes 18874368 | tf_op jit(solution)/shard_map/project/pallas_call | solution.py:115
  90.9 4.3 %collective-permute-done.12 = bf16[256,1024]{1,0:T(8,128)(2,1)S(1)} collective-permute-done((bf16[256,1024]{1,0:T(8,128)(2,1)S(1)}, bf16[256,1024]{1,0:T(8,128)(2,1)S(1)}, u32[]{:S(2)}, u32[]{:S(2)}) %collective-permute-start.12) | collective-permute-done | bytes 524320 | tf_op jit(solution)/shard_map/ppermute | solution.py:20
  95.2 3.8 %collective-permute-start.24 = (bf16[512,1024]{1,0:T(8,128)(2,1)S(1)}, bf16[512,1024]{1,0:T(8,128)(2,1)S(1)}, u32[]{:S(2)}, u32[]{:S(2)}) collective-permute-start(bf16[512,1024]{1,0:T(8,128)(2,1)S(1)} %collective-permute-done.17.refs_2_), channel_id=1, source_target_pairs={{0,4},{4,0},{8,12},{12,8},{16,20},{20,16},{24,28},{28,24},{1,5},{5... | collective-permute-start | bytes 3145736 | tf_op jit(solution)/shard_map/ppermute | solution.py:20
  99.1 0.3 collective-permute-start.22
  99.8 3.8 %collective-permute-done.26.refs_5_ = bf16[256,1024]{1,0:T(8,128)(2,1)S(1)} collective-permute-done((bf16[256,1024]{1,0:T(8,128)(2,1)S(1)}, bf16[256,1024]{1,0:T(8,128)(2,1)S(1)}, u32[]{:S(2)}, u32[]{:S(2)}) %collective-permute-start.26) | collective-permute-done | bytes 524320 | tf_op jit(solution)/shard_map/ppermute | solution.py:20
  103.6 0.4 collective-permute-start.28
  103.9 6.1 %project.7.refs_2_ = f32[1024,1024]{1,0:T(8,128)S(1)} custom-call(bf16[1024,2560]{1,0:T(8,128)(2,1)S(1)} %bitcast.126, bf16[512,1024]{1,0:T(8,128)(2,1)S(1)} %pad_maximum_fusion.3.refs_0_, bf16[512,1024]{1,0:T(8,128)(2,1)S(1)} %collective-permute-done.23.refs_1_, bf16[512,1024]{1,0:T(8,128)(2,1)S(1)} %collective-permute-done.17.refs_2_, ...), custom_call_target="tpu_custom_call" | custom-call | flops 5368709120 | bytes 18874368 | tf_op jit(solution)/shard_map/project/pallas_call | solution.py:115
  110.1 3.1 %collective-permute-done.22.refs_0_ = bf16[512,1024]{1,0:T(8,128)(2,1)S(1)} collective-permute-done((bf16[512,1024]{1,0:T(8,128)(2,1)S(1)}, bf16[512,1024]{1,0:T(8,128)(2,1)S(1)}, u32[]{:S(2)}, u32[]{:S(2)}) %collective-permute-start.22) | collective-permute-done | bytes 1048608 | tf_op jit(solution)/shard_map/ppermute | solution.py:20
  113.1 1.4 %collective-permute-start.27 = (bf16[512,1024]{1,0:T(8,128)(2,1)S(1)}, bf16[512,1024]{1,0:T(8,128)(2,1)S(1)}, u32[]{:S(2)}, u32[]{:S(2)}) collective-permute-start(bf16[512,1024]{1,0:T(8,128)(2,1)S(1)} %collective-permute-done.22.refs_0_), channel_id=1, source_target_pairs={{0,4},{4,0},{8,12},{12,8},{16,20},{20,16},{24,28},{28,24},{1,5},{5... | collective-permute-start | bytes 3145736 | tf_op jit(solution)/shard_map/ppermute | solution.py:20
  114.5 2.9 %project.8.refs_2_ = f32[1024,1024]{1,0:T(8,128)S(1)} custom-call(bf16[1024,1024]{1,0:T(8,128)(2,1)S(1)} %copy-done.2, bf16[512,1024]{1,0:T(8,128)(2,1)S(1)} %constant_dynamic-update-slice_fusion.refs_0_, bf16[512,1024]{1,0:T(8,128)(2,1)S(1)} %collective-permute-done.28.refs_1_, f32[1024,1024]{1,0:T(8,128)S(1)} %project.7.refs_2_), custom_call_target="tpu_custom_call" | custom-call | flops 2147483648 | bytes 12582912 | tf_op jit(solution)/shard_map/project/pallas_call | solution.py:115
  117.4 3.8 %project.9 = bf16[1024,1024]{1,0:T(8,128)(2,1)} custom-call(bf16[1024,1024]{1,0:T(8,128)(2,1)S(1)} %copy-done, bf16[512,1024]{1,0:T(8,128)(2,1)S(1)} %collective-permute-done.22.refs_0_, bf16[512,1024]{1,0:T(8,128)(2,1)S(1)} %collective-permute-done.27.refs_1_, f32[1024,1024]{1,0:T(8,128)S(1)} %project.8.refs_2_), custom_call_target="tpu_custom_call" | custom-call | flops 2147483648 | bytes 12582912 | tf_op jit(solution)/shard_map/project/pallas_call | solution.py:115
  (71 shorter events, 2.5 us)
Async XLA Ops:
  0.6 3.6 %copy-start.5 = (bf16[8192]{0:T(1024)(128)(2,1)S(1)}, bf16[8192]{0:T(1024)(128)(2,1)}, u32[]{:S(2)}) copy-start(bf16[8192]{0:T(1024)(128)(2,1)} %param.8) | copy-start | bytes 49156
  0.6 3.8 %copy-start.6 = (s32[8,16]{1,0:T(8,128)S(1)}, s32[8,16]{1,0:T(8,128)}, u32[]{:S(2)}) copy-start(s32[8,16]{1,0:T(8,128)} %param.10) | copy-start | bytes 1540
  0.7 3.8 %copy-start.7 = (s32[2048]{0:T(1024)S(1)}, s32[2048]{0:T(1024)}, u32[]{:S(2)}) copy-start(s32[2048]{0:T(1024)} %param.11) | copy-start | bytes 24580
  2.0 3.0 %collective-permute-start = (bf16[4,128,1024]{2,1,0:T(8,128)(2,1)S(1)}, bf16[4,128,1024]{2,1,0:T(8,128)(2,1)S(1)}, u32[]{:S(2)}, u32[]{:S(2)}) collective-permute-start(bf16[4,128,1024]{2,1,0:T(8,128)(2,1)S(1)} %dynamic-slice_bitcast_fusion.1), channel_id=1, source_target_pairs={{0,4},{4,0},{8,12},{12,8},{16,20},{20,16},{24,28},{28,24},{1,5},{5... | collective-permute-start | bytes 3145736 | tf_op jit(solution)/shard_map/ppermute | solution.py:20
  4.0 3.6 %collective-permute-start.1 = (bf16[4,128,1024]{2,1,0:T(8,128)(2,1)S(1)}, bf16[4,128,1024]{2,1,0:T(8,128)(2,1)}, u32[]{:S(2)}, u32[]{:S(2)}) collective-permute-start(bf16[4,128,1024]{2,1,0:T(8,128)(2,1)S(1)} %dynamic-slice_bitcast_fusion), channel_id=1, source_target_pairs={{0,4},{4,0},{8,12},{12,8},{16,20},{20,16},{24,28},{28,24},{1,5},{5... | collective-permute-start | bytes 3145736 | tf_op jit(solution)/shard_map/ppermute | solution.py:20
  6.3 10.1 %collective-permute-start.2 = (bf16[256,1024]{1,0:T(8,128)(2,1)S(1)}, bf16[256,1024]{1,0:T(8,128)(2,1)S(1)}, u32[]{:S(2)}, u32[]{:S(2)}) collective-permute-start(bf16[256,1024]{1,0:T(8,128)(2,1)S(1)} %pad_maximum_fusion.4), channel_id=1, source_target_pairs={{0,8},{4,20},{8,0},{12,28},{16,24},{20,4},{24,16},{28,12},{1,9},{5... | collective-permute-start | bytes 1572872 | tf_op jit(solution)/shard_map/ppermute | solution.py:20
  9.1 11.2 %collective-permute-start.3 = (bf16[256,1024]{1,0:T(8,128)(2,1)S(1)}, bf16[256,1024]{1,0:T(8,128)(2,1)S(1)}, u32[]{:S(2)}, u32[]{:S(2)}) collective-permute-start(bf16[256,1024]{1,0:T(8,128)(2,1)S(1)} %pad_maximum_fusion.5), channel_id=1, source_target_pairs={{0,8},{4,20},{8,0},{12,28},{16,24},{20,4},{24,16},{28,12},{1,9},{5... | collective-permute-start | bytes 1572872 | tf_op jit(solution)/shard_map/ppermute | solution.py:20
  16.7 10.2 %collective-permute-start.4 = (bf16[128,1024]{1,0:T(8,128)(2,1)S(1)}, bf16[128,1024]{1,0:T(8,128)(2,1)S(1)}, u32[]{:S(2)}, u32[]{:S(2)}) collective-permute-start(bf16[128,1024]{1,0:T(8,128)(2,1)S(1)} %get-tuple-element.165), channel_id=1, source_target_pairs={{0,16},{4,12},{8,24},{12,4},{16,0},{20,28},{24,8},{28,20},{1,17},{... | collective-permute-start | bytes 786440 | tf_op jit(solution)/shard_map/ppermute | solution.py:20
  20.5 6.4 %collective-permute-start.5 = (bf16[128,1024]{1,0:T(8,128)(2,1)S(1)}, bf16[128,1024]{1,0:T(8,128)(2,1)S(1)}, u32[]{:S(2)}, u32[]{:S(2)}) collective-permute-start(bf16[128,1024]{1,0:T(8,128)(2,1)S(1)} %get-tuple-element.163), channel_id=1, source_target_pairs={{0,16},{4,12},{8,24},{12,4},{16,0},{20,28},{24,8},{28,20},{1,17},{... | collective-permute-start | bytes 786440 | tf_op jit(solution)/shard_map/ppermute | solution.py:20
  26.8 1.2 %copy-start.3 = (f32[256,1024]{1,0:T(8,128)S(1)}, f32[256,1024]{1,0:T(8,128)}, u32[]{:S(2)}) copy-start(f32[256,1024]{1,0:T(8,128)} %param.12) | copy-start | bytes 3145732
  26.8 1.5 %copy-start.4 = (f32[256,1024]{1,0:T(8,128)S(1)}, f32[256,1024]{1,0:T(8,128)}, u32[]{:S(2)}) copy-start(f32[256,1024]{1,0:T(8,128)} %param.13) | copy-start | bytes 3145732
  30.1 8.4 %collective-permute-start.10 = (bf16[256,1024]{1,0:T(8,128)(2,1)S(1)}, bf16[256,1024]{1,0:T(8,128)(2,1)S(1)}, u32[]{:S(2)}, u32[]{:S(2)}) collective-permute-start(bf16[256,1024]{1,0:T(8,128)(2,1)S(1)} %get-tuple-element.149), channel_id=1, source_target_pairs={{0,8},{4,20},{8,0},{12,28},{16,24},{20,4},{24,16},{28,12},{1,9},{5... | collective-permute-start | bytes 1572872 | tf_op jit(solution)/shard_map/ppermute | solution.py:20
  31.3 12.8 %collective-permute-start.6 = (bf16[256,1024]{1,0:T(8,128)(2,1)S(1)}, bf16[256,1024]{1,0:T(8,128)(2,1)}, u32[]{:S(2)}, u32[]{:S(2)}) collective-permute-start(bf16[256,1024]{1,0:T(8,128)(2,1)S(1)} %get-tuple-element.149), channel_id=1, source_target_pairs={{0,1},{1,0},{2,3},{3,2},{4,5},{5,4},{6,7},{7,6},{8,9},{9,8},{10,11... | collective-permute-start | bytes 1572872 | tf_op jit(solution)/shard_map/ppermute | solution.py:138
  31.5 12.7 %collective-permute-start.7 = (bf16[256,1024]{1,0:T(8,128)(2,1)S(1)}, bf16[256,1024]{1,0:T(8,128)(2,1)}, u32[]{:S(2)}, u32[]{:S(2)}) collective-permute-start(bf16[256,1024]{1,0:T(8,128)(2,1)S(1)} %get-tuple-element.149), channel_id=1, source_target_pairs={{1,2},{2,1},{5,6},{6,5},{9,10},{10,9},{13,14},{14,13},{17,18},{18,... | collective-permute-start | bytes 1572872 | tf_op jit(solution)/shard_map/ppermute | solution.py:142
  38.6 25.8 %collective-permute-start.16 = (bf16[512,1024]{1,0:T(8,128)(2,1)S(1)}, bf16[512,1024]{1,0:T(8,128)(2,1)S(1)}, u32[]{:S(2)}, u32[]{:S(2)}) collective-permute-start(bf16[512,1024]{1,0:T(8,128)(2,1)S(1)} %pad_maximum_fusion.1.refs_0_), channel_id=1, source_target_pairs={{0,4},{4,0},{8,12},{12,8},{16,20},{20,16},{24,28},{28,24},{1,5},{5... | collective-permute-start | bytes 3145736 | tf_op jit(solution)/shard_map/ppermute | solution.py:20
  42.9 25.6 %collective-permute-start.11 = (bf16[512,1024]{1,0:T(8,128)(2,1)S(1)}, bf16[512,1024]{1,0:T(8,128)(2,1)S(1)}, u32[]{:S(2)}, u32[]{:S(2)}) collective-permute-start(bf16[512,1024]{1,0:T(8,128)(2,1)S(1)} %pad_maximum_fusion.1.refs_0_), channel_id=1, source_target_pairs={{0,16},{4,12},{8,24},{12,4},{16,0},{20,28},{24,8},{28,20},{1,17},{... | collective-permute-start | bytes 3145736 | tf_op jit(solution)/shard_map/ppermute | solution.py:20
  44.1 15.9 %collective-permute-start.13 = (bf16[256,1024]{1,0:T(8,128)(2,1)}, bf16[256,1024]{1,0:T(8,128)(2,1)}, u32[]{:S(2)}, u32[]{:S(2)}) collective-permute-start(bf16[256,1024]{1,0:T(8,128)(2,1)} %collective-permute-done.6), channel_id=1, source_target_pairs={{0,8},{4,20},{8,0},{12,28},{16,24},{20,4},{24,16},{28,12},{1,9},{5... | collective-permute-start | bytes 1572872 | tf_op jit(solution)/shard_map/ppermute | solution.py:20
  44.6 15.5 %collective-permute-start.14 = (bf16[256,1024]{1,0:T(8,128)(2,1)}, bf16[256,1024]{1,0:T(8,128)(2,1)}, u32[]{:S(2)}, u32[]{:S(2)}) collective-permute-start(bf16[256,1024]{1,0:T(8,128)(2,1)} %collective-permute-done.7), channel_id=1, source_target_pairs={{1,0},{2,3},{5,4},{6,7},{9,8},{10,11},{13,12},{14,15},{17,16},{18,... | collective-permute-start | bytes 1572872 | tf_op jit(solution)/shard_map/ppermute | solution.py:146
  47.0 21.6 %collective-permute-start.8 = (bf16[256,1024]{1,0:T(8,128)(2,1)}, bf16[256,1024]{1,0:T(8,128)(2,1)S(1)}, u32[]{:S(2)}, u32[]{:S(2)}) collective-permute-start(bf16[256,1024]{1,0:T(8,128)(2,1)} %collective-permute-done.6), channel_id=1, source_target_pairs={{1,2},{2,1},{5,6},{6,5},{9,10},{10,9},{13,14},{14,13},{17,18},{18,... | collective-permute-start | bytes 1572872 | tf_op jit(solution)/shard_map/ppermute | solution.py:142
  60.1 10.0 %copy-start.1 = (bf16[1024,1024]{1,0:T(8,128)(2,1)S(1)}, bf16[1024,1024]{1,0:T(8,128)(2,1)}, u32[]{:S(2)}) copy-start(bf16[1024,1024]{1,0:T(8,128)(2,1)} %get-tuple-element.115.normed) | copy-start | bytes 6291460
  61.4 11.7 %collective-permute-start.15 = (bf16[256,1024]{1,0:T(8,128)(2,1)S(1)}, bf16[256,1024]{1,0:T(8,128)(2,1)S(1)}, u32[]{:S(2)}, u32[]{:S(2)}) collective-permute-start(bf16[256,1024]{1,0:T(8,128)(2,1)S(1)} %broadcast_select_fusion), channel_id=1, source_target_pairs={{0,8},{4,20},{8,0},{12,28},{16,24},{20,4},{24,16},{28,12},{1,9},{5... | collective-permute-start | bytes 1572872 | tf_op jit(solution)/shard_map/ppermute | solution.py:20
  62.9 11.5 %collective-permute-start.20 = (bf16[256,1024]{1,0:T(8,128)(2,1)}, bf16[256,1024]{1,0:T(8,128)(2,1)S(1)}, u32[]{:S(2)}, u32[]{:S(2)}) collective-permute-start(bf16[256,1024]{1,0:T(8,128)(2,1)} %collective-permute-done.6), channel_id=1, source_target_pairs={{0,16},{4,12},{8,24},{12,4},{16,0},{20,28},{24,8},{28,20},{1,17},{... | collective-permute-start | bytes 1572872 | tf_op jit(solution)/shard_map/ppermute | solution.py:20
  64.4 20.3 %collective-permute-start.19 = (bf16[512,1024]{1,0:T(8,128)(2,1)S(1)}, bf16[512,1024]{1,0:T(8,128)(2,1)S(1)}, u32[]{:S(2)}, u32[]{:S(2)}) collective-permute-start(bf16[512,1024]{1,0:T(8,128)(2,1)S(1)} %pad_maximum_fusion.2.refs_2_), channel_id=1, source_target_pairs={{0,4},{4,0},{8,12},{12,8},{16,20},{20,16},{24,28},{28,24},{1,5},{5... | collective-permute-start | bytes 3145736 | tf_op jit(solution)/shard_map/ppermute | solution.py:20
  68.5 16.2 %collective-permute-start.18 = (bf16[512,1024]{1,0:T(8,128)(2,1)S(1)}, bf16[512,1024]{1,0:T(8,128)(2,1)S(1)}, u32[]{:S(2)}, u32[]{:S(2)}) collective-permute-start(bf16[512,1024]{1,0:T(8,128)(2,1)S(1)} %collective-permute-done.11.refs_0_), channel_id=1, source_target_pairs={{0,4},{4,0},{8,12},{12,8},{16,20},{20,16},{24,28},{28,24},{1,5},{5... | collective-permute-start | bytes 3145736 | tf_op jit(solution)/shard_map/ppermute | solution.py:20
  68.6 12.5 %collective-permute-start.9 = (bf16[256,1024]{1,0:T(8,128)(2,1)S(1)}, bf16[256,1024]{1,0:T(8,128)(2,1)S(1)}, u32[]{:S(2)}, u32[]{:S(2)}) collective-permute-start(bf16[256,1024]{1,0:T(8,128)(2,1)S(1)} %collective-permute-done.8), channel_id=1, source_target_pairs={{1,0},{2,3},{5,4},{6,7},{9,8},{10,11},{13,12},{14,15},{17,16},{18,... | collective-permute-start | bytes 1572872 | tf_op jit(solution)/shard_map/ppermute | solution.py:146
  70.1 14.7 %slice-start = ((s8[5242880]{0:T(1024)(128)(4,1)}), s8[4194304]{0:T(1024)(128)(4,1)S(1)}, s32[]{:S(2)}) async-start(s8[5242880]{0:T(1024)(128)(4,1)} %bitcast.123), calls=%async_computation | async-start | bytes 8388608
  70.1 14.6 %slice-start.1 = ((s8[5242880]{0:T(1024)(128)(4,1)}), s8[1048576]{0:T(1024)(128)(4,1)S(1)}, s32[]{:S(2)}) async-start(s8[5242880]{0:T(1024)(128)(4,1)} %bitcast.123), calls=%async_computation.1 | async-start | bytes 2097152
  73.1 22.1 %collective-permute-start.17 = (bf16[512,1024]{1,0:T(8,128)(2,1)S(1)}, bf16[512,1024]{1,0:T(8,128)(2,1)S(1)}, u32[]{:S(2)}, u32[]{:S(2)}) collective-permute-start(bf16[512,1024]{1,0:T(8,128)(2,1)S(1)} %pad_maximum_fusion.3.refs_0_), channel_id=1, source_target_pairs={{0,16},{4,12},{8,24},{12,4},{16,0},{20,28},{24,8},{28,20},{1,17},{... | collective-permute-start | bytes 3145736 | tf_op jit(solution)/shard_map/ppermute | solution.py:20
  74.4 8.1 %collective-permute-start.21 = (bf16[256,1024]{1,0:T(8,128)(2,1)S(1)}, bf16[256,1024]{1,0:T(8,128)(2,1)S(1)}, u32[]{:S(2)}, u32[]{:S(2)}) collective-permute-start(bf16[256,1024]{1,0:T(8,128)(2,1)S(1)} %collective-permute-done.20.refs_4_), channel_id=1, source_target_pairs={{0,4},{4,0},{8,12},{12,8},{16,20},{20,16},{24,28},{28,24},{1,5},{5... | collective-permute-start | bytes 1572872 | tf_op jit(solution)/shard_map/ppermute | solution.py:20
  81.1 14.1 %collective-permute-start.12 = (bf16[256,1024]{1,0:T(8,128)(2,1)S(1)}, bf16[256,1024]{1,0:T(8,128)(2,1)S(1)}, u32[]{:S(2)}, u32[]{:S(2)}) collective-permute-start(bf16[256,1024]{1,0:T(8,128)(2,1)S(1)} %broadcast_select_fusion.1), channel_id=1, source_target_pairs={{0,8},{4,20},{8,0},{12,28},{16,24},{20,4},{24,16},{28,12},{1,9},{5... | collective-permute-start | bytes 1572872 | tf_op jit(solution)/shard_map/ppermute | solution.py:20
  82.5 17.0 %collective-permute-start.25 = (bf16[256,1024]{1,0:T(8,128)(2,1)S(1)}, bf16[256,1024]{1,0:T(8,128)(2,1)S(1)}, u32[]{:S(2)}, u32[]{:S(2)}) collective-permute-start(bf16[256,1024]{1,0:T(8,128)(2,1)S(1)} %slice.19), channel_id=1, source_target_pairs={{0,1},{1,0},{2,3},{3,2},{4,5},{5,4},{6,7},{7,6},{8,9},{9,8},{10,11... | collective-permute-start | bytes 1572872 | tf_op jit(solution)/shard_map/ppermute | solution.py:138
  84.8 19.2 %slice-start.2 = ((s8[5242880]{0:T(1024)(128)(4,1)}), s8[4194304]{0:T(1024)(128)(4,1)S(1)}, s32[]{:S(2)}) async-start(s8[5242880]{0:T(1024)(128)(4,1)} %bitcast.125), calls=%async_computation.2 | async-start | bytes 8388608
  84.8 19.2 %slice-start.3 = ((s8[5242880]{0:T(1024)(128)(4,1)}), s8[1048576]{0:T(1024)(128)(4,1)S(1)}, s32[]{:S(2)}) async-start(s8[5242880]{0:T(1024)(128)(4,1)} %bitcast.125), calls=%async_computation.3 | async-start | bytes 2097152
  95.2 8.4 %collective-permute-start.24 = (bf16[512,1024]{1,0:T(8,128)(2,1)S(1)}, bf16[512,1024]{1,0:T(8,128)(2,1)S(1)}, u32[]{:S(2)}, u32[]{:S(2)}) collective-permute-start(bf16[512,1024]{1,0:T(8,128)(2,1)S(1)} %collective-permute-done.17.refs_2_), channel_id=1, source_target_pairs={{0,4},{4,0},{8,12},{12,8},{16,20},{20,16},{24,28},{28,24},{1,5},{5... | collective-permute-start | bytes 3145736 | tf_op jit(solution)/shard_map/ppermute | solution.py:20
  99.0 4.5 %collective-permute-start.23 = (bf16[512,1024]{1,0:T(8,128)(2,1)S(1)}, bf16[512,1024]{1,0:T(8,128)(2,1)S(1)}, u32[]{:S(2)}, u32[]{:S(2)}) collective-permute-start(bf16[512,1024]{1,0:T(8,128)(2,1)S(1)} %pad_maximum_fusion.3.refs_0_), channel_id=1, source_target_pairs={{0,4},{4,0},{8,12},{12,8},{16,20},{20,16},{24,28},{28,24},{1,5},{5... | collective-permute-start | bytes 3145736 | tf_op jit(solution)/shard_map/ppermute | solution.py:20
  99.1 14.0 %collective-permute-start.22 = (bf16[512,1024]{1,0:T(8,128)(2,1)S(1)}, bf16[512,1024]{1,0:T(8,128)(2,1)S(1)}, u32[]{:S(2)}, u32[]{:S(2)}) collective-permute-start(bf16[512,1024]{1,0:T(8,128)(2,1)S(1)} %constant_dynamic-update-slice_fusion.refs_0_), channel_id=1, source_target_pairs={{0,16},{4,12},{8,24},{12,4},{16,0},{20,28},{24,8},{28,20},{1,17},{... | collective-permute-start | bytes 3145736 | tf_op jit(solution)/shard_map/ppermute | solution.py:20
  99.4 4.1 %collective-permute-start.26 = (bf16[256,1024]{1,0:T(8,128)(2,1)S(1)}, bf16[256,1024]{1,0:T(8,128)(2,1)S(1)}, u32[]{:S(2)}, u32[]{:S(2)}) collective-permute-start(bf16[256,1024]{1,0:T(8,128)(2,1)S(1)} %collective-permute-done.25.refs_4_), channel_id=1, source_target_pairs={{0,4},{4,0},{8,12},{12,8},{16,20},{20,16},{24,28},{28,24},{1,5},{5... | collective-permute-start | bytes 1572872 | tf_op jit(solution)/shard_map/ppermute | solution.py:20
  103.6 10.9 %collective-permute-start.28 = (bf16[512,1024]{1,0:T(8,128)(2,1)S(1)}, bf16[512,1024]{1,0:T(8,128)(2,1)S(1)}, u32[]{:S(2)}, u32[]{:S(2)}) collective-permute-start(bf16[512,1024]{1,0:T(8,128)(2,1)S(1)} %constant_dynamic-update-slice_fusion.refs_0_), channel_id=1, source_target_pairs={{0,4},{4,0},{8,12},{12,8},{16,20},{20,16},{24,28},{28,24},{1,5},{5... | collective-permute-start | bytes 3145736 | tf_op jit(solution)/shard_map/ppermute | solution.py:20
  103.9 10.5 %copy-start.2 = (bf16[1024,1024]{1,0:T(8,128)(2,1)S(1)}, bf16[1024,1024]{1,0:T(8,128)(2,1)}, u32[]{:S(2)}) copy-start(bf16[1024,1024]{1,0:T(8,128)(2,1)} %get-tuple-element.144.normed) | copy-start | bytes 6291460
  113.1 4.3 %collective-permute-start.27 = (bf16[512,1024]{1,0:T(8,128)(2,1)S(1)}, bf16[512,1024]{1,0:T(8,128)(2,1)S(1)}, u32[]{:S(2)}, u32[]{:S(2)}) collective-permute-start(bf16[512,1024]{1,0:T(8,128)(2,1)S(1)} %collective-permute-done.22.refs_0_), channel_id=1, source_target_pairs={{0,4},{4,0},{8,12},{12,8},{16,20},{20,16},{24,28},{28,24},{1,5},{5... | collective-permute-start | bytes 3145736 | tf_op jit(solution)/shard_map/ppermute | solution.py:20
  114.5 2.9 %copy-start = (bf16[1024,1024]{1,0:T(8,128)(2,1)S(1)}, bf16[1024,1024]{1,0:T(8,128)(2,1)}, u32[]{:S(2)}) copy-start(bf16[1024,1024]{1,0:T(8,128)(2,1)} %get-tuple-element.110.normed) | copy-start | bytes 6291460

commit v5 on v4

--- a/solution.py
+++ b/solution.py
@@ -109,7 +109,7 @@
     cols = pieces[0].shape[1]
     depths = [piece.shape[0] for piece in pieces]
     depth = sum(depths)
-    tile = 256
+    tile = 512
     first = total.shape != (rows, cols)
     row_spec = pl.BlockSpec((tile, cols), lambda i: (i, 0))
     return pl.pallas_call(

time: 122 us -> 121 us (level)
  Pallas kernels: 40.7 us -> 39 us
    pallas_call x5, Pallas kernels: 21.8 us -> 20.1 us  [project(): pl.pallas_call(functools.partial(project_kernel, depths), grid=(rows // t...]
  transfers between devices with their start and end apart: 29 -> 29, of which waited for: 9 -> 9; matrix products, arithmetic and copies ran while one was open for 8% -> 8% of each run, Pallas kernels for 30% -> 29%
where the time goes in v5:
time: 121 us
  starting transfers between devices  46.1 us (38%)
  Pallas kernels  39 us (32%)
  waiting for transfers between devices  20.7 us (17%)
  other arithmetic  9.54 us (8%)
  local copies, waits for them, and re-layouts  4.28 us (4%)
    ppermute x23, starting transfers between devices, flip(): return lax.ppermute(value, 'rep', perm)  31.2 us
    pallas_call x5, Pallas kernels, project(): pl.pallas_call(functools.partial(project_kernel, depths), grid=(rows // t...  20.1 us
    pallas_call x3, Pallas kernels, normalize_in_order(): pl.pallas_call(functools.partial(normalize_kernel, width=width, parts=len...  18.9 us
    ppermute x23, waiting for transfers between devices, flip(): return lax.ppermute(value, 'rep', perm)  18.6 us
    ppermute x2, starting transfers between devices, inwards(): return lax.ppermute(value, 'fsdp', [(1, 2), (2, 1)])  8.64 us
    ppermute x2, starting transfers between devices, outwards(): return lax.ppermute(value, 'fsdp', [(1, 0), (2, 3)])  3.85 us
    another operation x2, other arithmetic  2.72 us
    reshape x2, local copies, waits for them, and re-layouts, on_block(): theirs = theirs.reshape(4, half_rows, cols)  2.6 us
  transfers between devices with their start and end apart: 29, of which 9 were waited for; matrix products, arithmetic and copies ran while one was open for 8% of the time, Pallas kernels for 29%

profile of v5, /device:TPU:9, one launch (start us, length us, event | category | flops | bytes accessed | tf_op | source)
XLA Modules:
  0.0 120.9 jit_solution(13039190355753937919)
XLA Ops:
  0.7 1.3 %dynamic-slice_bitcast_fusion.1 = bf16[4,128,1024]{2,1,0:T(8,128)(2,1)S(1)} fusion(bf16[4,2,2,128,1024]{4,3,2,1,0:T(8,128)(2,1)} %bitcast.127, s32[]{:T(128)S(6)} %select_n.62), kind=kLoop, calls=%fused_computation.7 | loop fusion | bytes 2097156 | tf_op jit(solution)/shard_map/reshape | solution.py:197
  2.0 0.7 collective-permute-start
  2.7 1.3 %dynamic-slice_bitcast_fusion = bf16[4,128,1024]{2,1,0:T(8,128)(2,1)S(1)} fusion(bf16[4,2,2,128,1024]{4,3,2,1,0:T(8,128)(2,1)} %bitcast.128, s32[]{:T(128)S(6)} %select_n.63), kind=kLoop, calls=%fused_computation.6 | loop fusion | bytes 2097156 | tf_op jit(solution)/shard_map/reshape | solution.py:197
  4.7 0.4 collective-permute-done
  5.0 1.3 %fusion.11 = (bf16[128,1024]{1,0:T(8,128)(2,1)S(1)}, bf16[128,1024]{1,0:T(8,128)(2,1)S(1)}) fusion(bf16[4,128,1024]{2,1,0:T(8,128)(2,1)S(1)} %collective-permute-done, s32[]{:T(128)S(6)} %select_n.130, f32[128]{0:T(128)S(1)} %get-tuple-element.184, bf16[4,2,2,128,1024]{4,3,2,1,0:T(8,128)(2,1)} %bitcast.129, s32[]{:T(128)S(6)} %select_n.131, ...), kind=kLoop, calls=%fused_computation.36 | loop fusion | flops 1572864 | bytes 1574924 | tf_op jit(solution)/shard_map/convert.18
  6.3 1.3 %collective-permute-start.2 = (bf16[256,1024]{1,0:T(8,128)(2,1)S(1)}, bf16[256,1024]{1,0:T(8,128)(2,1)S(1)}, u32[]{:S(2)}, u32[]{:S(2)}) collective-permute-start(bf16[256,1024]{1,0:T(8,128)(2,1)S(1)} %pad_maximum_fusion.4), channel_id=1, source_target_pairs={{0,8},{4,20},{8,0},{12,28},{16,24},{20,4},{24,16},{28,12},{1,9},{5... | collective-permute-start | bytes 1572872 | tf_op jit(solution)/shard_map/ppermute | solution.py:20
  7.7 1.4 %fusion.7 = (bf16[128,1024]{1,0:T(8,128)(2,1)S(1)}, bf16[128,1024]{1,0:T(8,128)(2,1)S(1)}) fusion(bf16[4,128,1024]{2,1,0:T(8,128)(2,1)} %collective-permute-done.1, s32[]{:T(128)S(6)} %select_n.130, f32[128]{0:T(128)S(1)} %get-tuple-element.186, bf16[4,2,2,128,1024]{4,3,2,1,0:T(8,128)(2,1)} %bitcast.130, s32[]{:T(128)S(6)} %select_n.131, ...), kind=kLoop, calls=%fused_computation.28 | loop fusion | flops 1572864 | bytes 1574924 | tf_op jit(solution)/shard_map/convert.16
  9.1 0.5 collective-permute-start.3
  9.7 5.1 %normalize_in_order.3 = (bf16[1024,1024]{1,0:T(8,128)(2,1)}, bf16[1024,2560]{1,0:T(8,128)(2,1)}, bf16[1024,2560]{1,0:T(8,128)(2,1)}, bf16[1024,1024]{1,0:T(8,128...) custom-call(s32[32]{0:T(128)S(1)} %stack.131.order, bf16[1024,8192]{1,0:T(8,128)(2,1)} %tokens.5, ...), custom_call_target="tpu_custom_call" | custom-call | flops 12582912 | bytes 8388608 | tf_op jit(solution)/shard_map/normalize_in_order/pallas_call | solution.py:68
  14.7 1.8 %fusion = (f32[128,1024]{1,0:T(8,128)S(1)}, f32[128,1024]{1,0:T(8,128)S(1)}, f32[128,1024]{1,0:T(8,128)S(1)}, f32[128,1024]{1,0:T(8,128)S(1)}) fusion(bf16[4,128,1024]{2,1,0:T(8,128)(2,1)} %collective-permute-done.1, s32[]{:T(128)S(6)} %select_n.138, f32[128]{0:T(128)S(1)} %get-tuple-element.191, bf16[4,2,2,128,1024]{4,3,2,1,0:T(8,128)(2,1)} %bitcast.131, ...), kind=kLoop, calls=%fused_computation.11 | loop fusion | flops 2621440 | bytes 4198412 | tf_op jit(solution)/shard_map/add | solution.py:188
  16.7 1.3 %collective-permute-start.4 = (bf16[128,1024]{1,0:T(8,128)(2,1)S(1)}, bf16[128,1024]{1,0:T(8,128)(2,1)S(1)}, u32[]{:S(2)}, u32[]{:S(2)}) collective-permute-start(bf16[128,1024]{1,0:T(8,128)(2,1)S(1)} %get-tuple-element.165), channel_id=1, source_target_pairs={{0,16},{4,12},{8,24},{12,4},{16,0},{20,28},{24,8},{28,20},{1,17},{... | collective-permute-start | bytes 786440 | tf_op jit(solution)/shard_map/ppermute | solution.py:20
  17.9 2.4 %collective-permute-done.3 = bf16[256,1024]{1,0:T(8,128)(2,1)S(1)} collective-permute-done((bf16[256,1024]{1,0:T(8,128)(2,1)S(1)}, bf16[256,1024]{1,0:T(8,128)(2,1)S(1)}, u32[]{:S(2)}, u32[]{:S(2)}) %collective-permute-start.3) | collective-permute-done | bytes 524320 | tf_op jit(solution)/shard_map/ppermute | solution.py:20
  20.5 1.3 %collective-permute-start.5 = (bf16[128,1024]{1,0:T(8,128)(2,1)S(1)}, bf16[128,1024]{1,0:T(8,128)(2,1)S(1)}, u32[]{:S(2)}, u32[]{:S(2)}) collective-permute-start(bf16[128,1024]{1,0:T(8,128)(2,1)S(1)} %get-tuple-element.163), channel_id=1, source_target_pairs={{0,16},{4,12},{8,24},{12,4},{16,0},{20,28},{24,8},{28,20},{1,17},{... | collective-permute-start | bytes 786440 | tf_op jit(solution)/shard_map/ppermute | solution.py:20
  21.8 5.1 %normalize_in_order.4 = (bf16[1024,1024]{1,0:T(8,128)(2,1)}, bf16[1024,2560]{1,0:T(8,128)(2,1)}, bf16[1024,2560]{1,0:T(8,128)(2,1)}, bf16[1024,1024]{1,0:T(8,128...) custom-call(s32[32]{0:T(128)S(1)} %stack.131.order, ...), custom_call_target="tpu_custom_call", output_to_operand_aliasing={{0}: (3, {}), {1}: (4, {}), {2}: (5, {}), {3}: (6, {}), {4}... | custom-call | flops 12582912 | bytes 8388608 | tf_op jit(solution)/shard_map/normalize_in_order/pallas_call | solution.py:68
  27.0 1.0 copy-done.3
  28.4 1.7 %fusion.30 = (bf16[256,1024]{1,0:T(8,128)(2,1)S(1)}, f32[256,1024]{1,0:T(8,128)}, f32[256,1024]{1,0:T(8,128)}) fusion(f32[256,1024]{1,0:T(8,128)S(1)} %copy-done.3, f32[128,1024]{1,0:T(8,128)S(1)} %convert_add_fusion, f32[128,1024]{1,0:T(8,128)S(1)} %convert_add_fusion.1, f32[256,1024]{1,0:T(8,128)S(1)} %copy-done.4), kind=kLoop, calls=%fused_computation.89 | loop fusion | flops 2097152 | bytes 5767168 | tf_op jit(solution)/shard_map/convert_element_type | solution.py:226
  30.1 1.2 %collective-permute-start.10 = (bf16[256,1024]{1,0:T(8,128)(2,1)S(1)}, bf16[256,1024]{1,0:T(8,128)(2,1)S(1)}, u32[]{:S(2)}, u32[]{:S(2)}) collective-permute-start(bf16[256,1024]{1,0:T(8,128)(2,1)S(1)} %get-tuple-element.149), channel_id=1, source_target_pairs={{0,8},{4,20},{8,0},{12,28},{16,24},{20,4},{24,16},{28,12},{1,9},{5... | collective-permute-start | bytes 1572872 | tf_op jit(solution)/shard_map/ppermute | solution.py:20
  31.5 4.3 %collective-permute-start.7 = (bf16[256,1024]{1,0:T(8,128)(2,1)S(1)}, bf16[256,1024]{1,0:T(8,128)(2,1)}, u32[]{:S(2)}, u32[]{:S(2)}) collective-permute-start(bf16[256,1024]{1,0:T(8,128)(2,1)S(1)} %get-tuple-element.149), channel_id=1, source_target_pairs={{1,2},{2,1},{5,6},{6,5},{9,10},{10,9},{13,14},{14,13},{17,18},{18,... | collective-permute-start | bytes 1572872 | tf_op jit(solution)/shard_map/ppermute | solution.py:142
  35.8 2.7 %collective-permute-done.10 = bf16[256,1024]{1,0:T(8,128)(2,1)S(1)} collective-permute-done((bf16[256,1024]{1,0:T(8,128)(2,1)S(1)}, bf16[256,1024]{1,0:T(8,128)(2,1)S(1)}, u32[]{:S(2)}, u32[]{:S(2)}) %collective-permute-start.10) | collective-permute-done | bytes 524320 | tf_op jit(solution)/shard_map/ppermute | solution.py:20
  38.6 4.3 %collective-permute-start.16 = (bf16[512,1024]{1,0:T(8,128)(2,1)S(1)}, bf16[512,1024]{1,0:T(8,128)(2,1)S(1)}, u32[]{:S(2)}, u32[]{:S(2)}) collective-permute-start(bf16[512,1024]{1,0:T(8,128)(2,1)S(1)} %pad_maximum_fusion.1.refs_0_), channel_id=1, source_target_pairs={{0,4},{4,0},{8,12},{12,8},{16,20},{20,16},{24,28},{28,24},{1,5},{5... | collective-permute-start | bytes 3145736 | tf_op jit(solution)/shard_map/ppermute | solution.py:20
  42.9 1.2 collective-permute-start.11
  44.1 0.5 collective-permute-start.13
  44.6 2.4 %collective-permute-start.14 = (bf16[256,1024]{1,0:T(8,128)(2,1)}, bf16[256,1024]{1,0:T(8,128)(2,1)}, u32[]{:S(2)}, u32[]{:S(2)}) collective-permute-start(bf16[256,1024]{1,0:T(8,128)(2,1)} %collective-permute-done.7), channel_id=1, source_target_pairs={{1,0},{2,3},{5,4},{6,7},{9,8},{10,11},{13,12},{14,15},{17,16},{18,... | collective-permute-start | bytes 1572872 | tf_op jit(solution)/shard_map/ppermute | solution.py:146
  47.0 4.3 %collective-permute-start.8 = (bf16[256,1024]{1,0:T(8,128)(2,1)}, bf16[256,1024]{1,0:T(8,128)(2,1)S(1)}, u32[]{:S(2)}, u32[]{:S(2)}) collective-permute-start(bf16[256,1024]{1,0:T(8,128)(2,1)} %collective-permute-done.6), channel_id=1, source_target_pairs={{1,2},{2,1},{5,6},{6,5},{9,10},{10,9},{13,14},{14,13},{17,18},{18,... | collective-permute-start | bytes 1572872 | tf_op jit(solution)/shard_map/ppermute | solution.py:142
  51.3 8.8 %normalize_in_order.5 = (bf16[1024,1024]{1,0:T(8,128)(2,1)}, bf16[1024,2560]{1,0:T(8,128)(2,1)}, bf16[1024,2560]{1,0:T(8,128)(2,1)}, bf16[1024,1024]{1,0:T(8,128...) custom-call(s32[32]{0:T(128)S(1)} %stack.131.order, ...), custom_call_target="tpu_custom_call", output_to_operand_aliasing={{0}: (3, {}), {1}: (4, {}), {2}: (5, {}), {3}: (6, {}), {4}... | custom-call | flops 25165824 | bytes 16777216 | tf_op jit(solution)/shard_map/normalize_in_order/pallas_call | solution.py:68
  60.1 1.3 %broadcast_select_fusion = bf16[256,1024]{1,0:T(8,128)(2,1)S(1)} fusion(bf16[256,1024]{1,0:T(8,128)(2,1)} %collective-permute-done.14, bf16[256,1024]{1,0:T(8,128)(2,1)} %collective-permute-done.7, pred[]{:T(512)S(6)} %or.3), kind=kLoop, calls=%fused_computation.44 | loop fusion | flops 262144 | bytes 1572865 | tf_op jit(solution)/shard_map/jit(_where)/select_n | solution.py:242
  61.4 1.5 %collective-permute-start.15 = (bf16[256,1024]{1,0:T(8,128)(2,1)S(1)}, bf16[256,1024]{1,0:T(8,128)(2,1)S(1)}, u32[]{:S(2)}, u32[]{:S(2)}) collective-permute-start(bf16[256,1024]{1,0:T(8,128)(2,1)S(1)} %broadcast_select_fusion), channel_id=1, source_target_pairs={{0,8},{4,20},{8,0},{12,28},{16,24},{20,4},{24,16},{28,12},{1,9},{5... | collective-permute-start | bytes 1572872 | tf_op jit(solution)/shard_map/ppermute | solution.py:20
  63.1 1.3 %pad_maximum_fusion.2.refs_2_ = bf16[512,1024]{1,0:T(8,128)(2,1)S(1)} fusion(bf16[256,1024]{1,0:T(8,128)(2,1)} %collective-permute-done.13, bf16[256,1024]{1,0:T(8,128)(2,1)} %collective-permute-done.6), kind=kLoop, calls=%fused_computation.2 | loop fusion | flops 2097152 | bytes 2097152 | tf_op jit(solution)/shard_map/concatenate | solution.py:243
  64.4 4.1 %collective-permute-start.19 = (bf16[512,1024]{1,0:T(8,128)(2,1)S(1)}, bf16[512,1024]{1,0:T(8,128)(2,1)S(1)}, u32[]{:S(2)}, u32[]{:S(2)}) collective-permute-start(bf16[512,1024]{1,0:T(8,128)(2,1)S(1)} %pad_maximum_fusion.2.refs_2_), channel_id=1, source_target_pairs={{0,4},{4,0},{8,12},{12,8},{16,20},{20,16},{24,28},{28,24},{1,5},{5... | collective-permute-start | bytes 3145736 | tf_op jit(solution)/shard_map/ppermute | solution.py:20
  68.6 1.5 %collective-permute-start.9 = (bf16[256,1024]{1,0:T(8,128)(2,1)S(1)}, bf16[256,1024]{1,0:T(8,128)(2,1)S(1)}, u32[]{:S(2)}, u32[]{:S(2)}) collective-permute-start(bf16[256,1024]{1,0:T(8,128)(2,1)S(1)} %collective-permute-done.8), channel_id=1, source_target_pairs={{1,0},{2,3},{5,4},{6,7},{9,8},{10,11},{13,12},{14,15},{17,16},{18,... | collective-permute-start | bytes 1572872 | tf_op jit(solution)/shard_map/ppermute | solution.py:146
  70.1 2.5 %project.5.refs_6_ = f32[1024,1024]{1,0:T(8,128)S(1)} custom-call(bf16[1024,1024]{1,0:T(8,128)(2,1)S(1)} %copy-done.1, bf16[512,1024]{1,0:T(8,128)(2,1)S(1)} %pad_maximum_fusion.1.refs_0_, bf16[512,1024]{1,0:T(8,128)(2,1)S(1)} %collective-permute-done.16.refs_1_, f32[8,128]{1,0:T(8,128)S(1)} %get-tuple-element.120.refs_2_), custom_call_target="tpu_custom_call" | custom-call | flops 2147483648 | bytes 12582912 | tf_op jit(solution)/shard_map/project/pallas_call | solution.py:115
  72.8 0.3 collective-permute-start.17
  73.1 1.3 %collective-permute-done.20.refs_4_ = bf16[256,1024]{1,0:T(8,128)(2,1)S(1)} collective-permute-done((bf16[256,1024]{1,0:T(8,128)(2,1)}, bf16[256,1024]{1,0:T(8,128)(2,1)S(1)}, u32[]{:S(2)}, u32[]{:S(2)}) %collective-permute-start.20) | collective-permute-done | bytes 524320 | tf_op jit(solution)/shard_map/ppermute | solution.py:20
  74.4 4.6 %collective-permute-start.21 = (bf16[256,1024]{1,0:T(8,128)(2,1)S(1)}, bf16[256,1024]{1,0:T(8,128)(2,1)S(1)}, u32[]{:S(2)}, u32[]{:S(2)}) collective-permute-start(bf16[256,1024]{1,0:T(8,128)(2,1)S(1)} %collective-permute-done.20.refs_4_), channel_id=1, source_target_pairs={{0,4},{4,0},{8,12},{12,8},{16,20},{20,16},{24,28},{28,24},{1,5},{5... | collective-permute-start | bytes 1572872 | tf_op jit(solution)/shard_map/ppermute | solution.py:20
  79.0 2.0 %collective-permute-done.9 = bf16[256,1024]{1,0:T(8,128)(2,1)S(1)} collective-permute-done((bf16[256,1024]{1,0:T(8,128)(2,1)S(1)}, bf16[256,1024]{1,0:T(8,128)(2,1)S(1)}, u32[]{:S(2)}, u32[]{:S(2)}) %collective-permute-start.9) | collective-permute-done | bytes 524320 | tf_op jit(solution)/shard_map/ppermute | solution.py:146
  81.1 1.3 %collective-permute-start.12 = (bf16[256,1024]{1,0:T(8,128)(2,1)S(1)}, bf16[256,1024]{1,0:T(8,128)(2,1)S(1)}, u32[]{:S(2)}, u32[]{:S(2)}) collective-permute-start(bf16[256,1024]{1,0:T(8,128)(2,1)S(1)} %broadcast_select_fusion.1), channel_id=1, source_target_pairs={{0,8},{4,20},{8,0},{12,28},{16,24},{20,4},{24,16},{28,12},{1,9},{5... | collective-permute-start | bytes 1572872 | tf_op jit(solution)/shard_map/ppermute | solution.py:20
  82.5 2.3 %collective-permute-start.25 = (bf16[256,1024]{1,0:T(8,128)(2,1)S(1)}, bf16[256,1024]{1,0:T(8,128)(2,1)S(1)}, u32[]{:S(2)}, u32[]{:S(2)}) collective-permute-start(bf16[256,1024]{1,0:T(8,128)(2,1)S(1)} %slice.19), channel_id=1, source_target_pairs={{0,1},{1,0},{2,3},{3,2},{4,5},{5,4},{6,7},{7,6},{8,9},{9,8},{10,11... | collective-permute-start | bytes 1572872 | tf_op jit(solution)/shard_map/ppermute | solution.py:138
  84.8 5.8 %project.6.refs_6_ = f32[1024,1024]{1,0:T(8,128)S(1)} custom-call(bf16[1024,2560]{1,0:T(8,128)(2,1)S(1)} %bitcast.124, bf16[512,1024]{1,0:T(8,128)(2,1)S(1)} %collective-permute-done.11.refs_0_, bf16[512,1024]{1,0:T(8,128)(2,1)S(1)} %collective-permute-done.18.refs_1_, bf16[512,1024]{1,0:T(8,128)(2,1)S(1)} %pad_maximum_fusion.2.refs_2_, ...), custom_call_target="tpu_custom_call" | custom-call | flops 5368709120 | bytes 18874368 | tf_op jit(solution)/shard_map/project/pallas_call | solution.py:115
  90.6 4.6 %collective-permute-done.12 = bf16[256,1024]{1,0:T(8,128)(2,1)S(1)} collective-permute-done((bf16[256,1024]{1,0:T(8,128)(2,1)S(1)}, bf16[256,1024]{1,0:T(8,128)(2,1)S(1)}, u32[]{:S(2)}, u32[]{:S(2)}) %collective-permute-start.12) | collective-permute-done | bytes 524320 | tf_op jit(solution)/shard_map/ppermute | solution.py:20
  95.2 4.2 %collective-permute-start.24 = (bf16[512,1024]{1,0:T(8,128)(2,1)S(1)}, bf16[512,1024]{1,0:T(8,128)(2,1)S(1)}, u32[]{:S(2)}, u32[]{:S(2)}) collective-permute-start(bf16[512,1024]{1,0:T(8,128)(2,1)S(1)} %collective-permute-done.17.refs_2_), channel_id=1, source_target_pairs={{0,4},{4,0},{8,12},{12,8},{16,20},{20,16},{24,28},{28,24},{1,5},{5... | collective-permute-start | bytes 3145736 | tf_op jit(solution)/shard_map/ppermute | solution.py:20
  99.5 0.3 collective-permute-start.22
  100.1 3.8 %collective-permute-done.26.refs_5_ = bf16[256,1024]{1,0:T(8,128)(2,1)S(1)} collective-permute-done((bf16[256,1024]{1,0:T(8,128)(2,1)S(1)}, bf16[256,1024]{1,0:T(8,128)(2,1)S(1)}, u32[]{:S(2)}, u32[]{:S(2)}) %collective-permute-start.26) | collective-permute-done | bytes 524320 | tf_op jit(solution)/shard_map/ppermute | solution.py:20
  103.9 0.4 collective-permute-start.28
  104.3 5.8 %project.7.refs_2_ = f32[1024,1024]{1,0:T(8,128)S(1)} custom-call(bf16[1024,2560]{1,0:T(8,128)(2,1)S(1)} %bitcast.126, bf16[512,1024]{1,0:T(8,128)(2,1)S(1)} %pad_maximum_fusion.3.refs_0_, bf16[512,1024]{1,0:T(8,128)(2,1)S(1)} %collective-permute-done.23.refs_1_, bf16[512,1024]{1,0:T(8,128)(2,1)S(1)} %collective-permute-done.17.refs_2_, ...), custom_call_target="tpu_custom_call" | custom-call | flops 5368709120 | bytes 18874368 | tf_op jit(solution)/shard_map/project/pallas_call | solution.py:115
  110.1 3.4 %collective-permute-done.22.refs_0_ = bf16[512,1024]{1,0:T(8,128)(2,1)S(1)} collective-permute-done((bf16[512,1024]{1,0:T(8,128)(2,1)S(1)}, bf16[512,1024]{1,0:T(8,128)(2,1)S(1)}, u32[]{:S(2)}, u32[]{:S(2)}) %collective-permute-start.22) | collective-permute-done | bytes 1048608 | tf_op jit(solution)/shard_map/ppermute | solution.py:20
  113.5 1.4 %collective-permute-start.27 = (bf16[512,1024]{1,0:T(8,128)(2,1)S(1)}, bf16[512,1024]{1,0:T(8,128)(2,1)S(1)}, u32[]{:S(2)}, u32[]{:S(2)}) collective-permute-start(bf16[512,1024]{1,0:T(8,128)(2,1)S(1)} %collective-permute-done.22.refs_0_), channel_id=1, source_target_pairs={{0,4},{4,0},{8,12},{12,8},{16,20},{20,16},{24,28},{28,24},{1,5},{5... | collective-permute-start | bytes 3145736 | tf_op jit(solution)/shard_map/ppermute | solution.py:20
  114.8 2.5 %project.8.refs_2_ = f32[1024,1024]{1,0:T(8,128)S(1)} custom-call(bf16[1024,1024]{1,0:T(8,128)(2,1)S(1)} %copy-done.2, bf16[512,1024]{1,0:T(8,128)(2,1)S(1)} %constant_dynamic-update-slice_fusion.refs_0_, bf16[512,1024]{1,0:T(8,128)(2,1)S(1)} %collective-permute-done.28.refs_1_, f32[1024,1024]{1,0:T(8,128)S(1)} %project.7.refs_2_), custom_call_target="tpu_custom_call" | custom-call | flops 2147483648 | bytes 12582912 | tf_op jit(solution)/shard_map/project/pallas_call | solution.py:115
  117.4 3.5 %project.9 = bf16[1024,1024]{1,0:T(8,128)(2,1)} custom-call(bf16[1024,1024]{1,0:T(8,128)(2,1)S(1)} %copy-done, bf16[512,1024]{1,0:T(8,128)(2,1)S(1)} %collective-permute-done.22.refs_0_, bf16[512,1024]{1,0:T(8,128)(2,1)S(1)} %collective-permute-done.27.refs_1_, f32[1024,1024]{1,0:T(8,128)S(1)} %project.8.refs_2_), custom_call_target="tpu_custom_call" | custom-call | flops 2147483648 | bytes 12582912 | tf_op jit(solution)/shard_map/project/pallas_call | solution.py:115
  (71 shorter events, 2.5 us)
Async XLA Ops:
  0.6 3.6 %copy-start.5 = (bf16[8192]{0:T(1024)(128)(2,1)S(1)}, bf16[8192]{0:T(1024)(128)(2,1)}, u32[]{:S(2)}) copy-start(bf16[8192]{0:T(1024)(128)(2,1)} %param.8) | copy-start | bytes 49156
  0.6 3.8 %copy-start.6 = (s32[8,16]{1,0:T(8,128)S(1)}, s32[8,16]{1,0:T(8,128)}, u32[]{:S(2)}) copy-start(s32[8,16]{1,0:T(8,128)} %param.10) | copy-start | bytes 1540
  0.7 3.8 %copy-start.7 = (s32[2048]{0:T(1024)S(1)}, s32[2048]{0:T(1024)}, u32[]{:S(2)}) copy-start(s32[2048]{0:T(1024)} %param.11) | copy-start | bytes 24580
  2.0 3.0 %collective-permute-start = (bf16[4,128,1024]{2,1,0:T(8,128)(2,1)S(1)}, bf16[4,128,1024]{2,1,0:T(8,128)(2,1)S(1)}, u32[]{:S(2)}, u32[]{:S(2)}) collective-permute-start(bf16[4,128,1024]{2,1,0:T(8,128)(2,1)S(1)} %dynamic-slice_bitcast_fusion.1), channel_id=1, source_target_pairs={{0,4},{4,0},{8,12},{12,8},{16,20},{20,16},{24,28},{28,24},{1,5},{5... | collective-permute-start | bytes 3145736 | tf_op jit(solution)/shard_map/ppermute | solution.py:20
  4.0 3.6 %collective-permute-start.1 = (bf16[4,128,1024]{2,1,0:T(8,128)(2,1)S(1)}, bf16[4,128,1024]{2,1,0:T(8,128)(2,1)}, u32[]{:S(2)}, u32[]{:S(2)}) collective-permute-start(bf16[4,128,1024]{2,1,0:T(8,128)(2,1)S(1)} %dynamic-slice_bitcast_fusion), channel_id=1, source_target_pairs={{0,4},{4,0},{8,12},{12,8},{16,20},{20,16},{24,28},{28,24},{1,5},{5... | collective-permute-start | bytes 3145736 | tf_op jit(solution)/shard_map/ppermute | solution.py:20
  6.3 10.1 %collective-permute-start.2 = (bf16[256,1024]{1,0:T(8,128)(2,1)S(1)}, bf16[256,1024]{1,0:T(8,128)(2,1)S(1)}, u32[]{:S(2)}, u32[]{:S(2)}) collective-permute-start(bf16[256,1024]{1,0:T(8,128)(2,1)S(1)} %pad_maximum_fusion.4), channel_id=1, source_target_pairs={{0,8},{4,20},{8,0},{12,28},{16,24},{20,4},{24,16},{28,12},{1,9},{5... | collective-permute-start | bytes 1572872 | tf_op jit(solution)/shard_map/ppermute | solution.py:20
  9.1 11.2 %collective-permute-start.3 = (bf16[256,1024]{1,0:T(8,128)(2,1)S(1)}, bf16[256,1024]{1,0:T(8,128)(2,1)S(1)}, u32[]{:S(2)}, u32[]{:S(2)}) collective-permute-start(bf16[256,1024]{1,0:T(8,128)(2,1)S(1)} %pad_maximum_fusion.5), channel_id=1, source_target_pairs={{0,8},{4,20},{8,0},{12,28},{16,24},{20,4},{24,16},{28,12},{1,9},{5... | collective-permute-start | bytes 1572872 | tf_op jit(solution)/shard_map/ppermute | solution.py:20
  16.7 10.2 %collective-permute-start.4 = (bf16[128,1024]{1,0:T(8,128)(2,1)S(1)}, bf16[128,1024]{1,0:T(8,128)(2,1)S(1)}, u32[]{:S(2)}, u32[]{:S(2)}) collective-permute-start(bf16[128,1024]{1,0:T(8,128)(2,1)S(1)} %get-tuple-element.165), channel_id=1, source_target_pairs={{0,16},{4,12},{8,24},{12,4},{16,0},{20,28},{24,8},{28,20},{1,17},{... | collective-permute-start | bytes 786440 | tf_op jit(solution)/shard_map/ppermute | solution.py:20
  20.5 6.4 %collective-permute-start.5 = (bf16[128,1024]{1,0:T(8,128)(2,1)S(1)}, bf16[128,1024]{1,0:T(8,128)(2,1)S(1)}, u32[]{:S(2)}, u32[]{:S(2)}) collective-permute-start(bf16[128,1024]{1,0:T(8,128)(2,1)S(1)} %get-tuple-element.163), channel_id=1, source_target_pairs={{0,16},{4,12},{8,24},{12,4},{16,0},{20,28},{24,8},{28,20},{1,17},{... | collective-permute-start | bytes 786440 | tf_op jit(solution)/shard_map/ppermute | solution.py:20
  26.8 1.2 %copy-start.3 = (f32[256,1024]{1,0:T(8,128)S(1)}, f32[256,1024]{1,0:T(8,128)}, u32[]{:S(2)}) copy-start(f32[256,1024]{1,0:T(8,128)} %param.12) | copy-start | bytes 3145732
  26.8 1.5 %copy-start.4 = (f32[256,1024]{1,0:T(8,128)S(1)}, f32[256,1024]{1,0:T(8,128)}, u32[]{:S(2)}) copy-start(f32[256,1024]{1,0:T(8,128)} %param.13) | copy-start | bytes 3145732
  30.1 8.4 %collective-permute-start.10 = (bf16[256,1024]{1,0:T(8,128)(2,1)S(1)}, bf16[256,1024]{1,0:T(8,128)(2,1)S(1)}, u32[]{:S(2)}, u32[]{:S(2)}) collective-permute-start(bf16[256,1024]{1,0:T(8,128)(2,1)S(1)} %get-tuple-element.149), channel_id=1, source_target_pairs={{0,8},{4,20},{8,0},{12,28},{16,24},{20,4},{24,16},{28,12},{1,9},{5... | collective-permute-start | bytes 1572872 | tf_op jit(solution)/shard_map/ppermute | solution.py:20
  31.3 12.8 %collective-permute-start.6 = (bf16[256,1024]{1,0:T(8,128)(2,1)S(1)}, bf16[256,1024]{1,0:T(8,128)(2,1)}, u32[]{:S(2)}, u32[]{:S(2)}) collective-permute-start(bf16[256,1024]{1,0:T(8,128)(2,1)S(1)} %get-tuple-element.149), channel_id=1, source_target_pairs={{0,1},{1,0},{2,3},{3,2},{4,5},{5,4},{6,7},{7,6},{8,9},{9,8},{10,11... | collective-permute-start | bytes 1572872 | tf_op jit(solution)/shard_map/ppermute | solution.py:138
  31.5 12.7 %collective-permute-start.7 = (bf16[256,1024]{1,0:T(8,128)(2,1)S(1)}, bf16[256,1024]{1,0:T(8,128)(2,1)}, u32[]{:S(2)}, u32[]{:S(2)}) collective-permute-start(bf16[256,1024]{1,0:T(8,128)(2,1)S(1)} %get-tuple-element.149), channel_id=1, source_target_pairs={{1,2},{2,1},{5,6},{6,5},{9,10},{10,9},{13,14},{14,13},{17,18},{18,... | collective-permute-start | bytes 1572872 | tf_op jit(solution)/shard_map/ppermute | solution.py:142
  38.6 25.8 %collective-permute-start.16 = (bf16[512,1024]{1,0:T(8,128)(2,1)S(1)}, bf16[512,1024]{1,0:T(8,128)(2,1)S(1)}, u32[]{:S(2)}, u32[]{:S(2)}) collective-permute-start(bf16[512,1024]{1,0:T(8,128)(2,1)S(1)} %pad_maximum_fusion.1.refs_0_), channel_id=1, source_target_pairs={{0,4},{4,0},{8,12},{12,8},{16,20},{20,16},{24,28},{28,24},{1,5},{5... | collective-permute-start | bytes 3145736 | tf_op jit(solution)/shard_map/ppermute | solution.py:20
  42.9 25.6 %collective-permute-start.11 = (bf16[512,1024]{1,0:T(8,128)(2,1)S(1)}, bf16[512,1024]{1,0:T(8,128)(2,1)S(1)}, u32[]{:S(2)}, u32[]{:S(2)}) collective-permute-start(bf16[512,1024]{1,0:T(8,128)(2,1)S(1)} %pad_maximum_fusion.1.refs_0_), channel_id=1, source_target_pairs={{0,16},{4,12},{8,24},{12,4},{16,0},{20,28},{24,8},{28,20},{1,17},{... | collective-permute-start | bytes 3145736 | tf_op jit(solution)/shard_map/ppermute | solution.py:20
  44.1 15.9 %collective-permute-start.13 = (bf16[256,1024]{1,0:T(8,128)(2,1)}, bf16[256,1024]{1,0:T(8,128)(2,1)}, u32[]{:S(2)}, u32[]{:S(2)}) collective-permute-start(bf16[256,1024]{1,0:T(8,128)(2,1)} %collective-permute-done.6), channel_id=1, source_target_pairs={{0,8},{4,20},{8,0},{12,28},{16,24},{20,4},{24,16},{28,12},{1,9},{5... | collective-permute-start | bytes 1572872 | tf_op jit(solution)/shard_map/ppermute | solution.py:20
  44.6 15.5 %collective-permute-start.14 = (bf16[256,1024]{1,0:T(8,128)(2,1)}, bf16[256,1024]{1,0:T(8,128)(2,1)}, u32[]{:S(2)}, u32[]{:S(2)}) collective-permute-start(bf16[256,1024]{1,0:T(8,128)(2,1)} %collective-permute-done.7), channel_id=1, source_target_pairs={{1,0},{2,3},{5,4},{6,7},{9,8},{10,11},{13,12},{14,15},{17,16},{18,... | collective-permute-start | bytes 1572872 | tf_op jit(solution)/shard_map/ppermute | solution.py:146
  47.0 21.6 %collective-permute-start.8 = (bf16[256,1024]{1,0:T(8,128)(2,1)}, bf16[256,1024]{1,0:T(8,128)(2,1)S(1)}, u32[]{:S(2)}, u32[]{:S(2)}) collective-permute-start(bf16[256,1024]{1,0:T(8,128)(2,1)} %collective-permute-done.6), channel_id=1, source_target_pairs={{1,2},{2,1},{5,6},{6,5},{9,10},{10,9},{13,14},{14,13},{17,18},{18,... | collective-permute-start | bytes 1572872 | tf_op jit(solution)/shard_map/ppermute | solution.py:142
  60.1 10.0 %copy-start.1 = (bf16[1024,1024]{1,0:T(8,128)(2,1)S(1)}, bf16[1024,1024]{1,0:T(8,128)(2,1)}, u32[]{:S(2)}) copy-start(bf16[1024,1024]{1,0:T(8,128)(2,1)} %get-tuple-element.115.normed) | copy-start | bytes 6291460
  61.4 11.3 %collective-permute-start.15 = (bf16[256,1024]{1,0:T(8,128)(2,1)S(1)}, bf16[256,1024]{1,0:T(8,128)(2,1)S(1)}, u32[]{:S(2)}, u32[]{:S(2)}) collective-permute-start(bf16[256,1024]{1,0:T(8,128)(2,1)S(1)} %broadcast_select_fusion), channel_id=1, source_target_pairs={{0,8},{4,20},{8,0},{12,28},{16,24},{20,4},{24,16},{28,12},{1,9},{5... | collective-permute-start | bytes 1572872 | tf_op jit(solution)/shard_map/ppermute | solution.py:20
  62.9 11.5 %collective-permute-start.20 = (bf16[256,1024]{1,0:T(8,128)(2,1)}, bf16[256,1024]{1,0:T(8,128)(2,1)S(1)}, u32[]{:S(2)}, u32[]{:S(2)}) collective-permute-start(bf16[256,1024]{1,0:T(8,128)(2,1)} %collective-permute-done.6), channel_id=1, source_target_pairs={{0,16},{4,12},{8,24},{12,4},{16,0},{20,28},{24,8},{28,20},{1,17},{... | collective-permute-start | bytes 1572872 | tf_op jit(solution)/shard_map/ppermute | solution.py:20
  64.4 20.3 %collective-permute-start.19 = (bf16[512,1024]{1,0:T(8,128)(2,1)S(1)}, bf16[512,1024]{1,0:T(8,128)(2,1)S(1)}, u32[]{:S(2)}, u32[]{:S(2)}) collective-permute-start(bf16[512,1024]{1,0:T(8,128)(2,1)S(1)} %pad_maximum_fusion.2.refs_2_), channel_id=1, source_target_pairs={{0,4},{4,0},{8,12},{12,8},{16,20},{20,16},{24,28},{28,24},{1,5},{5... | collective-permute-start | bytes 3145736 | tf_op jit(solution)/shard_map/ppermute | solution.py:20
  68.5 16.2 %collective-permute-start.18 = (bf16[512,1024]{1,0:T(8,128)(2,1)S(1)}, bf16[512,1024]{1,0:T(8,128)(2,1)S(1)}, u32[]{:S(2)}, u32[]{:S(2)}) collective-permute-start(bf16[512,1024]{1,0:T(8,128)(2,1)S(1)} %collective-permute-done.11.refs_0_), channel_id=1, source_target_pairs={{0,4},{4,0},{8,12},{12,8},{16,20},{20,16},{24,28},{28,24},{1,5},{5... | collective-permute-start | bytes 3145736 | tf_op jit(solution)/shard_map/ppermute | solution.py:20
  68.6 12.5 %collective-permute-start.9 = (bf16[256,1024]{1,0:T(8,128)(2,1)S(1)}, bf16[256,1024]{1,0:T(8,128)(2,1)S(1)}, u32[]{:S(2)}, u32[]{:S(2)}) collective-permute-start(bf16[256,1024]{1,0:T(8,128)(2,1)S(1)} %collective-permute-done.8), channel_id=1, source_target_pairs={{1,0},{2,3},{5,4},{6,7},{9,8},{10,11},{13,12},{14,15},{17,16},{18,... | collective-permute-start | bytes 1572872 | tf_op jit(solution)/shard_map/ppermute | solution.py:146
  70.1 14.7 %slice-start = ((s8[5242880]{0:T(1024)(128)(4,1)}), s8[4194304]{0:T(1024)(128)(4,1)S(1)}, s32[]{:S(2)}) async-start(s8[5242880]{0:T(1024)(128)(4,1)} %bitcast.123), calls=%async_computation | async-start | bytes 8388608
  70.1 14.6 %slice-start.1 = ((s8[5242880]{0:T(1024)(128)(4,1)}), s8[1048576]{0:T(1024)(128)(4,1)S(1)}, s32[]{:S(2)}) async-start(s8[5242880]{0:T(1024)(128)(4,1)} %bitcast.123), calls=%async_computation.1 | async-start | bytes 2097152
  72.8 22.4 %collective-permute-start.17 = (bf16[512,1024]{1,0:T(8,128)(2,1)S(1)}, bf16[512,1024]{1,0:T(8,128)(2,1)S(1)}, u32[]{:S(2)}, u32[]{:S(2)}) collective-permute-start(bf16[512,1024]{1,0:T(8,128)(2,1)S(1)} %pad_maximum_fusion.3.refs_0_), channel_id=1, source_target_pairs={{0,16},{4,12},{8,24},{12,4},{16,0},{20,28},{24,8},{28,20},{1,17},{... | collective-permute-start | bytes 3145736 | tf_op jit(solution)/shard_map/ppermute | solution.py:20
  74.4 8.1 %collective-permute-start.21 = (bf16[256,1024]{1,0:T(8,128)(2,1)S(1)}, bf16[256,1024]{1,0:T(8,128)(2,1)S(1)}, u32[]{:S(2)}, u32[]{:S(2)}) collective-permute-start(bf16[256,1024]{1,0:T(8,128)(2,1)S(1)} %collective-permute-done.20.refs_4_), channel_id=1, source_target_pairs={{0,4},{4,0},{8,12},{12,8},{16,20},{20,16},{24,28},{28,24},{1,5},{5... | collective-permute-start | bytes 1572872 | tf_op jit(solution)/shard_map/ppermute | solution.py:20
  81.1 14.1 %collective-permute-start.12 = (bf16[256,1024]{1,0:T(8,128)(2,1)S(1)}, bf16[256,1024]{1,0:T(8,128)(2,1)S(1)}, u32[]{:S(2)}, u32[]{:S(2)}) collective-permute-start(bf16[256,1024]{1,0:T(8,128)(2,1)S(1)} %broadcast_select_fusion.1), channel_id=1, source_target_pairs={{0,8},{4,20},{8,0},{12,28},{16,24},{20,4},{24,16},{28,12},{1,9},{5... | collective-permute-start | bytes 1572872 | tf_op jit(solution)/shard_map/ppermute | solution.py:20
  82.5 17.3 %collective-permute-start.25 = (bf16[256,1024]{1,0:T(8,128)(2,1)S(1)}, bf16[256,1024]{1,0:T(8,128)(2,1)S(1)}, u32[]{:S(2)}, u32[]{:S(2)}) collective-permute-start(bf16[256,1024]{1,0:T(8,128)(2,1)S(1)} %slice.19), channel_id=1, source_target_pairs={{0,1},{1,0},{2,3},{3,2},{4,5},{5,4},{6,7},{7,6},{8,9},{9,8},{10,11... | collective-permute-start | bytes 1572872 | tf_op jit(solution)/shard_map/ppermute | solution.py:138
  84.8 19.5 %slice-start.2 = ((s8[5242880]{0:T(1024)(128)(4,1)}), s8[4194304]{0:T(1024)(128)(4,1)S(1)}, s32[]{:S(2)}) async-start(s8[5242880]{0:T(1024)(128)(4,1)} %bitcast.125), calls=%async_computation.2 | async-start | bytes 8388608
  84.8 19.5 %slice-start.3 = ((s8[5242880]{0:T(1024)(128)(4,1)}), s8[1048576]{0:T(1024)(128)(4,1)S(1)}, s32[]{:S(2)}) async-start(s8[5242880]{0:T(1024)(128)(4,1)} %bitcast.125), calls=%async_computation.3 | async-start | bytes 2097152
  95.2 8.7 %collective-permute-start.24 = (bf16[512,1024]{1,0:T(8,128)(2,1)S(1)}, bf16[512,1024]{1,0:T(8,128)(2,1)S(1)}, u32[]{:S(2)}, u32[]{:S(2)}) collective-permute-start(bf16[512,1024]{1,0:T(8,128)(2,1)S(1)} %collective-permute-done.17.refs_2_), channel_id=1, source_target_pairs={{0,4},{4,0},{8,12},{12,8},{16,20},{20,16},{24,28},{28,24},{1,5},{5... | collective-permute-start | bytes 3145736 | tf_op jit(solution)/shard_map/ppermute | solution.py:20
  99.4 4.5 %collective-permute-start.23 = (bf16[512,1024]{1,0:T(8,128)(2,1)S(1)}, bf16[512,1024]{1,0:T(8,128)(2,1)S(1)}, u32[]{:S(2)}, u32[]{:S(2)}) collective-permute-start(bf16[512,1024]{1,0:T(8,128)(2,1)S(1)} %pad_maximum_fusion.3.refs_0_), channel_id=1, source_target_pairs={{0,4},{4,0},{8,12},{12,8},{16,20},{20,16},{24,28},{28,24},{1,5},{5... | collective-permute-start | bytes 3145736 | tf_op jit(solution)/shard_map/ppermute | solution.py:20
  99.5 14.0 %collective-permute-start.22 = (bf16[512,1024]{1,0:T(8,128)(2,1)S(1)}, bf16[512,1024]{1,0:T(8,128)(2,1)S(1)}, u32[]{:S(2)}, u32[]{:S(2)}) collective-permute-start(bf16[512,1024]{1,0:T(8,128)(2,1)S(1)} %constant_dynamic-update-slice_fusion.refs_0_), channel_id=1, source_target_pairs={{0,16},{4,12},{8,24},{12,4},{16,0},{20,28},{24,8},{28,20},{1,17},{... | collective-permute-start | bytes 3145736 | tf_op jit(solution)/shard_map/ppermute | solution.py:20
  99.8 4.1 %collective-permute-start.26 = (bf16[256,1024]{1,0:T(8,128)(2,1)S(1)}, bf16[256,1024]{1,0:T(8,128)(2,1)S(1)}, u32[]{:S(2)}, u32[]{:S(2)}) collective-permute-start(bf16[256,1024]{1,0:T(8,128)(2,1)S(1)} %collective-permute-done.25.refs_4_), channel_id=1, source_target_pairs={{0,4},{4,0},{8,12},{12,8},{16,20},{20,16},{24,28},{28,24},{1,5},{5... | collective-permute-start | bytes 1572872 | tf_op jit(solution)/shard_map/ppermute | solution.py:20
  103.9 10.9 %collective-permute-start.28 = (bf16[512,1024]{1,0:T(8,128)(2,1)S(1)}, bf16[512,1024]{1,0:T(8,128)(2,1)S(1)}, u32[]{:S(2)}, u32[]{:S(2)}) collective-permute-start(bf16[512,1024]{1,0:T(8,128)(2,1)S(1)} %constant_dynamic-update-slice_fusion.refs_0_), channel_id=1, source_target_pairs={{0,4},{4,0},{8,12},{12,8},{16,20},{20,16},{24,28},{28,24},{1,5},{5... | collective-permute-start | bytes 3145736 | tf_op jit(solution)/shard_map/ppermute | solution.py:20
  104.3 10.5 %copy-start.2 = (bf16[1024,1024]{1,0:T(8,128)(2,1)S(1)}, bf16[1024,1024]{1,0:T(8,128)(2,1)}, u32[]{:S(2)}) copy-start(bf16[1024,1024]{1,0:T(8,128)(2,1)} %get-tuple-element.144.normed) | copy-start | bytes 6291460
  113.5 3.9 %collective-permute-start.27 = (bf16[512,1024]{1,0:T(8,128)(2,1)S(1)}, bf16[512,1024]{1,0:T(8,128)(2,1)S(1)}, u32[]{:S(2)}, u32[]{:S(2)}) collective-permute-start(bf16[512,1024]{1,0:T(8,128)(2,1)S(1)} %collective-permute-done.22.refs_0_), channel_id=1, source_target_pairs={{0,4},{4,0},{8,12},{12,8},{16,20},{20,16},{24,28},{28,24},{1,5},{5... | collective-permute-start | bytes 3145736 | tf_op jit(solution)/shard_map/ppermute | solution.py:20
  114.8 2.6 %copy-start = (bf16[1024,1024]{1,0:T(8,128)(2,1)S(1)}, bf16[1024,1024]{1,0:T(8,128)(2,1)}, u32[]{:S(2)}) copy-start(bf16[1024,1024]{1,0:T(8,128)(2,1)} %get-tuple-element.110.normed) | copy-start | bytes 6291460

commit v6 on v5

--- a/solution.py
+++ b/solution.py
@@ -238,7 +238,7 @@
 
     order, pair = together(order, pair)
     normed = normalize_in_order(tokens, norm_gain, order, rows, parts, 4, 4, normed)
-    beside, near_out, normed[-1] = together(beside, near_out, normed[-1])
+    near_out, normed[-1] = together(near_out, normed[-1])
     near = jnp.where(outer, near_out, near_in)
     half1 = jnp.concatenate([pair, beside], 0)
     beside = swap_first(near)

time: 121 us -> 121 us (level)
  no operation moved by 1% of the time
where the time goes in v6:
time: 121 us
  starting transfers between devices  46.5 us (38%)
  Pallas kernels  39 us (32%)
  waiting for transfers between devices  20.3 us (17%)
  other arithmetic  9.54 us (8%)
  local copies, waits for them, and re-layouts  4.29 us (4%)
  between operations  1.22 us (1%)
    ppermute x23, starting transfers between devices, flip(): return lax.ppermute(value, 'rep', perm)  31.1 us
    pallas_call x5, Pallas kernels, project(): pl.pallas_call(functools.partial(project_kernel, depths), grid=(rows // t...  20.1 us
    pallas_call x3, Pallas kernels, normalize_in_order(): pl.pallas_call(functools.partial(normalize_kernel, width=width, parts=len...  18.9 us
    ppermute x23, waiting for transfers between devices, flip(): return lax.ppermute(value, 'rep', perm)  18.2 us
    ppermute x2, starting transfers between devices, inwards(): return lax.ppermute(value, 'fsdp', [(1, 2), (2, 1)])  8.64 us
    ppermute x2, starting transfers between devices, outwards(): return lax.ppermute(value, 'fsdp', [(1, 0), (2, 3)])  4.32 us
    another operation x2, other arithmetic  2.72 us
    reshape x2, local copies, waits for them, and re-layouts, on_block(): theirs = theirs.reshape(4, half_rows, cols)  2.6 us
  transfers between devices with their start and end apart: 29, of which 9 were waited for; matrix products, arithmetic and copies ran while one was open for 8% of the time, Pallas kernels for 29%

profile of v6, /device:TPU:9, one launch (start us, length us, event | category | flops | bytes accessed | tf_op | source)
XLA Modules:
  0.0 120.9 jit_solution(1964388165000497305)
XLA Ops:
  0.7 1.3 %dynamic-slice_bitcast_fusion.1 = bf16[4,128,1024]{2,1,0:T(8,128)(2,1)S(1)} fusion(bf16[4,2,2,128,1024]{4,3,2,1,0:T(8,128)(2,1)} %bitcast.127, s32[]{:T(128)S(6)} %select_n.62), kind=kLoop, calls=%fused_computation.7 | loop fusion | bytes 2097156 | tf_op jit(solution)/shard_map/reshape | solution.py:197
  2.0 0.7 collective-permute-start
  2.7 1.3 %dynamic-slice_bitcast_fusion = bf16[4,128,1024]{2,1,0:T(8,128)(2,1)S(1)} fusion(bf16[4,2,2,128,1024]{4,3,2,1,0:T(8,128)(2,1)} %bitcast.128, s32[]{:T(128)S(6)} %select_n.63), kind=kLoop, calls=%fused_computation.6 | loop fusion | bytes 2097156 | tf_op jit(solution)/shard_map/reshape | solution.py:197
  4.7 0.4 collective-permute-done
  5.0 1.3 %fusion.11 = (bf16[128,1024]{1,0:T(8,128)(2,1)S(1)}, bf16[128,1024]{1,0:T(8,128)(2,1)S(1)}) fusion(bf16[4,128,1024]{2,1,0:T(8,128)(2,1)S(1)} %collective-permute-done, s32[]{:T(128)S(6)} %select_n.130, f32[128]{0:T(128)S(1)} %get-tuple-element.182, bf16[4,2,2,128,1024]{4,3,2,1,0:T(8,128)(2,1)} %bitcast.129, s32[]{:T(128)S(6)} %select_n.131, ...), kind=kLoop, calls=%fused_computation.36 | loop fusion | flops 1572864 | bytes 1574924 | tf_op jit(solution)/shard_map/convert.18
  6.3 1.3 %collective-permute-start.2 = (bf16[256,1024]{1,0:T(8,128)(2,1)S(1)}, bf16[256,1024]{1,0:T(8,128)(2,1)S(1)}, u32[]{:S(2)}, u32[]{:S(2)}) collective-permute-start(bf16[256,1024]{1,0:T(8,128)(2,1)S(1)} %pad_maximum_fusion.4), channel_id=1, source_target_pairs={{0,8},{4,20},{8,0},{12,28},{16,24},{20,4},{24,16},{28,12},{1,9},{5... | collective-permute-start | bytes 1572872 | tf_op jit(solution)/shard_map/ppermute | solution.py:20
  7.7 1.4 %fusion.7 = (bf16[128,1024]{1,0:T(8,128)(2,1)S(1)}, bf16[128,1024]{1,0:T(8,128)(2,1)S(1)}) fusion(bf16[4,128,1024]{2,1,0:T(8,128)(2,1)} %collective-permute-done.1, s32[]{:T(128)S(6)} %select_n.130, f32[128]{0:T(128)S(1)} %get-tuple-element.184, bf16[4,2,2,128,1024]{4,3,2,1,0:T(8,128)(2,1)} %bitcast.130, s32[]{:T(128)S(6)} %select_n.131, ...), kind=kLoop, calls=%fused_computation.28 | loop fusion | flops 1572864 | bytes 1574924 | tf_op jit(solution)/shard_map/convert.16
  9.1 0.5 collective-permute-start.3
  9.7 5.1 %normalize_in_order.3 = (bf16[1024,1024]{1,0:T(8,128)(2,1)}, bf16[1024,2560]{1,0:T(8,128)(2,1)}, bf16[1024,2560]{1,0:T(8,128)(2,1)}, bf16[1024,1024]{1,0:T(8,128...) custom-call(s32[32]{0:T(128)S(1)} %stack.131.order, bf16[1024,8192]{1,0:T(8,128)(2,1)} %tokens.5, ...), custom_call_target="tpu_custom_call" | custom-call | flops 12582912 | bytes 8388608 | tf_op jit(solution)/shard_map/normalize_in_order/pallas_call | solution.py:68
  14.7 1.8 %fusion = (f32[128,1024]{1,0:T(8,128)S(1)}, f32[128,1024]{1,0:T(8,128)S(1)}, f32[128,1024]{1,0:T(8,128)S(1)}, f32[128,1024]{1,0:T(8,128)S(1)}) fusion(bf16[4,128,1024]{2,1,0:T(8,128)(2,1)} %collective-permute-done.1, s32[]{:T(128)S(6)} %select_n.138, f32[128]{0:T(128)S(1)} %get-tuple-element.189, bf16[4,2,2,128,1024]{4,3,2,1,0:T(8,128)(2,1)} %bitcast.131, ...), kind=kLoop, calls=%fused_computation.11 | loop fusion | flops 2621440 | bytes 4198412 | tf_op jit(solution)/shard_map/add | solution.py:188
  16.7 1.3 %collective-permute-start.4 = (bf16[128,1024]{1,0:T(8,128)(2,1)S(1)}, bf16[128,1024]{1,0:T(8,128)(2,1)S(1)}, u32[]{:S(2)}, u32[]{:S(2)}) collective-permute-start(bf16[128,1024]{1,0:T(8,128)(2,1)S(1)} %get-tuple-element.163), channel_id=1, source_target_pairs={{0,16},{4,12},{8,24},{12,4},{16,0},{20,28},{24,8},{28,20},{1,17},{... | collective-permute-start | bytes 786440 | tf_op jit(solution)/shard_map/ppermute | solution.py:20
  17.9 2.4 %collective-permute-done.3 = bf16[256,1024]{1,0:T(8,128)(2,1)S(1)} collective-permute-done((bf16[256,1024]{1,0:T(8,128)(2,1)S(1)}, bf16[256,1024]{1,0:T(8,128)(2,1)S(1)}, u32[]{:S(2)}, u32[]{:S(2)}) %collective-permute-start.3) | collective-permute-done | bytes 524320 | tf_op jit(solution)/shard_map/ppermute | solution.py:20
  20.5 1.3 %collective-permute-start.5 = (bf16[128,1024]{1,0:T(8,128)(2,1)S(1)}, bf16[128,1024]{1,0:T(8,128)(2,1)S(1)}, u32[]{:S(2)}, u32[]{:S(2)}) collective-permute-start(bf16[128,1024]{1,0:T(8,128)(2,1)S(1)} %get-tuple-element.161), channel_id=1, source_target_pairs={{0,16},{4,12},{8,24},{12,4},{16,0},{20,28},{24,8},{28,20},{1,17},{... | collective-permute-start | bytes 786440 | tf_op jit(solution)/shard_map/ppermute | solution.py:20
  21.8 5.1 %normalize_in_order.4 = (bf16[1024,1024]{1,0:T(8,128)(2,1)}, bf16[1024,2560]{1,0:T(8,128)(2,1)}, bf16[1024,2560]{1,0:T(8,128)(2,1)}, bf16[1024,1024]{1,0:T(8,128...) custom-call(s32[32]{0:T(128)S(1)} %stack.131.order, ...), custom_call_target="tpu_custom_call", output_to_operand_aliasing={{0}: (3, {}), {1}: (4, {}), {2}: (5, {}), {3}: (6, {}), {4}... | custom-call | flops 12582912 | bytes 8388608 | tf_op jit(solution)/shard_map/normalize_in_order/pallas_call | solution.py:68
  27.0 1.0 copy-done.3
  28.1 0.3 copy-done.4
  28.4 1.7 %fusion.30 = (bf16[256,1024]{1,0:T(8,128)(2,1)S(1)}, f32[256,1024]{1,0:T(8,128)}, f32[256,1024]{1,0:T(8,128)}) fusion(f32[256,1024]{1,0:T(8,128)S(1)} %copy-done.3, f32[128,1024]{1,0:T(8,128)S(1)} %convert_add_fusion, f32[128,1024]{1,0:T(8,128)S(1)} %convert_add_fusion.1, f32[256,1024]{1,0:T(8,128)S(1)} %copy-done.4), kind=kLoop, calls=%fused_computation.89 | loop fusion | flops 2097152 | bytes 5767168 | tf_op jit(solution)/shard_map/convert_element_type | solution.py:226
  30.1 1.2 %collective-permute-start.10 = (bf16[256,1024]{1,0:T(8,128)(2,1)S(1)}, bf16[256,1024]{1,0:T(8,128)(2,1)S(1)}, u32[]{:S(2)}, u32[]{:S(2)}) collective-permute-start(bf16[256,1024]{1,0:T(8,128)(2,1)S(1)} %get-tuple-element.147), channel_id=1, source_target_pairs={{0,8},{4,20},{8,0},{12,28},{16,24},{20,4},{24,16},{28,12},{1,9},{5... | collective-permute-start | bytes 1572872 | tf_op jit(solution)/shard_map/ppermute | solution.py:20
  31.5 4.3 %collective-permute-start.7 = (bf16[256,1024]{1,0:T(8,128)(2,1)S(1)}, bf16[256,1024]{1,0:T(8,128)(2,1)}, u32[]{:S(2)}, u32[]{:S(2)}) collective-permute-start(bf16[256,1024]{1,0:T(8,128)(2,1)S(1)} %get-tuple-element.147), channel_id=1, source_target_pairs={{1,2},{2,1},{5,6},{6,5},{9,10},{10,9},{13,14},{14,13},{17,18},{18,... | collective-permute-start | bytes 1572872 | tf_op jit(solution)/shard_map/ppermute | solution.py:142
  35.8 2.7 %collective-permute-done.10 = bf16[256,1024]{1,0:T(8,128)(2,1)S(1)} collective-permute-done((bf16[256,1024]{1,0:T(8,128)(2,1)S(1)}, bf16[256,1024]{1,0:T(8,128)(2,1)S(1)}, u32[]{:S(2)}, u32[]{:S(2)}) %collective-permute-start.10) | collective-permute-done | bytes 524320 | tf_op jit(solution)/shard_map/ppermute | solution.py:20
  38.6 4.3 %collective-permute-start.16 = (bf16[512,1024]{1,0:T(8,128)(2,1)S(1)}, bf16[512,1024]{1,0:T(8,128)(2,1)S(1)}, u32[]{:S(2)}, u32[]{:S(2)}) collective-permute-start(bf16[512,1024]{1,0:T(8,128)(2,1)S(1)} %pad_maximum_fusion.1.refs_0_), channel_id=1, source_target_pairs={{0,4},{4,0},{8,12},{12,8},{16,20},{20,16},{24,28},{28,24},{1,5},{5... | collective-permute-start | bytes 3145736 | tf_op jit(solution)/shard_map/ppermute | solution.py:20
  42.9 1.2 collective-permute-start.11
  44.1 2.8 %collective-permute-start.13 = (bf16[256,1024]{1,0:T(8,128)(2,1)}, bf16[256,1024]{1,0:T(8,128)(2,1)}, u32[]{:S(2)}, u32[]{:S(2)}) collective-permute-start(bf16[256,1024]{1,0:T(8,128)(2,1)} %collective-permute-done.7), channel_id=1, source_target_pairs={{1,0},{2,3},{5,4},{6,7},{9,8},{10,11},{13,12},{14,15},{17,16},{18,... | collective-permute-start | bytes 1572872 | tf_op jit(solution)/shard_map/ppermute | solution.py:146
  47.0 4.3 %collective-permute-start.8 = (bf16[256,1024]{1,0:T(8,128)(2,1)}, bf16[256,1024]{1,0:T(8,128)(2,1)S(1)}, u32[]{:S(2)}, u32[]{:S(2)}) collective-permute-start(bf16[256,1024]{1,0:T(8,128)(2,1)} %collective-permute-done.6), channel_id=1, source_target_pairs={{1,2},{2,1},{5,6},{6,5},{9,10},{10,9},{13,14},{14,13},{17,18},{18,... | collective-permute-start | bytes 1572872 | tf_op jit(solution)/shard_map/ppermute | solution.py:142
  51.3 8.8 %normalize_in_order.5 = (bf16[1024,1024]{1,0:T(8,128)(2,1)}, bf16[1024,2560]{1,0:T(8,128)(2,1)}, bf16[1024,2560]{1,0:T(8,128)(2,1)}, bf16[1024,1024]{1,0:T(8,128...) custom-call(s32[32]{0:T(128)S(1)} %stack.131.order, ...), custom_call_target="tpu_custom_call", output_to_operand_aliasing={{0}: (3, {}), {1}: (4, {}), {2}: (5, {}), {3}: (6, {}), {4}... | custom-call | flops 25165824 | bytes 16777216 | tf_op jit(solution)/shard_map/normalize_in_order/pallas_call | solution.py:68
  60.1 1.3 %broadcast_select_fusion = bf16[256,1024]{1,0:T(8,128)(2,1)S(1)} fusion(bf16[256,1024]{1,0:T(8,128)(2,1)} %collective-permute-done.13, bf16[256,1024]{1,0:T(8,128)(2,1)} %collective-permute-done.7, pred[]{:T(512)S(6)} %or.3), kind=kLoop, calls=%fused_computation.44 | loop fusion | flops 262144 | bytes 1572865 | tf_op jit(solution)/shard_map/jit(_where)/select_n | solution.py:242
  61.4 1.5 %collective-permute-start.14 = (bf16[256,1024]{1,0:T(8,128)(2,1)S(1)}, bf16[256,1024]{1,0:T(8,128)(2,1)S(1)}, u32[]{:S(2)}, u32[]{:S(2)}) collective-permute-start(bf16[256,1024]{1,0:T(8,128)(2,1)S(1)} %broadcast_select_fusion), channel_id=1, source_target_pairs={{0,8},{4,20},{8,0},{12,28},{16,24},{20,4},{24,16},{28,12},{1,9},{5... | collective-permute-start | bytes 1572872 | tf_op jit(solution)/shard_map/ppermute | solution.py:20
  63.2 1.3 %pad_maximum_fusion.2.refs_2_ = bf16[512,1024]{1,0:T(8,128)(2,1)S(1)} fusion(bf16[256,1024]{1,0:T(8,128)(2,1)} %collective-permute-done.15, bf16[256,1024]{1,0:T(8,128)(2,1)} %collective-permute-done.6), kind=kLoop, calls=%fused_computation.2 | loop fusion | flops 2097152 | bytes 2097152 | tf_op jit(solution)/shard_map/concatenate | solution.py:243
  64.4 4.1 %collective-permute-start.18 = (bf16[512,1024]{1,0:T(8,128)(2,1)S(1)}, bf16[512,1024]{1,0:T(8,128)(2,1)S(1)}, u32[]{:S(2)}, u32[]{:S(2)}) collective-permute-start(bf16[512,1024]{1,0:T(8,128)(2,1)S(1)} %collective-permute-done.11.refs_0_), channel_id=1, source_target_pairs={{0,4},{4,0},{8,12},{12,8},{16,20},{20,16},{24,28},{28,24},{1,5},{5... | collective-permute-start | bytes 3145736 | tf_op jit(solution)/shard_map/ppermute | solution.py:20
  68.6 1.5 %collective-permute-start.9 = (bf16[256,1024]{1,0:T(8,128)(2,1)S(1)}, bf16[256,1024]{1,0:T(8,128)(2,1)S(1)}, u32[]{:S(2)}, u32[]{:S(2)}) collective-permute-start(bf16[256,1024]{1,0:T(8,128)(2,1)S(1)} %collective-permute-done.8), channel_id=1, source_target_pairs={{1,0},{2,3},{5,4},{6,7},{9,8},{10,11},{13,12},{14,15},{17,16},{18,... | collective-permute-start | bytes 1572872 | tf_op jit(solution)/shard_map/ppermute | solution.py:146
  70.2 2.5 %project.5.refs_6_ = f32[1024,1024]{1,0:T(8,128)S(1)} custom-call(bf16[1024,1024]{1,0:T(8,128)(2,1)S(1)} %copy-done.1, bf16[512,1024]{1,0:T(8,128)(2,1)S(1)} %pad_maximum_fusion.1.refs_0_, bf16[512,1024]{1,0:T(8,128)(2,1)S(1)} %collective-permute-done.16.refs_1_, f32[8,128]{1,0:T(8,128)S(1)} %get-tuple-element.118.refs_2_), custom_call_target="tpu_custom_call" | custom-call | flops 2147483648 | bytes 12582912 | tf_op jit(solution)/shard_map/project/pallas_call | solution.py:115
  72.8 0.7 collective-permute-start.17
  73.5 0.9 collective-permute-done.20.refs_4_
  74.4 4.6 %collective-permute-start.21 = (bf16[256,1024]{1,0:T(8,128)(2,1)S(1)}, bf16[256,1024]{1,0:T(8,128)(2,1)S(1)}, u32[]{:S(2)}, u32[]{:S(2)}) collective-permute-start(bf16[256,1024]{1,0:T(8,128)(2,1)S(1)} %collective-permute-done.20.refs_4_), channel_id=1, source_target_pairs={{0,4},{4,0},{8,12},{12,8},{16,20},{20,16},{24,28},{28,24},{1,5},{5... | collective-permute-start | bytes 1572872 | tf_op jit(solution)/shard_map/ppermute | solution.py:20
  79.1 2.0 %collective-permute-done.9 = bf16[256,1024]{1,0:T(8,128)(2,1)S(1)} collective-permute-done((bf16[256,1024]{1,0:T(8,128)(2,1)S(1)}, bf16[256,1024]{1,0:T(8,128)(2,1)S(1)}, u32[]{:S(2)}, u32[]{:S(2)}) %collective-permute-start.9) | collective-permute-done | bytes 524320 | tf_op jit(solution)/shard_map/ppermute | solution.py:146
  81.1 1.3 %collective-permute-start.12 = (bf16[256,1024]{1,0:T(8,128)(2,1)S(1)}, bf16[256,1024]{1,0:T(8,128)(2,1)S(1)}, u32[]{:S(2)}, u32[]{:S(2)}) collective-permute-start(bf16[256,1024]{1,0:T(8,128)(2,1)S(1)} %broadcast_select_fusion.1), channel_id=1, source_target_pairs={{0,8},{4,20},{8,0},{12,28},{16,24},{20,4},{24,16},{28,12},{1,9},{5... | collective-permute-start | bytes 1572872 | tf_op jit(solution)/shard_map/ppermute | solution.py:20
  82.5 2.3 %collective-permute-start.25 = (bf16[256,1024]{1,0:T(8,128)(2,1)S(1)}, bf16[256,1024]{1,0:T(8,128)(2,1)S(1)}, u32[]{:S(2)}, u32[]{:S(2)}) collective-permute-start(bf16[256,1024]{1,0:T(8,128)(2,1)S(1)} %slice.19), channel_id=1, source_target_pairs={{0,1},{1,0},{2,3},{3,2},{4,5},{5,4},{6,7},{7,6},{8,9},{9,8},{10,11... | collective-permute-start | bytes 1572872 | tf_op jit(solution)/shard_map/ppermute | solution.py:138
  84.8 5.8 %project.6.refs_6_ = f32[1024,1024]{1,0:T(8,128)S(1)} custom-call(bf16[1024,2560]{1,0:T(8,128)(2,1)S(1)} %bitcast.124, bf16[512,1024]{1,0:T(8,128)(2,1)S(1)} %collective-permute-done.11.refs_0_, bf16[512,1024]{1,0:T(8,128)(2,1)S(1)} %collective-permute-done.18.refs_1_, bf16[512,1024]{1,0:T(8,128)(2,1)S(1)} %pad_maximum_fusion.2.refs_2_, ...), custom_call_target="tpu_custom_call" | custom-call | flops 5368709120 | bytes 18874368 | tf_op jit(solution)/shard_map/project/pallas_call | solution.py:115
  90.6 4.6 %collective-permute-done.12 = bf16[256,1024]{1,0:T(8,128)(2,1)S(1)} collective-permute-done((bf16[256,1024]{1,0:T(8,128)(2,1)S(1)}, bf16[256,1024]{1,0:T(8,128)(2,1)S(1)}, u32[]{:S(2)}, u32[]{:S(2)}) %collective-permute-start.12) | collective-permute-done | bytes 524320 | tf_op jit(solution)/shard_map/ppermute | solution.py:20
  95.2 4.2 %collective-permute-start.23 = (bf16[512,1024]{1,0:T(8,128)(2,1)S(1)}, bf16[512,1024]{1,0:T(8,128)(2,1)S(1)}, u32[]{:S(2)}, u32[]{:S(2)}) collective-permute-start(bf16[512,1024]{1,0:T(8,128)(2,1)S(1)} %pad_maximum_fusion.3.refs_0_), channel_id=1, source_target_pairs={{0,4},{4,0},{8,12},{12,8},{16,20},{20,16},{24,28},{28,24},{1,5},{5... | collective-permute-start | bytes 3145736 | tf_op jit(solution)/shard_map/ppermute | solution.py:20
  99.6 0.6 collective-permute-start.26
  100.1 3.8 %collective-permute-done.26.refs_5_ = bf16[256,1024]{1,0:T(8,128)(2,1)S(1)} collective-permute-done((bf16[256,1024]{1,0:T(8,128)(2,1)S(1)}, bf16[256,1024]{1,0:T(8,128)(2,1)S(1)}, u32[]{:S(2)}, u32[]{:S(2)}) %collective-permute-start.26) | collective-permute-done | bytes 524320 | tf_op jit(solution)/shard_map/ppermute | solution.py:20
  103.9 0.4 collective-permute-start.28
  104.3 5.8 %project.7.refs_2_ = f32[1024,1024]{1,0:T(8,128)S(1)} custom-call(bf16[1024,2560]{1,0:T(8,128)(2,1)S(1)} %bitcast.126, bf16[512,1024]{1,0:T(8,128)(2,1)S(1)} %pad_maximum_fusion.3.refs_0_, bf16[512,1024]{1,0:T(8,128)(2,1)S(1)} %collective-permute-done.23.refs_1_, bf16[512,1024]{1,0:T(8,128)(2,1)S(1)} %collective-permute-done.17.refs_2_, ...), custom_call_target="tpu_custom_call" | custom-call | flops 5368709120 | bytes 18874368 | tf_op jit(solution)/shard_map/project/pallas_call | solution.py:115
  110.1 3.4 %collective-permute-done.22.refs_0_ = bf16[512,1024]{1,0:T(8,128)(2,1)S(1)} collective-permute-done((bf16[512,1024]{1,0:T(8,128)(2,1)S(1)}, bf16[512,1024]{1,0:T(8,128)(2,1)S(1)}, u32[]{:S(2)}, u32[]{:S(2)}) %collective-permute-start.22) | collective-permute-done | bytes 1048608 | tf_op jit(solution)/shard_map/ppermute | solution.py:20
  113.5 1.4 %collective-permute-start.27 = (bf16[512,1024]{1,0:T(8,128)(2,1)S(1)}, bf16[512,1024]{1,0:T(8,128)(2,1)S(1)}, u32[]{:S(2)}, u32[]{:S(2)}) collective-permute-start(bf16[512,1024]{1,0:T(8,128)(2,1)S(1)} %collective-permute-done.22.refs_0_), channel_id=1, source_target_pairs={{0,4},{4,0},{8,12},{12,8},{16,20},{20,16},{24,28},{28,24},{1,5},{5... | collective-permute-start | bytes 3145736 | tf_op jit(solution)/shard_map/ppermute | solution.py:20
  114.9 2.5 %project.8.refs_2_ = f32[1024,1024]{1,0:T(8,128)S(1)} custom-call(bf16[1024,1024]{1,0:T(8,128)(2,1)S(1)} %copy-done.2, bf16[512,1024]{1,0:T(8,128)(2,1)S(1)} %constant_dynamic-update-slice_fusion.refs_0_, bf16[512,1024]{1,0:T(8,128)(2,1)S(1)} %collective-permute-done.28.refs_1_, f32[1024,1024]{1,0:T(8,128)S(1)} %project.7.refs_2_), custom_call_target="tpu_custom_call" | custom-call | flops 2147483648 | bytes 12582912 | tf_op jit(solution)/shard_map/project/pallas_call | solution.py:115
  117.4 3.5 %project.9 = bf16[1024,1024]{1,0:T(8,128)(2,1)} custom-call(bf16[1024,1024]{1,0:T(8,128)(2,1)S(1)} %copy-done, bf16[512,1024]{1,0:T(8,128)(2,1)S(1)} %collective-permute-done.22.refs_0_, bf16[512,1024]{1,0:T(8,128)(2,1)S(1)} %collective-permute-done.27.refs_1_, f32[1024,1024]{1,0:T(8,128)S(1)} %project.8.refs_2_), custom_call_target="tpu_custom_call" | custom-call | flops 2147483648 | bytes 12582912 | tf_op jit(solution)/shard_map/project/pallas_call | solution.py:115
  (71 shorter events, 2.0 us)
Async XLA Ops:
  0.6 3.6 %copy-start.5 = (bf16[8192]{0:T(1024)(128)(2,1)S(1)}, bf16[8192]{0:T(1024)(128)(2,1)}, u32[]{:S(2)}) copy-start(bf16[8192]{0:T(1024)(128)(2,1)} %param.8) | copy-start | bytes 49156
  0.6 3.8 %copy-start.6 = (s32[8,16]{1,0:T(8,128)S(1)}, s32[8,16]{1,0:T(8,128)}, u32[]{:S(2)}) copy-start(s32[8,16]{1,0:T(8,128)} %param.10) | copy-start | bytes 1540
  0.7 3.8 %copy-start.7 = (s32[2048]{0:T(1024)S(1)}, s32[2048]{0:T(1024)}, u32[]{:S(2)}) copy-start(s32[2048]{0:T(1024)} %param.11) | copy-start | bytes 24580
  2.0 3.0 %collective-permute-start = (bf16[4,128,1024]{2,1,0:T(8,128)(2,1)S(1)}, bf16[4,128,1024]{2,1,0:T(8,128)(2,1)S(1)}, u32[]{:S(2)}, u32[]{:S(2)}) collective-permute-start(bf16[4,128,1024]{2,1,0:T(8,128)(2,1)S(1)} %dynamic-slice_bitcast_fusion.1), channel_id=1, source_target_pairs={{0,4},{4,0},{8,12},{12,8},{16,20},{20,16},{24,28},{28,24},{1,5},{5... | collective-permute-start | bytes 3145736 | tf_op jit(solution)/shard_map/ppermute | solution.py:20
  4.0 3.6 %collective-permute-start.1 = (bf16[4,128,1024]{2,1,0:T(8,128)(2,1)S(1)}, bf16[4,128,1024]{2,1,0:T(8,128)(2,1)}, u32[]{:S(2)}, u32[]{:S(2)}) collective-permute-start(bf16[4,128,1024]{2,1,0:T(8,128)(2,1)S(1)} %dynamic-slice_bitcast_fusion), channel_id=1, source_target_pairs={{0,4},{4,0},{8,12},{12,8},{16,20},{20,16},{24,28},{28,24},{1,5},{5... | collective-permute-start | bytes 3145736 | tf_op jit(solution)/shard_map/ppermute | solution.py:20
  6.3 10.1 %collective-permute-start.2 = (bf16[256,1024]{1,0:T(8,128)(2,1)S(1)}, bf16[256,1024]{1,0:T(8,128)(2,1)S(1)}, u32[]{:S(2)}, u32[]{:S(2)}) collective-permute-start(bf16[256,1024]{1,0:T(8,128)(2,1)S(1)} %pad_maximum_fusion.4), channel_id=1, source_target_pairs={{0,8},{4,20},{8,0},{12,28},{16,24},{20,4},{24,16},{28,12},{1,9},{5... | collective-permute-start | bytes 1572872 | tf_op jit(solution)/shard_map/ppermute | solution.py:20
  9.1 11.2 %collective-permute-start.3 = (bf16[256,1024]{1,0:T(8,128)(2,1)S(1)}, bf16[256,1024]{1,0:T(8,128)(2,1)S(1)}, u32[]{:S(2)}, u32[]{:S(2)}) collective-permute-start(bf16[256,1024]{1,0:T(8,128)(2,1)S(1)} %pad_maximum_fusion.5), channel_id=1, source_target_pairs={{0,8},{4,20},{8,0},{12,28},{16,24},{20,4},{24,16},{28,12},{1,9},{5... | collective-permute-start | bytes 1572872 | tf_op jit(solution)/shard_map/ppermute | solution.py:20
  16.7 10.2 %collective-permute-start.4 = (bf16[128,1024]{1,0:T(8,128)(2,1)S(1)}, bf16[128,1024]{1,0:T(8,128)(2,1)S(1)}, u32[]{:S(2)}, u32[]{:S(2)}) collective-permute-start(bf16[128,1024]{1,0:T(8,128)(2,1)S(1)} %get-tuple-element.163), channel_id=1, source_target_pairs={{0,16},{4,12},{8,24},{12,4},{16,0},{20,28},{24,8},{28,20},{1,17},{... | collective-permute-start | bytes 786440 | tf_op jit(solution)/shard_map/ppermute | solution.py:20
  20.5 6.4 %collective-permute-start.5 = (bf16[128,1024]{1,0:T(8,128)(2,1)S(1)}, bf16[128,1024]{1,0:T(8,128)(2,1)S(1)}, u32[]{:S(2)}, u32[]{:S(2)}) collective-permute-start(bf16[128,1024]{1,0:T(8,128)(2,1)S(1)} %get-tuple-element.161), channel_id=1, source_target_pairs={{0,16},{4,12},{8,24},{12,4},{16,0},{20,28},{24,8},{28,20},{1,17},{... | collective-permute-start | bytes 786440 | tf_op jit(solution)/shard_map/ppermute | solution.py:20
  26.8 1.2 %copy-start.3 = (f32[256,1024]{1,0:T(8,128)S(1)}, f32[256,1024]{1,0:T(8,128)}, u32[]{:S(2)}) copy-start(f32[256,1024]{1,0:T(8,128)} %param.12) | copy-start | bytes 3145732
  26.8 1.5 %copy-start.4 = (f32[256,1024]{1,0:T(8,128)S(1)}, f32[256,1024]{1,0:T(8,128)}, u32[]{:S(2)}) copy-start(f32[256,1024]{1,0:T(8,128)} %param.13) | copy-start | bytes 3145732
  30.1 8.4 %collective-permute-start.10 = (bf16[256,1024]{1,0:T(8,128)(2,1)S(1)}, bf16[256,1024]{1,0:T(8,128)(2,1)S(1)}, u32[]{:S(2)}, u32[]{:S(2)}) collective-permute-start(bf16[256,1024]{1,0:T(8,128)(2,1)S(1)} %get-tuple-element.147), channel_id=1, source_target_pairs={{0,8},{4,20},{8,0},{12,28},{16,24},{20,4},{24,16},{28,12},{1,9},{5... | collective-permute-start | bytes 1572872 | tf_op jit(solution)/shard_map/ppermute | solution.py:20
  31.3 12.8 %collective-permute-start.6 = (bf16[256,1024]{1,0:T(8,128)(2,1)S(1)}, bf16[256,1024]{1,0:T(8,128)(2,1)}, u32[]{:S(2)}, u32[]{:S(2)}) collective-permute-start(bf16[256,1024]{1,0:T(8,128)(2,1)S(1)} %get-tuple-element.147), channel_id=1, source_target_pairs={{0,1},{1,0},{2,3},{3,2},{4,5},{5,4},{6,7},{7,6},{8,9},{9,8},{10,11... | collective-permute-start | bytes 1572872 | tf_op jit(solution)/shard_map/ppermute | solution.py:138
  31.5 12.7 %collective-permute-start.7 = (bf16[256,1024]{1,0:T(8,128)(2,1)S(1)}, bf16[256,1024]{1,0:T(8,128)(2,1)}, u32[]{:S(2)}, u32[]{:S(2)}) collective-permute-start(bf16[256,1024]{1,0:T(8,128)(2,1)S(1)} %get-tuple-element.147), channel_id=1, source_target_pairs={{1,2},{2,1},{5,6},{6,5},{9,10},{10,9},{13,14},{14,13},{17,18},{18,... | collective-permute-start | bytes 1572872 | tf_op jit(solution)/shard_map/ppermute | solution.py:142
  38.6 25.8 %collective-permute-start.16 = (bf16[512,1024]{1,0:T(8,128)(2,1)S(1)}, bf16[512,1024]{1,0:T(8,128)(2,1)S(1)}, u32[]{:S(2)}, u32[]{:S(2)}) collective-permute-start(bf16[512,1024]{1,0:T(8,128)(2,1)S(1)} %pad_maximum_fusion.1.refs_0_), channel_id=1, source_target_pairs={{0,4},{4,0},{8,12},{12,8},{16,20},{20,16},{24,28},{28,24},{1,5},{5... | collective-permute-start | bytes 3145736 | tf_op jit(solution)/shard_map/ppermute | solution.py:20
  42.9 21.6 %collective-permute-start.11 = (bf16[512,1024]{1,0:T(8,128)(2,1)S(1)}, bf16[512,1024]{1,0:T(8,128)(2,1)S(1)}, u32[]{:S(2)}, u32[]{:S(2)}) collective-permute-start(bf16[512,1024]{1,0:T(8,128)(2,1)S(1)} %pad_maximum_fusion.1.refs_0_), channel_id=1, source_target_pairs={{0,16},{4,12},{8,24},{12,4},{16,0},{20,28},{24,8},{28,20},{1,17},{... | collective-permute-start | bytes 3145736 | tf_op jit(solution)/shard_map/ppermute | solution.py:20
  44.1 15.9 %collective-permute-start.13 = (bf16[256,1024]{1,0:T(8,128)(2,1)}, bf16[256,1024]{1,0:T(8,128)(2,1)}, u32[]{:S(2)}, u32[]{:S(2)}) collective-permute-start(bf16[256,1024]{1,0:T(8,128)(2,1)} %collective-permute-done.7), channel_id=1, source_target_pairs={{1,0},{2,3},{5,4},{6,7},{9,8},{10,11},{13,12},{14,15},{17,16},{18,... | collective-permute-start | bytes 1572872 | tf_op jit(solution)/shard_map/ppermute | solution.py:146
  47.0 15.9 %collective-permute-start.15 = (bf16[256,1024]{1,0:T(8,128)(2,1)}, bf16[256,1024]{1,0:T(8,128)(2,1)}, u32[]{:S(2)}, u32[]{:S(2)}) collective-permute-start(bf16[256,1024]{1,0:T(8,128)(2,1)} %collective-permute-done.6), channel_id=1, source_target_pairs={{0,8},{4,20},{8,0},{12,28},{16,24},{20,4},{24,16},{28,12},{1,9},{5... | collective-permute-start | bytes 1572872 | tf_op jit(solution)/shard_map/ppermute | solution.py:20
  47.0 21.6 %collective-permute-start.8 = (bf16[256,1024]{1,0:T(8,128)(2,1)}, bf16[256,1024]{1,0:T(8,128)(2,1)S(1)}, u32[]{:S(2)}, u32[]{:S(2)}) collective-permute-start(bf16[256,1024]{1,0:T(8,128)(2,1)} %collective-permute-done.6), channel_id=1, source_target_pairs={{1,2},{2,1},{5,6},{6,5},{9,10},{10,9},{13,14},{14,13},{17,18},{18,... | collective-permute-start | bytes 1572872 | tf_op jit(solution)/shard_map/ppermute | solution.py:142
  60.1 10.1 %copy-start.1 = (bf16[1024,1024]{1,0:T(8,128)(2,1)S(1)}, bf16[1024,1024]{1,0:T(8,128)(2,1)}, u32[]{:S(2)}) copy-start(bf16[1024,1024]{1,0:T(8,128)(2,1)} %get-tuple-element.114.normed) | copy-start | bytes 6291460
  61.4 11.4 %collective-permute-start.14 = (bf16[256,1024]{1,0:T(8,128)(2,1)S(1)}, bf16[256,1024]{1,0:T(8,128)(2,1)S(1)}, u32[]{:S(2)}, u32[]{:S(2)}) collective-permute-start(bf16[256,1024]{1,0:T(8,128)(2,1)S(1)} %broadcast_select_fusion), channel_id=1, source_target_pairs={{0,8},{4,20},{8,0},{12,28},{16,24},{20,4},{24,16},{28,12},{1,9},{5... | collective-permute-start | bytes 1572872 | tf_op jit(solution)/shard_map/ppermute | solution.py:20
  62.9 11.5 %collective-permute-start.20 = (bf16[256,1024]{1,0:T(8,128)(2,1)}, bf16[256,1024]{1,0:T(8,128)(2,1)S(1)}, u32[]{:S(2)}, u32[]{:S(2)}) collective-permute-start(bf16[256,1024]{1,0:T(8,128)(2,1)} %collective-permute-done.6), channel_id=1, source_target_pairs={{0,16},{4,12},{8,24},{12,4},{16,0},{20,28},{24,8},{28,20},{1,17},{... | collective-permute-start | bytes 1572872 | tf_op jit(solution)/shard_map/ppermute | solution.py:20
  64.4 20.3 %collective-permute-start.18 = (bf16[512,1024]{1,0:T(8,128)(2,1)S(1)}, bf16[512,1024]{1,0:T(8,128)(2,1)S(1)}, u32[]{:S(2)}, u32[]{:S(2)}) collective-permute-start(bf16[512,1024]{1,0:T(8,128)(2,1)S(1)} %collective-permute-done.11.refs_0_), channel_id=1, source_target_pairs={{0,4},{4,0},{8,12},{12,8},{16,20},{20,16},{24,28},{28,24},{1,5},{5... | collective-permute-start | bytes 3145736 | tf_op jit(solution)/shard_map/ppermute | solution.py:20
  68.5 16.2 %collective-permute-start.19 = (bf16[512,1024]{1,0:T(8,128)(2,1)S(1)}, bf16[512,1024]{1,0:T(8,128)(2,1)S(1)}, u32[]{:S(2)}, u32[]{:S(2)}) collective-permute-start(bf16[512,1024]{1,0:T(8,128)(2,1)S(1)} %pad_maximum_fusion.2.refs_2_), channel_id=1, source_target_pairs={{0,4},{4,0},{8,12},{12,8},{16,20},{20,16},{24,28},{28,24},{1,5},{5... | collective-permute-start | bytes 3145736 | tf_op jit(solution)/shard_map/ppermute | solution.py:20
  68.6 12.5 %collective-permute-start.9 = (bf16[256,1024]{1,0:T(8,128)(2,1)S(1)}, bf16[256,1024]{1,0:T(8,128)(2,1)S(1)}, u32[]{:S(2)}, u32[]{:S(2)}) collective-permute-start(bf16[256,1024]{1,0:T(8,128)(2,1)S(1)} %collective-permute-done.8), channel_id=1, source_target_pairs={{1,0},{2,3},{5,4},{6,7},{9,8},{10,11},{13,12},{14,15},{17,16},{18,... | collective-permute-start | bytes 1572872 | tf_op jit(solution)/shard_map/ppermute | solution.py:146
  70.1 14.6 %slice-start = ((s8[5242880]{0:T(1024)(128)(4,1)}), s8[4194304]{0:T(1024)(128)(4,1)S(1)}, s32[]{:S(2)}) async-start(s8[5242880]{0:T(1024)(128)(4,1)} %bitcast.123), calls=%async_computation | async-start | bytes 8388608
  70.1 14.6 %slice-start.1 = ((s8[5242880]{0:T(1024)(128)(4,1)}), s8[1048576]{0:T(1024)(128)(4,1)S(1)}, s32[]{:S(2)}) async-start(s8[5242880]{0:T(1024)(128)(4,1)} %bitcast.123), calls=%async_computation.1 | async-start | bytes 2097152
  72.8 22.4 %collective-permute-start.17 = (bf16[512,1024]{1,0:T(8,128)(2,1)S(1)}, bf16[512,1024]{1,0:T(8,128)(2,1)S(1)}, u32[]{:S(2)}, u32[]{:S(2)}) collective-permute-start(bf16[512,1024]{1,0:T(8,128)(2,1)S(1)} %pad_maximum_fusion.3.refs_0_), channel_id=1, source_target_pairs={{0,16},{4,12},{8,24},{12,4},{16,0},{20,28},{24,8},{28,20},{1,17},{... | collective-permute-start | bytes 3145736 | tf_op jit(solution)/shard_map/ppermute | solution.py:20
  74.4 8.1 %collective-permute-start.21 = (bf16[256,1024]{1,0:T(8,128)(2,1)S(1)}, bf16[256,1024]{1,0:T(8,128)(2,1)S(1)}, u32[]{:S(2)}, u32[]{:S(2)}) collective-permute-start(bf16[256,1024]{1,0:T(8,128)(2,1)S(1)} %collective-permute-done.20.refs_4_), channel_id=1, source_target_pairs={{0,4},{4,0},{8,12},{12,8},{16,20},{20,16},{24,28},{28,24},{1,5},{5... | collective-permute-start | bytes 1572872 | tf_op jit(solution)/shard_map/ppermute | solution.py:20
  81.1 14.1 %collective-permute-start.12 = (bf16[256,1024]{1,0:T(8,128)(2,1)S(1)}, bf16[256,1024]{1,0:T(8,128)(2,1)S(1)}, u32[]{:S(2)}, u32[]{:S(2)}) collective-permute-start(bf16[256,1024]{1,0:T(8,128)(2,1)S(1)} %broadcast_select_fusion.1), channel_id=1, source_target_pairs={{0,8},{4,20},{8,0},{12,28},{16,24},{20,4},{24,16},{28,12},{1,9},{5... | collective-permute-start | bytes 1572872 | tf_op jit(solution)/shard_map/ppermute | solution.py:20
  82.5 17.1 %collective-permute-start.25 = (bf16[256,1024]{1,0:T(8,128)(2,1)S(1)}, bf16[256,1024]{1,0:T(8,128)(2,1)S(1)}, u32[]{:S(2)}, u32[]{:S(2)}) collective-permute-start(bf16[256,1024]{1,0:T(8,128)(2,1)S(1)} %slice.19), channel_id=1, source_target_pairs={{0,1},{1,0},{2,3},{3,2},{4,5},{5,4},{6,7},{7,6},{8,9},{9,8},{10,11... | collective-permute-start | bytes 1572872 | tf_op jit(solution)/shard_map/ppermute | solution.py:138
  84.8 19.6 %slice-start.2 = ((s8[5242880]{0:T(1024)(128)(4,1)}), s8[4194304]{0:T(1024)(128)(4,1)S(1)}, s32[]{:S(2)}) async-start(s8[5242880]{0:T(1024)(128)(4,1)} %bitcast.125), calls=%async_computation.2 | async-start | bytes 8388608
  84.8 19.5 %slice-start.3 = ((s8[5242880]{0:T(1024)(128)(4,1)}), s8[1048576]{0:T(1024)(128)(4,1)S(1)}, s32[]{:S(2)}) async-start(s8[5242880]{0:T(1024)(128)(4,1)} %bitcast.125), calls=%async_computation.3 | async-start | bytes 2097152
  95.2 8.7 %collective-permute-start.23 = (bf16[512,1024]{1,0:T(8,128)(2,1)S(1)}, bf16[512,1024]{1,0:T(8,128)(2,1)S(1)}, u32[]{:S(2)}, u32[]{:S(2)}) collective-permute-start(bf16[512,1024]{1,0:T(8,128)(2,1)S(1)} %pad_maximum_fusion.3.refs_0_), channel_id=1, source_target_pairs={{0,4},{4,0},{8,12},{12,8},{16,20},{20,16},{24,28},{28,24},{1,5},{5... | collective-permute-start | bytes 3145736 | tf_op jit(solution)/shard_map/ppermute | solution.py:20
  99.4 4.5 %collective-permute-start.24 = (bf16[512,1024]{1,0:T(8,128)(2,1)S(1)}, bf16[512,1024]{1,0:T(8,128)(2,1)S(1)}, u32[]{:S(2)}, u32[]{:S(2)}) collective-permute-start(bf16[512,1024]{1,0:T(8,128)(2,1)S(1)} %collective-permute-done.17.refs_2_), channel_id=1, source_target_pairs={{0,4},{4,0},{8,12},{12,8},{16,20},{20,16},{24,28},{28,24},{1,5},{5... | collective-permute-start | bytes 3145736 | tf_op jit(solution)/shard_map/ppermute | solution.py:20
  99.5 14.0 %collective-permute-start.22 = (bf16[512,1024]{1,0:T(8,128)(2,1)S(1)}, bf16[512,1024]{1,0:T(8,128)(2,1)S(1)}, u32[]{:S(2)}, u32[]{:S(2)}) collective-permute-start(bf16[512,1024]{1,0:T(8,128)(2,1)S(1)} %constant_dynamic-update-slice_fusion.refs_0_), channel_id=1, source_target_pairs={{0,16},{4,12},{8,24},{12,4},{16,0},{20,28},{24,8},{28,20},{1,17},{... | collective-permute-start | bytes 3145736 | tf_op jit(solution)/shard_map/ppermute | solution.py:20
  99.6 4.4 %collective-permute-start.26 = (bf16[256,1024]{1,0:T(8,128)(2,1)S(1)}, bf16[256,1024]{1,0:T(8,128)(2,1)S(1)}, u32[]{:S(2)}, u32[]{:S(2)}) collective-permute-start(bf16[256,1024]{1,0:T(8,128)(2,1)S(1)} %collective-permute-done.25.refs_4_), channel_id=1, source_target_pairs={{0,4},{4,0},{8,12},{12,8},{16,20},{20,16},{24,28},{28,24},{1,5},{5... | collective-permute-start | bytes 1572872 | tf_op jit(solution)/shard_map/ppermute | solution.py:20
  103.9 10.9 %collective-permute-start.28 = (bf16[512,1024]{1,0:T(8,128)(2,1)S(1)}, bf16[512,1024]{1,0:T(8,128)(2,1)S(1)}, u32[]{:S(2)}, u32[]{:S(2)}) collective-permute-start(bf16[512,1024]{1,0:T(8,128)(2,1)S(1)} %constant_dynamic-update-slice_fusion.refs_0_), channel_id=1, source_target_pairs={{0,4},{4,0},{8,12},{12,8},{16,20},{20,16},{24,28},{28,24},{1,5},{5... | collective-permute-start | bytes 3145736 | tf_op jit(solution)/shard_map/ppermute | solution.py:20
  104.3 10.5 %copy-start.2 = (bf16[1024,1024]{1,0:T(8,128)(2,1)S(1)}, bf16[1024,1024]{1,0:T(8,128)(2,1)}, u32[]{:S(2)}) copy-start(bf16[1024,1024]{1,0:T(8,128)(2,1)} %get-tuple-element.142.normed) | copy-start | bytes 6291460
  113.5 3.9 %collective-permute-start.27 = (bf16[512,1024]{1,0:T(8,128)(2,1)S(1)}, bf16[512,1024]{1,0:T(8,128)(2,1)S(1)}, u32[]{:S(2)}, u32[]{:S(2)}) collective-permute-start(bf16[512,1024]{1,0:T(8,128)(2,1)S(1)} %collective-permute-done.22.refs_0_), channel_id=1, source_target_pairs={{0,4},{4,0},{8,12},{12,8},{16,20},{20,16},{24,28},{28,24},{1,5},{5... | collective-permute-start | bytes 3145736 | tf_op jit(solution)/shard_map/ppermute | solution.py:20
  114.9 2.6 %copy-start = (bf16[1024,1024]{1,0:T(8,128)(2,1)S(1)}, bf16[1024,1024]{1,0:T(8,128)(2,1)}, u32[]{:S(2)}) copy-start(bf16[1024,1024]{1,0:T(8,128)(2,1)} %get-tuple-element.109.normed) | copy-start | bytes 6291460
